TPU v7x, 32 devices: a whole 2x2x4 slice. The times are simulated.
32 devices in a mesh: nest: 2 (over core), bin: 16 (over z, y, x).
Axes of the slice: x: 2, y: 2, z: 4, core: 2. Of those that a mesh axis runs over, the one named last changes fastest.
Arguments:
- spectra: float32 [2, 1152, 1024], P('nest', 'bin'), may hold values from 0.05 to 2
- courant: float32 [2, 1152], P(None, 'bin'), may hold values from -0.9 to 0.9
- coupling: bfloat16 [1152, 1152], replicated, may hold values from -0.1875 to 0.1875
- growth: float32 [1152], replicated, may hold values from 0.05 to 0.5
- dissipation: float32 [1152], replicated, may hold values from 0.2 to 2
- wind: float32 [2, 1024], P('nest'), may hold values from 0.5 to 2
- neighbours: int32 [2, 4, 1024], P('nest'), may hold values from 0 to 1023, as said below
- wet_mask: int32 [2, 1024], P('nest'), may hold values from 0 to 1, as said below
- send_list: int32 [2, 256], P('nest'), may hold values from 0 to 1023, as said below
- recv_list: int32 [2, 256], P('nest'), may hold values from 0 to 1023, as said below
- substep_count: int32 [2], P('nest'), may hold values from 1 to 2, as said below
Outputs:
- new_spectra: float32 [2, 1152, 1024], P('nest', 'bin')
Inputs may be any that keep to these rules, and one draw needn't show every extreme that they name: `neighbours`: row 0 holds each point's east neighbour, row 1 west, row 2 north, row 3 south, on a periodic grid of 4 rows of 256 points; grid row r holds the point numbers r * 256 to (r + 1) * 256 - 1 in some order. `wet_mask`: exactly 512 points of each nest are sea points. `send_list`: distinct sea points of the nest, none of them in recv_list of the same nest. `recv_list`: distinct sea points of the nest. `substep_count`: some nest takes 2 substeps.
All inputs are finite; a program needn't handle non-finite values.
Results may differ from a plain program's by a relative error of at most 0.0012.
Values sent between devices are 32-bit elements; how exact they have to be, the bound alone decides.
No kernel may reach another device: no remote copies, remote signals or barrier semaphores. Data moves between devices by JAX's collectives and lax.ppermute only.
A program may use at most 64 MiB of HBM per device.

v0:
```python
import jax
import jax.numpy as jnp
from jax import lax
from jax.sharding import PartitionSpec as P

SUBSTEPS = 2
SRC = 5


source_dt = 0.25
tiny_add = 1e-06


def from_partner(array, axis, stride):
    return lax.ppermute(array, axis, [(i, i ^ 1 << stride) for i in range(lax.axis_size(axis))])


def advect_grid(field, rate, axis_dim):
    magnitude = jnp.abs(rate)
    forward = rate >= 0.0
    next_cell = jnp.roll(field, -1, axis=axis_dim)
    prev_cell = jnp.roll(field, 1, axis=axis_dim)
    next_next = jnp.roll(field, -2, axis=axis_dim)
    upwind = jnp.where(forward, field, next_cell)
    downwind = jnp.where(forward, next_cell, field)
    far_upwind = jnp.where(forward, prev_cell, next_next)
    estimate = (
        0.5 * (upwind + downwind)
        - 0.5 * magnitude * (downwind - upwind)
        - (1.0 - magnitude * magnitude) / 6.0 * (downwind - 2.0 * upwind + far_upwind)
    )
    face_value = jnp.clip(estimate, jnp.minimum(upwind, downwind), jnp.maximum(upwind, downwind))
    return field - rate * (face_value - jnp.roll(face_value, 1, axis=axis_dim))


def integrate(columns, wind_cols, coupling, growth, dissipation):
    for repeat in range(SRC):
        linear = jnp.dot(coupling, columns.astype(jnp.bfloat16), preferred_element_type=jnp.float32)
        spread = jnp.sqrt(jnp.mean(columns * columns, axis=0) + tiny_add)
        columns = (
            columns + source_dt * (linear + growth[:, None] * wind_cols[None, :] * columns)
        ) / (1.0 + source_dt * dissipation[:, None] * spread[None, :])
    return columns


def wet_points(sea_int, total):
    position = jnp.cumsum(sea_int) - 1
    target = jnp.where(sea_int == 1, position, total)
    return (
        jnp.zeros((total,), jnp.int32)
        .at[target]
        .set(jnp.arange(sea_int.shape[0], dtype=jnp.int32), mode="drop")
    )


def grid_order(east_index, north_index, rows_count, cols_count):

    def north_walk(point, unused):
        return (north_index[point], point)

    def east_walk(point, unused):
        return (east_index[point], point)

    starts = lax.scan(north_walk, jnp.int32(0), None, length=rows_count)[1]
    walked = lax.scan(east_walk, starts, None, length=cols_count)[1]
    return walked.T.reshape(-1)


def local(
    spectra,
    courant,
    coupling,
    growth,
    dissipation,
    wind,
    neighbours,
    wet_mask,
    send_list,
    recv_list,
    substep_count,
):
    field = spectra[0]
    bins_here = field.shape[0]
    points = field.shape[1]
    cols_count = min(256, points // 4)
    rows_count = points // cols_count
    tables = neighbours[0]
    ordering = grid_order(tables[0], tables[2], rows_count, cols_count)
    position = jnp.zeros((points,), jnp.int32).at[ordering].set(jnp.arange(points, dtype=jnp.int32))
    sea_int = wet_mask[0]
    sea = sea_int.astype(jnp.float32)
    sea_grid = sea[ordering].reshape(1, rows_count, cols_count)
    steps_here = substep_count[0]
    rates = courant / steps_here.astype(jnp.float32)
    rate_east = rates[0][:, None, None]
    rate_north = rates[1][:, None, None]
    send_slots = position[send_list[0]]
    recv_slots = position[recv_list[0]]
    gridded = (field * sea[None, :])[:, ordering]
    for substep in range(SUBSTEPS):
        outgoing = gridded[:, send_slots]
        incoming = from_partner(outgoing, "nest", 0)
        current = gridded.at[:, recv_slots].set(incoming).reshape(bins_here, rows_count, cols_count)
        current = advect_grid(current, rate_east, 2)
        current = advect_grid(current, rate_north, 1)
        current = (current * sea_grid).reshape(bins_here, points)
        gridded = jnp.where(substep < steps_here, current, gridded)
    field = gridded[:, position]
    devices = lax.axis_size("bin")
    my_rank = lax.axis_index("bin")
    wind_here = wind[0]
    wet_index = wet_points(sea_int, points // 2)
    columns = lax.all_to_all(field[:, wet_index], "bin", split_axis=1, concat_axis=0, tiled=True)
    share = wet_index.shape[0] // devices
    wind_cols = lax.dynamic_slice_in_dim(wind_here[wet_index], my_rank * share, share)
    columns = integrate(columns, wind_cols, coupling, growth, dissipation)
    returned = lax.all_to_all(columns, "bin", split_axis=0, concat_axis=1, tiled=True)
    result_field = jnp.zeros_like(field).at[:, wet_index].set(returned)
    return result_field[None]


def solution(mesh):
    in_specs = (
        P("nest", "bin", None),
        P(None, "bin"),
        P(),
        P(),
        P(),
        P("nest", None),
        P("nest", None, None),
        P("nest", None),
        P("nest", None),
        P("nest", None),
        P("nest"),
    )
    out_specs = P("nest", "bin", None)
    return jax.shard_map(local, mesh=mesh, in_specs=in_specs, out_specs=out_specs, check_vma=False)
```

profile of v0, /device:TPU:0, one launch (start us, length us, event | category | flops | bytes accessed | tf_op | source)
XLA Modules:
  0.0 265.6 jit_solution(9251582719118182656)
XLA Ops:
  0.0 0.9 fusion.78
  0.9 5.5 %while.24 = (s32[]{:T(128)}, s32[]{:T(128)}, s32[4]{0:T(128)S(1)}, s32[1024]{0:T(1024)S(1)}, s32[]{:T(128)}, /*index=5*/s32[]{:T(128)}, s32[]{:T(128)}) while((s32[]{:T(128)}, s32[]{:T(128)}, s32[4]{0:T(128)S(1)}, s32[1024]{0:T(1024)S(1)}, s32[]{:T(128)}, /*index=5*/s32[]{:T(128)}, s32[]{:T(128)}) %tuple.72), condition=%wide.region_4.5_spmd, body=%wide.region_3.4_spmd.sunk | while | flops 5 | bytes 143 | solution.py:64
  0.9 0.6 dynamic_slice.8
  2.3 0.6 dynamic_slice.8
  3.7 0.6 dynamic_slice.8
  5.1 0.6 dynamic_slice.8
  6.5 172.0 %while.25 = (s32[]{:T(128)}, s32[4]{0:T(128)S(1)}, s32[256,4]{1,0:T(8,128)S(1)}, s32[1024]{0:T(1024)S(1)}, s32[]{:T(128)}, /*index=5*/s32[]{:T(128)}) while((s32[]{:T(128)}, s32[4]{0:T(128)S(1)}, s32[256,4]{1,0:T(8,128)S(1)}, s32[1024]{0:T(1024)S(1)}, s32[]{:T(128)}, /*index=5*/s32[]{:T(128)}) %tuple.71), condition=%wide.region_6.7_spmd, body=%wide.region_5.6_spmd.sunk | while | flops 1038 | bytes 4297 | solution.py:65
  6.6 0.6 gather_fusion
  7.2 0.6 gather_fusion
  16.0 0.6 gather_fusion
  16.6 0.6 gather_fusion
  17.3 0.6 gather_fusion
  18.0 0.6 gather_fusion
  18.6 0.6 gather_fusion
  19.3 0.6 gather_fusion
  20.0 0.6 gather_fusion
  28.7 0.6 gather_fusion
  29.4 0.6 gather_fusion
  30.1 0.6 gather_fusion
  30.7 0.6 gather_fusion
  31.4 0.6 gather_fusion
  32.1 0.6 gather_fusion
  32.8 0.6 gather_fusion
  41.5 0.6 gather_fusion
  42.2 0.6 gather_fusion
  42.8 0.6 gather_fusion
  43.5 0.6 gather_fusion
  44.2 0.6 gather_fusion
  44.8 0.6 gather_fusion
  45.5 0.6 gather_fusion
  54.2 0.6 gather_fusion
  54.9 0.6 gather_fusion
  55.6 0.6 gather_fusion
  56.3 0.6 gather_fusion
  56.9 0.6 gather_fusion
  178.6 1.0 copy.21
  179.6 4.3 %scatter_custom_fusion.1 = s32[1024]{0:T(1024)S(1)} fusion(s32[1024]{0:T(1024)S(1)} %bitcast.309, s32[1024]{0:T(1024)S(1)} %iota.7, s32[]{:T(128)} %constant.22.clone.1), kind=kCustom, calls=%fused_computation.152 | custom fusion | bytes 4100 | tf_op jit(solution)/shard_map/scatter | solution.py:89
  184.0 1.4 gather_fusion.3
  185.4 2.0 bitcast_multiply_fusion
  187.4 5.0 %gather_fusion.1 = f32[1024,72]{1,0:T(8,128)} fusion(f32[72,1024]{0,1:T(8,128)} %bitcast_multiply_fusion, s32[1024]{0:T(1024)S(1)} %broadcast_clamp_fusion), kind=kCustom, calls=%fused_computation.1 | custom fusion | bytes 593920 | tf_op jit(solution)/shard_map/gather | solution.py:99
  192.4 1.8 gather_fusion.4
  195.5 1.4 gather_fusion.2
  197.5 4.3 %scatter_custom_fusion = s32[512]{0:T(512)S(1)} fusion(s32[1024]{0:T(1024)S(1)} %bitcast.312, s32[1024]{0:T(1024)S(1)} %iota.6, s32[]{:T(128)} %constant.22.clone.1), kind=kCustom, calls=%fused_computation.154 | custom fusion | bytes 2052 | tf_op jit(solution)/shard_map/scatter | solution.py:52
  201.8 1.0 copy.47
  202.8 4.5 %gather_fusion.5 = f32[1024]{0:T(1024)S(1)} fusion(f32[1024]{0:T(1024)S(1)} %bitcast.279, s32[1024]{0:T(1024)S(1)} %broadcast_clamp_fusion), kind=kCustom, calls=%fused_computation.5 | custom fusion | bytes 12288 | tf_op jit(solution)/shard_map/gather | solution.py:92
  207.4 1.4 scatter_custom_fusion.2
  210.7 1.5 fusion.39
  212.2 1.8 gather_fusion.6
  214.1 1.0 copy.48
  215.4 1.4 scatter_custom_fusion.3
  218.7 1.5 fusion.23
  220.2 3.9 %gather_fusion.7 = f32[1024,72]{1,0:T(8,128)S(1)} fusion(f32[72,1024]{0,1:T(8,128)} %fusion.23, s32[1024]{0:T(1024)S(1)} %fusion.63), kind=kCustom, calls=%fused_computation.7 | custom fusion | bytes 593920 | tf_op jit(solution)/shard_map/gather | solution.py:108
  224.1 1.6 gather_fusion.8
  225.8 8.1 %all-to-all-start = ((f32[72,16,32]{0,2,1:T(8,128)}), f32[72,16,32]{0,2,1:T(8,128)S(1)}, u32[]{:S(2)}, u32[]{:S(2)}) async-start(f32[72,16,32]{0,2,1:T(8,128)} %bitcast.51), calls=%async_computation | async-start | bytes 524288 | tf_op jit(solution)/shard_map/all_to_all | solution.py:113
  233.9 2.3 gather_fusion.9
  236.2 7.9 %all-to-all-done = f32[72,16,32]{0,2,1:T(8,128)S(1)} async-done(((f32[72,16,32]{0,2,1:T(8,128)}), f32[72,16,32]{0,2,1:T(8,128)S(1)}, u32[]{:S(2)}, u32[]{:S(2)}) %all-to-all-start) | async-done | bytes 147488 | tf_op jit(solution)/shard_map/all_to_all | solution.py:113
  244.6 1.0 multiply_reduce_fusion.4
  245.7 1.0 multiply_reduce_fusion.3
  246.7 1.0 multiply_reduce_fusion.2
  247.8 1.0 multiply_reduce_fusion.1
  248.8 0.9 fusion.3
  250.0 12.8 %all_to_all.38 = f32[16,72,32]{1,2,0:T(8,128)S(1)} all-to-all(f32[16,72,32]{1,2,0:T(8,128)S(1)} %copy.24), channel_id=1, replica_groups=mesh['nest'=2,'bin'=16] {'bin'}, dimensions={0} | all-to-all | bytes 294912 | tf_op jit(solution)/shard_map/all_to_all | solution.py:117
  262.8 1.8 scatter_custom_fusion.4
  264.7 0.9 copy.25
  (1095 shorter events, 159.6 us)
Async XLA Ops:
  0.0 244.6 %copy-start = (bf16[1152,1152]{1,0:T(8,128)(2,1)S(1)}, bf16[1152,1152]{1,0:T(8,128)(2,1)}, u32[]{:S(2)}) copy-start(bf16[1152,1152]{1,0:T(8,128)(2,1)} %param.17) | copy-start | bytes 7962628
  0.0 178.6 %copy-start.6 = (s32[1,1024]{1,0:T(1,128)S(1)}, s32[1,1024]{1,0:T(1,128)}, u32[]{:S(2)}) copy-start(s32[1,1024]{1,0:T(1,128)} %param.22) | copy-start | bytes 12292
  0.0 178.6 %copy-start.4 = (f32[1,72,1024]{2,1,0:T(8,128)S(1)}, f32[1,72,1024]{2,1,0:T(8,128)}, u32[]{:S(2)}) copy-start(f32[1,72,1024]{2,1,0:T(8,128)} %param.15) | copy-start | bytes 884740
  0.0 183.9 %copy-start.8 = (s32[1,256]{1,0:T(1,128)S(1)}, s32[1,256]{1,0:T(1,128)}, u32[]{:S(2)}) copy-start(s32[1,256]{1,0:T(1,128)} %param.23) | copy-start | bytes 3076
  183.9 11.4 %copy-start.9 = (f32[2,72]{1,0:T(2,128)S(1)}, f32[2,72]{1,0:T(2,128)}, u32[]{:S(2)}) copy-start(f32[2,72]{1,0:T(2,128)} %param.16) | copy-start | bytes 1732
  184.0 11.5 %copy-start.10 = (s32[1,256]{1,0:T(1,128)S(1)}, s32[1,256]{1,0:T(1,128)}, u32[]{:S(2)}) copy-start(s32[1,256]{1,0:T(1,128)} %param.24) | copy-start | bytes 3076
  194.2 13.2 %collective-permute-start = (f32[72,256]{0,1:T(8,128)S(1)}, f32[72,256]{0,1:T(8,128)S(1)}, u32[]{:S(2)}, u32[]{:S(2)}) collective-permute-start(f32[72,256]{0,1:T(8,128)S(1)} %bitcast.303), channel_id=1, source_target_pairs={{0,16},{16,0},{1,17},{17,1},{2,18},{18,2},{3,19},{19,3},{4,20},{20... | collective-permute-start | bytes 221192 | tf_op jit(solution)/shard_map/ppermute | solution.py:15
  209.6 1.0 copy-start.3
  214.0 1.4 collective-permute-start.1
  217.6 1.0 copy-start.2
  220.2 13.6 %copy-start.1 = (f32[1,1024]{1,0:T(1,128)S(1)}, f32[1,1024]{1,0:T(1,128)}, u32[]{:S(2)}) copy-start(f32[1,1024]{1,0:T(1,128)} %param.20) | copy-start | bytes 12292
  220.2 16.0 %copy-start.7 = (f32[1152]{0:T(1024)S(1)}, f32[1152]{0:T(1024)}, u32[]{:S(2)}) copy-start(f32[1152]{0:T(1024)} %param.19) | copy-start | bytes 13828
  224.1 20.5 %copy-start.5 = (f32[1152]{0:T(1024)S(1)}, f32[1152]{0:T(1024)}, u32[]{:S(2)}) copy-start(f32[1152]{0:T(1024)} %param.18) | copy-start | bytes 13828
  225.8 18.4 %all-to-all-start = ((f32[72,16,32]{0,2,1:T(8,128)}), f32[72,16,32]{0,2,1:T(8,128)S(1)}, u32[]{:S(2)}, u32[]{:S(2)}) async-start(f32[72,16,32]{0,2,1:T(8,128)} %bitcast.51), calls=%async_computation | async-start | bytes 524288 | tf_op jit(solution)/shard_map/all_to_all | solution.py:113
where the time goes:
time: 266 us
  local copies, waits for them, and re-layouts  215 us (81%)
  blocking collectives  12.8 us (5%)
  other arithmetic  10.7 us (4%)
  starting transfers between devices  8.72 us (3%)
  waiting for transfers between devices  8.18 us (3%)
  matrix products  5 us (2%)
  loops' own time  3.96 us (1%)
    gather x256, local copies, waits for them, and re-layouts, east_walk(): return (east_index[point], point)  161 us
    all_to_all x1, blocking collectives, local(): lax.all_to_all(columns, 'bin', split_axis=0, concat_axis=1, tiled=True)  12.8 us
    all_to_all x1, starting transfers between devices, local(): lax.all_to_all(field[:, wet_index], 'bin', split_axis=1, concat_axis=0, t...  8.08 us
    all_to_all x1, waiting for transfers between devices, local(): lax.all_to_all(field[:, wet_index], 'bin', split_axis=1, concat_axis=0, t...  7.92 us
    dynamic_update_slice x256, local copies, waits for them, and re-layouts, grid_order(): walked = lax.scan(east_walk, starts, None, length=cols_count)[1]  6.61 us
  transfers between devices with their start and end apart: 3, of which 2 were waited for; matrix products, arithmetic and copies ran while one was open for 6% of the time, Pallas kernels for 0%

commit v1 on v0

v1 whole, which is shorter than its diff:
```python
import functools

import jax
import jax.numpy as jnp
from jax import lax
from jax.experimental import pallas as pl
from jax.experimental.pallas import tpu as pltpu
from jax.sharding import PartitionSpec as P

SUBSTEPS = 2
SRC = 5
LANES = 128
SUBLANES = 8

source_dt = 0.25
tiny_add = 1e-06
f32 = jnp.float32
bf16 = jnp.bfloat16


def up_to(value, unit):
    return -(-value // unit) * unit


def grid_shape(points):
    cols_count = min(256, points // 4)
    return points // cols_count, cols_count


def dot(left, right):
    return jnp.dot(left, right, preferred_element_type=f32)


def dot_t(left, right):
    return lax.dot_general(left, right, (((1,), (1,)), ((), ())), preferred_element_type=f32)


def split(values):
    rest = values - values.astype(bf16).astype(f32)
    return jnp.concatenate([values, rest], axis=0).astype(bf16)


def joined(terms):
    half = terms.shape[0] // 2
    return terms[:half] + terms[half:]


def one_hot(rows, index):
    at = lax.broadcasted_iota(jnp.int32, (rows, index.shape[1]), 0)
    return jnp.where(at == index, 1.0, 0.0).astype(bf16)


def column(row):
    size = row.shape[1]
    at = lax.broadcasted_iota(jnp.int32, (size, size), 0)
    across = lax.broadcasted_iota(jnp.int32, (size, size), 1)
    return jnp.sum(jnp.where(at == across, row, 0.0), axis=1, keepdims=True)


def each(count, body):
    if count <= 8:
        for step in range(count):
            body(step)
    else:
        pl.loop(0, count)(body)


def span(start, size):
    if isinstance(start, int):
        return pl.ds(start * size, size)
    return pl.ds(pl.multiple_of(start * size, size), size)


def walk(tables, order):
    rows_count, cols_count, _ = order.shape
    step = one_hot(cols_count, tables[0:1, 0:cols_count])
    across = lax.broadcasted_iota(jnp.int32, (cols_count, cols_count), 1)
    at = lax.broadcasted_iota(jnp.int32, (cols_count, cols_count), 0)
    found = jnp.where(at == 0, 1.0, 0.0)
    bits = (cols_count - 1).bit_length()
    for bit in range(bits):
        moved = dot(step, found.astype(bf16))
        found = jnp.where((across >> bit) & 1 == 1, moved, found)
        if bit < bits - 1:
            step = dot(step, step).astype(bf16)
    order[0] = found.astype(bf16)

    def next_row(row):
        north = tables[2:3, span(row, cols_count)] - (row + 1) * cols_count
        order[row + 1] = dot(one_hot(cols_count, north), order[row]).astype(bf16)

    each(rows_count - 1, next_row)


def sea_matrix(wet, row, cols_count, before, count):
    here = jnp.broadcast_to(wet[0:1, span(row, cols_count)].astype(f32), (SUBLANES, cols_count))
    at = lax.broadcasted_iota(jnp.int32, (cols_count, cols_count), 0)
    across = lax.broadcasted_iota(jnp.int32, (cols_count, cols_count), 1)
    upper = jnp.where(at <= across, 1.0, 0.0).astype(bf16)
    place = dot(here.astype(bf16), upper)[0:1] + before
    place = jnp.where(here[0:1] > 0.0, place - 1.0, -1.0).astype(jnp.int32)
    return one_hot(count, place), before + jnp.sum(here[0:1], axis=1, keepdims=True)


def face_at(cell, onward, curve, weights):
    rate, lean, bend, forward = weights
    estimate = cell + lean * (onward - cell) - bend * curve
    return jnp.clip(estimate, jnp.minimum(cell, onward), jnp.maximum(cell, onward))


def advect_east(cell, weights):
    size = cell.shape[1]
    onward = pltpu.roll(cell, size - 1, 1)
    slope = onward - cell
    bent = slope - pltpu.roll(slope, 1, 1)
    curve = jnp.where(weights[3], bent, pltpu.roll(bent, size - 1, 1))
    face = face_at(cell, onward, curve, weights)
    return cell - weights[0] * (face - pltpu.roll(face, 1, 1))


def rate_weights(courant, which, steps):
    rate = column(courant[which : which + 1, :]) / steps.astype(f32)
    return rate, 0.5 - 0.5 * rate, (1.0 - rate * rate) / 6.0, rate >= 0.0


def advance(field, sea, weights_east, weights_north, scratch):
    rows_count = field.shape[0]
    moved, faces = scratch

    def east(row):
        moved[row] = advect_east(field[row], weights_east)

    each(rows_count, east)

    def face(row):
        ahead, second, behind = ((row + k + rows_count) % rows_count for k in (1, 2, -1))
        cell, onward = moved[row], moved[ahead]
        slope = onward - cell
        curve = jnp.where(
            weights_north[3],
            slope - (cell - moved[behind]),
            (moved[second] - onward) - slope,
        )
        faces[row] = face_at(cell, onward, curve, weights_north)

    each(rows_count, face)

    def north(row):
        behind = (row - 1 + rows_count) % rows_count
        field[row] = (moved[row] - weights_north[0] * (faces[row] - faces[behind])) * sea[row]

    each(rows_count, north)


def propagate_kernel(
    share,
    spectra,
    courant,
    wind,
    tables,
    wet,
    send,
    recv,
    steps,
    spectra_b,
    tables_b,
    wet_b,
    send_b,
    recv_b,
    steps_b,
    pieces,
    order,
    order_b,
    field,
    field_b,
    moved,
    faces,
    sea,
    sea_b,
    out_cols,
):
    rows_count, bins, cols_count = field.shape
    sea_count = out_cols.shape[1]
    listed = send.shape[1]
    walk(tables, order)
    walk(tables_b, order_b)

    def sent(raw, list_ref):
        total = jnp.zeros((2 * bins, listed), f32)

        def add(row, total):
            own = one_hot(cols_count, list_ref[...] - row * cols_count)
            return total + dot(split(raw[:, span(row, cols_count)]), own)

        if rows_count <= 8:
            for row in range(rows_count):
                total = add(row, total)
        else:
            total = lax.fori_loop(0, rows_count, add, total)
        return total.astype(bf16)

    def start(raw, incoming, wet_ref, recv_ref, order_ref, sea_ref, field_ref):
        def place(row):
            into = one_hot(cols_count, recv_ref[...] - row * cols_count)
            taken = dot_t(jnp.ones((SUBLANES, listed), bf16), into)[0:1] > 0.5
            here = wet_ref[0:1, span(row, cols_count)].astype(f32)
            values = jnp.where(
                taken, joined(dot_t(incoming, into)), raw[:, span(row, cols_count)] * here
            )
            field_ref[row] = joined(dot(split(values), order_ref[row]))
            wide = jnp.broadcast_to(here, (SUBLANES, cols_count)).astype(bf16)
            sea_ref[row] = dot(wide, order_ref[row])[0:1]

        each(rows_count, place)

    from_b = sent(spectra_b, send_b)
    from_a = sent(spectra, send)
    start(spectra, from_b, wet, recv, order, sea, field)
    start(spectra_b, from_a, wet_b, recv_b, order_b, sea_b, field_b)
    east_a = rate_weights(courant, 0, steps[...])
    north_a = rate_weights(courant, 1, steps[...])
    advance(field, sea, east_a, north_a, (moved, faces))
    advance(
        field_b,
        sea_b,
        rate_weights(courant, 0, steps_b[...]),
        rate_weights(courant, 1, steps_b[...]),
        (moved, faces),
    )

    def add_b(row, total):
        plain = dot_t(split(field_b[row]), order_b[row]).astype(bf16)
        return total + dot(plain, one_hot(cols_count, send_b[...] - row * cols_count))

    total = jnp.zeros((2 * bins, listed), f32)
    if rows_count <= 8:
        for row in range(rows_count):
            total = add_b(row, total)
    else:
        total = lax.fori_loop(0, rows_count, add_b, total)
    from_b = total.astype(bf16)

    def take(row):
        into = one_hot(cols_count, recv[...] - row * cols_count)
        taken = dot_t(jnp.ones((SUBLANES, listed), bf16), into).astype(bf16)
        taken = dot(taken, order[row])[0:1] > 0.5
        incoming = joined(dot(dot_t(from_b, into).astype(bf16), order[row]))
        old = field[row]
        field_b[row] = old
        field[row] = jnp.where(taken, incoming, old)

    each(rows_count, take)
    advance(field, sea, east_a, north_a, (moved, faces))
    second = steps[...] > 1

    def gather(row, carry):
        total, before = carry
        picks, before = sea_matrix(wet, row, cols_count, before, sea_count)
        last = jnp.where(second, field[row], field_b[row])
        plain = dot_t(split(last), order[row]).astype(bf16)
        blown = jnp.broadcast_to(wind[0:1, span(row, cols_count)], (SUBLANES, cols_count))
        return total + dot_t(jnp.concatenate([plain, split(blown)], axis=0), picks), before

    carry = (jnp.zeros((2 * bins + 2 * SUBLANES, sea_count), f32), jnp.zeros((1, 1), f32))
    if rows_count <= 8:
        for row in range(rows_count):
            carry = gather(row, carry)
    else:
        carry = lax.fori_loop(0, rows_count, gather, carry)
    total = carry[0]
    out_cols[0:bins] = joined(total[: 2 * bins])
    out_cols[bins : bins + SUBLANES] = joined(total[2 * bins :])

    per = LANES // share
    block = bins // (per - 1)
    lane_group = lax.broadcasted_iota(jnp.int32, (block, LANES), 1) // share

    def fold(tile):
        columns = out_cols[:, span(tile, LANES)]
        for j in range(per):
            last = jnp.broadcast_to(columns[bins : bins + 1], (block, LANES))
            piece = pltpu.roll(last, (per - 1 - j) * share, 1)
            for q in range(per - 1):
                part = columns[q * block : (q + 1) * block]
                if q != j:
                    part = pltpu.roll(part, ((q - j) % per) * share, 1)
                piece = jnp.where(lane_group == q, part, piece)
            pieces[tile * per + j] = piece

    each(sea_count // LANES, fold)


def integrate_kernel(share, pieces, coupling, growth, dissipation, out, values, push, drag):
    devices, block, _ = pieces.shape
    per = LANES // share
    size = coupling.shape[0]
    bins = size // devices
    groups = -(-bins // block)

    def rows(device, q):
        start = device * bins + q * block
        return pl.ds(start if isinstance(start, int) else pl.multiple_of(start, bins & -bins), block)

    blown = pltpu.roll(pieces[0, 0:SUBLANES], share, 1)[0:1]

    def unfold(source):
        piece = pieces[source]
        for q in range(groups):
            part = piece if q == 0 else pltpu.roll(piece, LANES - q * share, 1)
            values[rows(source, q)] = part

    each(devices, unfold)

    def rates(chunk):
        here = span(chunk, LANES)
        push[here] = 1.0 + source_dt * (column(growth[0:1, here]) * blown)
        drag[here] = jnp.broadcast_to(source_dt * column(dissipation[0:1, here]), (LANES, LANES))

    each(size // LANES, rates)
    for repeat in range(SRC):
        now = values[0:size]
        linear = dot(coupling[...], now.astype(bf16))
        spread = jnp.sqrt(jnp.mean(now * now, axis=0, keepdims=True) + tiny_add)
        values[0:size] = (now * push[...] + source_dt * linear) / (1.0 + drag[...] * spread)

    lane_group = lax.broadcasted_iota(jnp.int32, (block, LANES), 1) // share

    def fold(target):
        piece = values[rows(target, 0)]
        for q in range(1, groups):
            part = pltpu.roll(values[rows(target, q)], q * share, 1)
            piece = jnp.where(lane_group == q, part, piece)
        out[target] = piece

    each(devices, fold)


def spread_kernel(share, pieces, wet, out, columns):
    devices, block, _ = pieces.shape
    per = LANES // share
    sea_count = devices * share
    points = wet.shape[1]
    rows_count, cols_count = grid_shape(points)
    lane_group = lax.broadcasted_iota(jnp.int32, (block, LANES), 1) // share

    def unfold(tile):
        for q in range(per - 1):
            part = jnp.zeros((block, LANES), f32)
            for j in range(per):
                piece = pieces[tile * per + j]
                if j != q:
                    piece = pltpu.roll(piece, ((j - q) % per) * share, 1)
                part = jnp.where(lane_group == j, piece, part)
            columns[q * block : (q + 1) * block, span(tile, LANES)] = part

    each(sea_count // LANES, unfold)
    terms = split(columns[...])

    def scatter(row, before):
        picks, before = sea_matrix(wet, row, cols_count, before, sea_count)
        out[:, span(row, cols_count)] = joined(dot(terms, picks))
        return before

    before = jnp.zeros((1, 1), f32)
    if rows_count <= 8:
        for row in range(rows_count):
            before = scatter(row, before)
    else:
        lax.fori_loop(0, rows_count, scatter, before)


def call(kernel, out_shape, scratch, operands, flops):
    held = sum(x.size * x.dtype.itemsize for x in operands)
    return pl.pallas_call(
        kernel,
        out_shape=out_shape,
        in_specs=[pl.BlockSpec(memory_space=pltpu.VMEM)] * len(operands),
        out_specs=pl.BlockSpec(memory_space=pltpu.VMEM),
        scratch_shapes=scratch,
        compiler_params=pltpu.CompilerParams(vmem_limit_bytes=min(56 << 20, (24 << 20) + 2 * held)),
        cost_estimate=pl.CostEstimate(flops=flops, bytes_accessed=held, transcendentals=0),
    )(*operands)


def local(
    spectra,
    courant,
    coupling,
    growth,
    dissipation,
    wind,
    neighbours,
    wet_mask,
    send_list,
    recv_list,
    substep_count,
):
    devices = lax.axis_size("bin")
    field = spectra[0]
    bins_here, points = field.shape
    rows_count, cols_count = grid_shape(points)
    sea_count = points // 2
    share = sea_count // devices
    per = LANES // share
    bins = up_to(bins_here, SUBLANES * (per - 1))
    extra = bins - bins_here
    if extra:
        field = jnp.pad(field, ((0, extra), (0, 0)))
        courant = jnp.pad(courant, ((0, 0), (0, extra)))
    own = (field, neighbours[0], wet_mask, send_list, recv_list, substep_count.reshape(1, 1))
    other = [lax.ppermute(x, "nest", [(0, 1), (1, 0)]) for x in own]
    grid = (rows_count, bins, cols_count)
    operands = (own[0], courant, wind, *own[1:], *other)
    pieces = call(
        functools.partial(propagate_kernel, share),
        jax.ShapeDtypeStruct((devices, bins // (per - 1), LANES), f32),
        [
            pltpu.VMEM((rows_count, cols_count, cols_count), bf16),
            pltpu.VMEM((rows_count, cols_count, cols_count), bf16),
            pltpu.VMEM(grid, f32),
            pltpu.VMEM(grid, f32),
            pltpu.VMEM(grid, f32),
            pltpu.VMEM(grid, f32),
            pltpu.VMEM((rows_count, 1, cols_count), f32),
            pltpu.VMEM((rows_count, 1, cols_count), f32),
            pltpu.VMEM((bins + SUBLANES, sea_count), f32),
        ],
        operands,
        10**9,
    )
    pieces = lax.all_to_all(pieces, "bin", split_axis=0, concat_axis=0)
    size = devices * bins_here
    pieces = call(
        functools.partial(integrate_kernel, share),
        jax.ShapeDtypeStruct(pieces.shape, f32),
        [pltpu.VMEM((size + bins, LANES), f32), *[pltpu.VMEM((size, LANES), f32)] * 2],
        (pieces, coupling, growth.reshape(1, size), dissipation.reshape(1, size)),
        10**9,
    )
    pieces = lax.all_to_all(pieces, "bin", split_axis=0, concat_axis=0)
    result = call(
        functools.partial(spread_kernel, share),
        jax.ShapeDtypeStruct((bins, points), f32),
        [pltpu.VMEM((bins, sea_count), f32)],
        (pieces, wet_mask),
        10**8,
    )
    return result[None, :bins_here]


def solution(mesh):
    in_specs = (
        P("nest", "bin", None),
        P(None, "bin"),
        P(),
        P(),
        P(),
        P("nest", None),
        P("nest", None, None),
        P("nest", None),
        P("nest", None),
        P("nest", None),
        P("nest"),
    )
    out_specs = P("nest", "bin", None)
    return jax.shard_map(local, mesh=mesh, in_specs=in_specs, out_specs=out_specs, check_vma=False)
```

time: 266 us -> 59.7 us (0.22)
  local copies, waits for them, and re-layouts: 215 us -> 5.11 us
  Pallas kernels: 0 us -> 21.7 us
  other arithmetic: 10.7 us -> 0 us
  matrix products: 5 us -> 0 us
  loops' own time: 3.96 us -> 0 us
    gather x265 -> x0, local copies, waits for them, and re-layouts: 185 us -> none  [the longest x256 161 us: east_walk(): return (east_index[point], point)]
    pallas_call x0 -> x3, Pallas kernels: none -> 21.7 us  [call(): pl.pallas_call(kernel, out_shape=out_shape, in_specs=[pl.BlockSpec(memory...]
    scatter x5 -> x0, local copies, waits for them, and re-layouts: 13.2 us -> none  [the longest x1 4.31 us: local(): jnp.zeros((points,), jnp.int32).at[ordering]]
    dynamic_update_slice x260 -> x0, local copies, waits for them, and re-layouts: 7.02 us -> none  [the longest x256 6.61 us: grid_order(): walked = lax.scan(east_walk, starts, None, length=cols_count)[1]]
    dot_general x5 -> x0, matrix products: 5 us -> none  [integrate(): jnp.dot(coupling, columns.astype(jnp.bfloat16), preferred_element_type=jn...]
    another operation x2 -> x0, loops' own time: 3.96 us -> none  [the longest x1 2.59 us: grid_order(): starts = lax.scan(north_walk, jnp.int32(0), None, length=rows_count)[1]]
    select_n x265 -> x0, other arithmetic: 3.93 us -> none  [the longest x2 3.07 us: local(): gridded = jnp.where(substep < steps_here, current, gridded)]
  transfers between devices with their start and end apart: 3 -> 7, of which waited for: 2 -> 3; matrix products, arithmetic and copies ran while one was open for 6% -> 0% of each run, Pallas kernels for 0% -> 0%
where the time goes in v1:
time: 59.7 us; the launch traced here: 59.2 us
  Pallas kernels  21.7 us (36%)
  blocking collectives  11.3 us (19%)
  waiting for transfers between devices  10.4 us (17%)
  starting transfers between devices  10 us (17%)
  local copies, waits for them, and re-layouts  5.11 us (9%)
  between operations  0.73 us (1%)
    pallas_call x3, Pallas kernels, call(): pl.pallas_call(kernel, out_shape=out_shape, in_specs=[pl.BlockSpec(memory...  21.7 us
    all_to_all x1, blocking collectives, local(): pieces = lax.all_to_all(pieces, 'bin', split_axis=0, concat_axis=0)  11.3 us
    all_to_all x1, waiting for transfers between devices, local(): pieces = lax.all_to_all(pieces, 'bin', split_axis=0, concat_axis=0)  8.99 us
    all_to_all x1, starting transfers between devices, local(): pieces = lax.all_to_all(pieces, 'bin', split_axis=0, concat_axis=0)  8.27 us
    unnamed x22, local copies, waits for them, and re-layouts  5.1 us
    ppermute x6, starting transfers between devices, local(): other = [lax.ppermute(x, 'nest', [(0, 1), (1, 0)]) for x in own]  1.75 us
    ppermute x6, waiting for transfers between devices, local(): other = [lax.ppermute(x, 'nest', [(0, 1), (1, 0)]) for x in own]  1.37 us
  transfers between devices with their start and end apart: 7, of which 3 were waited for; matrix products, arithmetic and copies ran while one was open for 0% of the time, Pallas kernels for 0%

profile of v1, /device:TPU:0, one launch (start us, length us, event | category | flops | bytes accessed | tf_op | source)
XLA Modules:
  0.0 59.2 jit_solution(8487955486455151616)
XLA Ops:
  0.0 0.0 copy-start.9
  0.0 0.5 collective-permute-start
  0.5 0.1 collective-permute-start.1
  0.5 0.4 collective-permute-start.2
  1.0 0.1 collective-permute-start.3
  1.0 0.4 collective-permute-start.5
  1.5 1.0 %collective-permute-done.5.steps_b = s32[1,1]{1,0:T(1,128)} collective-permute-done((s32[1,1]{1,0:T(1,128)}, s32[1,1]{1,0:T(1,128)}, u32[]{:S(2)}, u32[]{:S(2)}) %collective-permute-start.5) | collective-permute-done | bytes 36 | tf_op jit(solution)/shard_map/ppermute | solution.py:411
  2.4 0.3 collective-permute-start.4
  3.4 0.0 collective-permute-done.3.send_b
  3.4 0.4 collective-permute-done.4.recv_b
  3.8 0.0 collective-permute-done.2.wet_b
  3.8 0.0 collective-permute-done.1.tables_b
  3.8 0.0 collective-permute-done.spectra_b
  3.8 0.0 copy-start
  3.8 0.7 %copy-done = s32[1,1024]{1,0:T(1,128)S(1)} copy-done((s32[1,1024]{1,0:T(1,128)S(1)}, s32[1,1024]{1,0:T(1,128)}, u32[]{:S(2)}) %copy-start) | copy-done | bytes 4120
  4.5 0.0 copy-start.3
  4.5 1.0 %copy-done.3 = f32[1,72,1024]{2,1,0:T(8,128)S(1)} copy-done((f32[1,72,1024]{2,1,0:T(8,128)S(1)}, f32[1,72,1024]{2,1,0:T(8,128)}, u32[]{:S(2)}) %copy-start.3) | copy-done | bytes 294936
  5.4 0.0 copy-start.4
  5.4 0.7 %copy-done.4 = s32[1,4,1024]{2,1,0:T(4,128)S(1)} copy-done((s32[1,4,1024]{2,1,0:T(4,128)S(1)}, s32[1,4,1024]{2,1,0:T(4,128)}, u32[]{:S(2)}) %copy-start.4) | copy-done | bytes 16408
  6.2 0.0 copy-start.5
  6.2 0.7 %copy-done.5 = f32[1,1024]{1,0:T(1,128)S(1)} copy-done((f32[1,1024]{1,0:T(1,128)S(1)}, f32[1,1024]{1,0:T(1,128)}, u32[]{:S(2)}) %copy-start.5) | copy-done | bytes 4120
  6.9 0.0 copy-start.6
  6.9 0.7 %copy-done.6 = f32[2,72]{1,0:T(2,128)S(1)} copy-done((f32[2,72]{1,0:T(2,128)S(1)}, f32[2,72]{1,0:T(2,128)}, u32[]{:S(2)}) %copy-start.6) | copy-done | bytes 600
  7.5 0.0 copy-start.7
  7.5 0.7 %copy-done.7 = s32[1,256]{1,0:T(1,128)S(1)} copy-done((s32[1,256]{1,0:T(1,128)S(1)}, s32[1,256]{1,0:T(1,128)}, u32[]{:S(2)}) %copy-start.7) | copy-done | bytes 1048
  8.2 0.0 copy-start.8
  8.2 0.7 %copy-done.8 = s32[1,256]{1,0:T(1,128)S(1)} copy-done((s32[1,256]{1,0:T(1,128)S(1)}, s32[1,256]{1,0:T(1,128)}, u32[]{:S(2)}) %copy-start.8) | copy-done | bytes 1048
  8.9 0.0 copy-start.10
  8.9 0.0 copy-start.2
  8.9 11.3 %shard_map.109 = f32[16,24,128]{2,1,0:T(8,128)} custom-call(f32[72,1024]{1,0:T(8,128)S(1)} %bitcast.6, f32[2,72]{1,0:T(2,128)S(1)} %copy-done.6, f32[1,1024]{1,0:T(1,128)S(1)} %copy-done.5, s32[4,1024]{1,0:T(4,128)S(1)} %bitcast.8, s32[1,1024]{1,0:T(1,128)S(1)} %copy-done, s32[1,256]{1,0:T(1,128)S(1)} %copy-done.7, s32[1,256]{1,0:T(1,128)S(1)} %copy-done.8, ...), custom_call_target="tpu_custom_call" | custom-call | flops 1000000000 | bytes 639560 | tf_op jit(solution)/shard_map/pallas_call | solution.py:374
  20.2 0.0 copy-start.1
  20.2 8.3 %all-to-all-start = ((f32[16,24,128]{2,1,0:T(8,128)}), f32[16,24,128]{2,1,0:T(8,128)S(1)}, u32[]{:S(2)}, u32[]{:S(2)}) async-start(f32[16,24,128]{2,1,0:T(8,128)} %shard_map.109), calls=%async_computation | async-start | bytes 393216 | tf_op jit(solution)/shard_map/all_to_all | solution.py:431
  28.5 0.0 copy-done.9
  28.5 0.0 copy-done.10
  28.5 9.0 %all-to-all-done.pieces = f32[16,24,128]{2,1,0:T(8,128)S(1)} async-done(((f32[16,24,128]{2,1,0:T(8,128)}), f32[16,24,128]{2,1,0:T(8,128)S(1)}, u32[]{:S(2)}, u32[]{:S(2)}) %all-to-all-start) | async-done | bytes 196640 | tf_op jit(solution)/shard_map/all_to_all | solution.py:431
  37.5 0.0 copy-done.2
  37.5 9.0 %shard_map.110 = f32[16,24,128]{2,1,0:T(8,128)S(1)} custom-call(f32[16,24,128]{2,1,0:T(8,128)S(1)} %all-to-all-done.pieces, bf16[1152,1152]{1,0:T(8,128)(2,1)S(1)} %copy-done.2, f32[1,1152]{1,0:T(1,128)S(1)} %reshape.10.growth, f32[1,1152]{1,0:T(1,128)S(1)} %reshape.11.dissipation), custom_call_target="tpu_custom_call" | custom-call | flops 1000000000 | bytes 2860032 | tf_op jit(solution)/shard_map/pallas_call | solution.py:374
  46.5 11.3 %all_to_all.10.pieces = f32[16,24,128]{2,1,0:T(8,128)S(1)} all-to-all(f32[16,24,128]{2,1,0:T(8,128)S(1)} %shard_map.110), channel_id=1, replica_groups=mesh['nest'=2,'bin'=16] {'bin'}, dimensions={0} | all-to-all | bytes 393216 | tf_op jit(solution)/shard_map/all_to_all | solution.py:440
  57.8 0.0 copy-done.1
  57.8 1.4 %shard_map.111 = f32[72,1024]{1,0:T(8,128)} custom-call(f32[16,24,128]{2,1,0:T(8,128)S(1)} %all_to_all.10.pieces, s32[1,1024]{1,0:T(1,128)S(1)} %copy-done.1), custom_call_target="tpu_custom_call" | custom-call | flops 100000000 | bytes 200704 | tf_op jit(solution)/shard_map/pallas_call | solution.py:374
  (2 shorter events, 0.0 us)
Async XLA Ops:
  0.0 28.5 %copy-start.9 = (f32[1152]{0:T(1024)S(1)}, f32[1152]{0:T(1024)}, u32[]{:S(2)}) copy-start(f32[1152]{0:T(1024)} %param.14) | copy-start | bytes 13828
  0.0 3.8 %collective-permute-start = (f32[72,1024]{1,0:T(8,128)}, f32[72,1024]{1,0:T(8,128)S(1)}, u32[]{:S(2)}, u32[]{:S(2)}) collective-permute-start(f32[72,1024]{1,0:T(8,128)} %bitcast.5), channel_id=1, source_target_pairs={{0,16},{16,0},{1,17},{17,1},{2,18},{18,2},{3,19},{19,3},{4,20},{20... | collective-permute-start | bytes 884744 | tf_op jit(solution)/shard_map/ppermute | solution.py:411
  0.5 3.3 %collective-permute-start.1 = (s32[4,1024]{1,0:T(4,128)}, s32[4,1024]{1,0:T(4,128)S(1)}, u32[]{:S(2)}, u32[]{:S(2)}) collective-permute-start(s32[4,1024]{1,0:T(4,128)} %bitcast.7), channel_id=1, source_target_pairs={{0,16},{16,0},{1,17},{17,1},{2,18},{18,2},{3,19},{19,3},{4,20},{20... | collective-permute-start | bytes 49160 | tf_op jit(solution)/shard_map/ppermute | solution.py:411
  0.5 3.3 %collective-permute-start.2 = (s32[1,1024]{1,0:T(1,128)}, s32[1,1024]{1,0:T(1,128)S(1)}, u32[]{:S(2)}, u32[]{:S(2)}) collective-permute-start(s32[1,1024]{1,0:T(1,128)} %wet.3), channel_id=1, source_target_pairs={{0,16},{16,0},{1,17},{17,1},{2,18},{18,2},{3,19},{19,3},{4,20},{20... | collective-permute-start | bytes 12296 | tf_op jit(solution)/shard_map/ppermute | solution.py:411
  1.0 2.4 %collective-permute-start.3 = (s32[1,256]{1,0:T(1,128)}, s32[1,256]{1,0:T(1,128)S(1)}, u32[]{:S(2)}, u32[]{:S(2)}) collective-permute-start(s32[1,256]{1,0:T(1,128)} %send.1), channel_id=1, source_target_pairs={{0,16},{16,0},{1,17},{17,1},{2,18},{18,2},{3,19},{19,3},{4,20},{20... | collective-permute-start | bytes 3080 | tf_op jit(solution)/shard_map/ppermute | solution.py:411
  1.0 1.4 %collective-permute-start.5 = (s32[1,1]{1,0:T(1,128)}, s32[1,1]{1,0:T(1,128)}, u32[]{:S(2)}, u32[]{:S(2)}) collective-permute-start(s32[1,1]{1,0:T(1,128)} %bitcast.2), channel_id=1, source_target_pairs={{0,16},{16,0},{1,17},{17,1},{2,18},{18,2},{3,19},{19,3},{4,20},{20... | collective-permute-start | bytes 20 | tf_op jit(solution)/shard_map/ppermute | solution.py:411
  2.4 1.4 %collective-permute-start.4 = (s32[1,256]{1,0:T(1,128)}, s32[1,256]{1,0:T(1,128)S(1)}, u32[]{:S(2)}, u32[]{:S(2)}) collective-permute-start(s32[1,256]{1,0:T(1,128)} %recv.1), channel_id=1, source_target_pairs={{0,16},{16,0},{1,17},{17,1},{2,18},{18,2},{3,19},{19,3},{4,20},{20... | collective-permute-start | bytes 3080 | tf_op jit(solution)/shard_map/ppermute | solution.py:411
  3.8 0.7 %copy-start = (s32[1,1024]{1,0:T(1,128)S(1)}, s32[1,1024]{1,0:T(1,128)}, u32[]{:S(2)}) copy-start(s32[1,1024]{1,0:T(1,128)} %wet.3) | copy-start | bytes 12292
  4.5 1.0 %copy-start.3 = (f32[1,72,1024]{2,1,0:T(8,128)S(1)}, f32[1,72,1024]{2,1,0:T(8,128)}, u32[]{:S(2)}) copy-start(f32[1,72,1024]{2,1,0:T(8,128)} %param.11) | copy-start | bytes 884740
  5.4 0.7 %copy-start.4 = (s32[1,4,1024]{2,1,0:T(4,128)S(1)}, s32[1,4,1024]{2,1,0:T(4,128)}, u32[]{:S(2)}) copy-start(s32[1,4,1024]{2,1,0:T(4,128)} %param.17) | copy-start | bytes 49156
  6.2 0.7 %copy-start.5 = (f32[1,1024]{1,0:T(1,128)S(1)}, f32[1,1024]{1,0:T(1,128)}, u32[]{:S(2)}) copy-start(f32[1,1024]{1,0:T(1,128)} %wind.1) | copy-start | bytes 12292
  6.9 0.7 %copy-start.6 = (f32[2,72]{1,0:T(2,128)S(1)}, f32[2,72]{1,0:T(2,128)}, u32[]{:S(2)}) copy-start(f32[2,72]{1,0:T(2,128)} %courant.1) | copy-start | bytes 1732
  7.5 0.7 %copy-start.7 = (s32[1,256]{1,0:T(1,128)S(1)}, s32[1,256]{1,0:T(1,128)}, u32[]{:S(2)}) copy-start(s32[1,256]{1,0:T(1,128)} %send.1) | copy-start | bytes 3076
  8.2 0.7 %copy-start.8 = (s32[1,256]{1,0:T(1,128)S(1)}, s32[1,256]{1,0:T(1,128)}, u32[]{:S(2)}) copy-start(s32[1,256]{1,0:T(1,128)} %recv.1) | copy-start | bytes 3076
  8.9 19.6 %copy-start.10 = (f32[1152]{0:T(1024)S(1)}, f32[1152]{0:T(1024)}, u32[]{:S(2)}) copy-start(f32[1152]{0:T(1024)} %param.15) | copy-start | bytes 13828
  8.9 28.6 %copy-start.2 = (bf16[1152,1152]{1,0:T(8,128)(2,1)S(1)}, bf16[1152,1152]{1,0:T(8,128)(2,1)}, u32[]{:S(2)}) copy-start(bf16[1152,1152]{1,0:T(8,128)(2,1)} %coupling.1) | copy-start | bytes 7962628
  20.2 37.6 %copy-start.1 = (s32[1,1024]{1,0:T(1,128)S(1)}, s32[1,1024]{1,0:T(1,128)}, u32[]{:S(2)}) copy-start(s32[1,1024]{1,0:T(1,128)} %wet.3) | copy-start | bytes 12292
  20.2 17.3 %all-to-all-start = ((f32[16,24,128]{2,1,0:T(8,128)}), f32[16,24,128]{2,1,0:T(8,128)S(1)}, u32[]{:S(2)}, u32[]{:S(2)}) async-start(f32[16,24,128]{2,1,0:T(8,128)} %shard_map.109), calls=%async_computation | async-start | bytes 393216 | tf_op jit(solution)/shard_map/all_to_all | solution.py:431

commit v2 on v1

v2 whole, which is shorter than its diff:
```python
import functools
import math

import jax
import jax.numpy as jnp
from jax import lax
from jax.experimental import pallas as pl
from jax.experimental.pallas import tpu as pltpu
from jax.sharding import PartitionSpec as P

SUBSTEPS = 2
SRC = 5
LANES = 128
SUBLANES = 8

source_dt = 0.25
tiny_add = 1e-06
f32 = jnp.float32
bf16 = jnp.bfloat16


def up_to(value, unit):
    return -(-value // unit) * unit


def grid_shape(points):
    cols_count = min(256, points // 4)
    return points // cols_count, cols_count


def dot(left, right):
    return jnp.dot(left, right, preferred_element_type=f32)


def dot_t(left, right):
    return lax.dot_general(left, right, (((1,), (1,)), ((), ())), preferred_element_type=f32)


def split(values):
    rest = values - values.astype(bf16).astype(f32)
    return jnp.concatenate([values, rest], axis=0).astype(bf16)


def joined(terms):
    half = terms.shape[0] // 2
    return terms[:half] + terms[half:]


def one_hot(rows, index):
    at = lax.broadcasted_iota(jnp.int32, (rows, index.shape[1]), 0)
    return jnp.where(at == index, 1.0, 0.0).astype(bf16)


def column(row):
    size = row.shape[1]
    at = lax.broadcasted_iota(jnp.int32, (size, size), 0)
    across = lax.broadcasted_iota(jnp.int32, (size, size), 1)
    return jnp.sum(jnp.where(at == across, row, 0.0), axis=1, keepdims=True)


def each(count, body):
    if count <= 16:
        for step in range(count):
            body(step)
    else:
        pl.loop(0, count)(body)


def total_of(count, shape, term):
    total = jnp.zeros(shape, f32)
    if count <= 16:
        for step in range(count):
            total = total + term(step)
        return total
    return lax.fori_loop(0, count, lambda step, total: total + term(step), total)


def span(start, size):
    if isinstance(start, int):
        return pl.ds(start * size, size)
    return pl.ds(pl.multiple_of(start * size, size), size)


def walk(tables, order):
    rows_count, cols_count, _ = order.shape
    step = one_hot(cols_count, tables[0:1, 0:cols_count])
    across = lax.broadcasted_iota(jnp.int32, (cols_count, cols_count), 1)
    at = lax.broadcasted_iota(jnp.int32, (cols_count, cols_count), 0)
    found = jnp.where(at == 0, 1.0, 0.0)
    bits = (cols_count - 1).bit_length()
    for bit in range(bits):
        moved = dot(step, found.astype(bf16))
        found = jnp.where((across >> bit) & 1 == 1, moved, found)
        if bit < bits - 1:
            step = dot(step, step).astype(bf16)
    order[0] = found.astype(bf16)

    def next_row(row):
        north = tables[2:3, span(row, cols_count)] - (row + 1) * cols_count
        order[row + 1] = dot(one_hot(cols_count, north), order[row]).astype(bf16)

    each(rows_count - 1, next_row)


def down(row):
    wide = jnp.broadcast_to(row.astype(f32), (LANES, row.shape[1]))
    return jnp.transpose(wide).astype(jnp.int32)


def one_hot_across(index, first, count):
    lane = lax.broadcasted_iota(jnp.int32, index.shape, 1)
    tiles = [
        jnp.where(lane + (first + tile * LANES) == index, 1.0, 0.0).astype(bf16)
        for tile in range(count // LANES)
    ]
    return jnp.concatenate(tiles, axis=1)


def eight(row):
    return jnp.broadcast_to(row, (SUBLANES, row.shape[1]))


def face_at(cell, onward, curve, rate):
    estimate = cell + (0.5 - 0.5 * rate) * (onward - cell) - (1.0 - rate * rate) / 6.0 * curve
    return jnp.clip(estimate, jnp.minimum(cell, onward), jnp.maximum(cell, onward))


def advance(field, moved, faces, sea, rate_east, rate_north):
    rows_count, _, cols_count = field.shape

    def east(row):
        cell = field[row]
        onward = pltpu.roll(cell, cols_count - 1, 1)
        slope = onward - cell
        bent = slope - pltpu.roll(slope, 1, 1)
        curve = jnp.where(rate_east >= 0.0, bent, pltpu.roll(bent, cols_count - 1, 1))
        face = face_at(cell, onward, curve, rate_east)
        moved[row] = cell - rate_east * (face - pltpu.roll(face, 1, 1))

    each(rows_count, east)

    def face(row):
        ahead, second, behind = ((row + k + rows_count) % rows_count for k in (1, 2, -1))
        cell, onward = moved[row], moved[ahead]
        slope = onward - cell
        curve = jnp.where(
            rate_north >= 0.0, slope - (cell - moved[behind]), (moved[second] - onward) - slope
        )
        faces[row] = face_at(cell, onward, curve, rate_north)

    each(rows_count, face)

    def north(row):
        behind = (row - 1 + rows_count) % rows_count
        field[row] = (moved[row] - rate_north * (faces[row] - faces[behind])) * sea[row]

    each(rows_count, north)


def landing(row, into, order, lists):
    if into.shape[0] == order.shape[0]:
        return into[row]
    cols_count = order.shape[2]
    here = one_hot_across(down(lists[1:2]), row * cols_count, cols_count)
    return dot(here, order[row]).astype(bf16)


def prepare_kernel(
    spectra_in,
    courant_in,
    tables_in,
    wet_in,
    send_in,
    recv_in,
    steps,
    order,
    base,
    into,
    sea,
    taken,
    rates,
    lists,
    spectra,
    courant,
    tables,
    wet,
    arrived,
):
    copies = [
        pltpu.make_async_copy(source, target, arrived.at[which])
        for which, (source, target) in enumerate(
            (
                (tables_in, tables),
                (send_in, lists.at[0:1]),
                (recv_in, lists.at[1:2]),
                (wet_in, wet),
                (courant_in, courant),
                (spectra_in, spectra),
            )
        )
    ]
    for copy in copies:
        copy.start()
    rows_count, bins, cols_count = base.shape
    listed = lists.shape[1]
    copies[0].wait()
    walk(tables, order)
    for copy in copies[1:]:
        copy.wait()
    recv_down = down(lists[1:2])
    count = steps[0, 0]
    second = jnp.where(count > 1, 1.0, 0.0)

    def place(row):
        own = order[row]
        here = one_hot_across(recv_down, row * cols_count, cols_count)
        if into.shape[0] == rows_count:
            into[row] = dot(here, own).astype(bf16)
        got = dot(jnp.ones((SUBLANES, listed), bf16), here)[0:1]
        taken[row] = dot(eight(got).astype(bf16), own)[0:1] * second
        covered = wet[0:1, span(row, cols_count)].astype(f32)
        sea[row] = dot(eight(covered).astype(bf16), own)[0:1]
        values = spectra[:, span(row, cols_count)] * (covered * (1.0 - got))
        base[row] = joined(dot(split(values), own))

    each(rows_count, place)
    for which in range(2):
        rate = column(courant[which : which + 1, :]) / count.astype(f32)
        rates[which] = jnp.broadcast_to(rate, (bins, cols_count))
        rates[2 + which] = jnp.broadcast_to(rate * second, (bins, cols_count))


def first_kernel(
    base, into, order, sea, rates, lists, spectra_b, send_b, field, outgoing, moved, faces
):
    rows_count, bins, cols_count = base.shape
    listed = lists.shape[1]

    def sent(row):
        own = one_hot(cols_count, send_b[...] - row * cols_count)
        return dot(split(spectra_b[:, span(row, cols_count)]), own)

    incoming = total_of(rows_count, (2 * bins, listed), sent).astype(bf16)

    def take(row):
        field[row] = base[row] + joined(dot(incoming, landing(row, into, order, lists)))

    each(rows_count, take)
    advance(field, moved, faces, sea, rates[0], rates[1])

    def sending(row):
        plain = dot_t(split(field[row]), order[row]).astype(bf16)
        return dot(plain, one_hot(cols_count, lists[0:1] - row * cols_count))

    outgoing[...] = joined(total_of(rows_count, (2 * bins, listed), sending))


def picked(row, ranks, picks, sea_count):
    if picks.shape[0] == ranks.shape[0]:
        return picks[row]
    return one_hot_across(down(ranks[row] - 1.0), 0, sea_count)


def places_kernel(order, sea, wind, ranks, picks, place, blown):
    rows_count, cols_count, _ = order.shape
    sea_count = blown.shape[1]
    at = lax.broadcasted_iota(jnp.int32, (cols_count, cols_count), 0)
    across = lax.broadcasted_iota(jnp.int32, (cols_count, cols_count), 1)
    upper = jnp.where(at <= across, 1.0, 0.0).astype(bf16)

    def number(row, before):
        here = sea[row]
        rank = dot(eight(here).astype(bf16), upper)[0:1] + before
        rank = jnp.where(here > 0.0, rank, 0.0)
        ranks[row] = rank
        if picks.shape[0] == rows_count:
            picks[row] = one_hot_across(down(rank - 1.0), 0, sea_count)
        high = jnp.floor(rank * (1.0 / cols_count))
        digits = jnp.concatenate([eight(high), eight(rank - high * cols_count)], axis=0)
        plain = dot_t(digits.astype(bf16), order[row])
        plain = plain[0:1] * cols_count + plain[SUBLANES : SUBLANES + 1]
        place[0:1, span(row, cols_count)] = plain.astype(jnp.int32)
        return before + jnp.sum(here, axis=1, keepdims=True)

    before = jnp.zeros((1, 1), f32)
    if rows_count <= 16:
        for row in range(rows_count):
            before = number(row, before)
    else:
        lax.fori_loop(0, rows_count, number, before)

    def there(row):
        terms = split(eight(wind[0:1, span(row, cols_count)]))
        by_grid = dot(terms, order[row]).astype(bf16)
        return dot(by_grid, picked(row, ranks, picks, sea_count))

    blown[...] = joined(total_of(rows_count, (2 * SUBLANES, sea_count), there))


def second_kernel(
    share,
    field_in,
    incoming,
    into,
    order,
    lists,
    taken,
    sea,
    rates,
    ranks,
    picks,
    blown,
    pieces,
    field,
    moved,
    faces,
    columns,
):
    rows_count, bins, cols_count = field.shape
    sea_count = blown.shape[1]
    terms = split(incoming[...])

    def take(row):
        got = joined(dot(terms, landing(row, into, order, lists)))
        field[row] = jnp.where(taken[row] > 0.5, got, field_in[row])

    each(rows_count, take)
    advance(field, moved, faces, sea, rates[2], rates[3])

    def at_sea(row):
        return dot(split(field[row]), picked(row, ranks, picks, sea_count))

    columns[...] = joined(total_of(rows_count, (2 * bins, sea_count), at_sea))
    per = LANES // share
    block = bins // (per - 1)
    lane_group = lax.broadcasted_iota(jnp.int32, (block, LANES), 1) // share

    def fold(tile):
        winds = jnp.broadcast_to(blown[0:1, span(tile, LANES)], (block, LANES))
        for j in range(per):
            piece = pltpu.roll(winds, (per - 1 - j) * share, 1)
            for q in range(per - 1):
                part = columns[q * block : (q + 1) * block, span(tile, LANES)]
                if q != j:
                    part = pltpu.roll(part, ((q - j) % per) * share, 1)
                piece = jnp.where(lane_group == q, part, piece)
            pieces[tile * per + j] = piece

    each(sea_count // LANES, fold)


def weights_kernel(devices, bins, coupling_in, weights, coupling, rows, sorted_rows, turned, arrived):
    copy = pltpu.make_async_copy(coupling_in, coupling, arrived)
    copy.start()
    copy.wait()
    size = coupling.shape[0]
    block = rows.shape[0] - size
    groups = sorted_rows.shape[0] // (devices * block)
    at = lax.broadcasted_iota(jnp.int32, (block, LANES), 0)
    rows[size:] = jnp.zeros((block, LANES), f32)

    def sort(tile):
        rows[0:size] = tile
        for q in range(groups):
            if q * block >= bins:
                none = jnp.zeros((devices * block, LANES), f32)
                sorted_rows[q * devices * block : (q + 1) * devices * block] = none
                continue

            def move(device, q=q):
                start = device * bins + q * block
                if not isinstance(start, int):
                    start = pl.multiple_of(start, bins & -bins)
                taken = rows[pl.ds(start, block)]
                if (q + 1) * block > bins:
                    taken = jnp.where(at < bins - q * block, taken, 0.0)
                sorted_rows[span(q * devices + device, block)] = taken

            each(devices, move)
        return sorted_rows[...]

    def turn(tile):
        turned[span(tile, LANES)] = jnp.transpose(sort(coupling[:, span(tile, LANES)].astype(f32)))

    def lay(tile):
        weights[:, span(tile, LANES)] = sort(turned[:, span(tile, LANES)]).astype(bf16)

    each(size // LANES, turn)
    each(weights.shape[1] // LANES, lay)


def integrate_kernel(share, total_bins, pieces, weights, rates, out):
    devices, block, _ = pieces.shape
    groups = LANES // share - 1
    width = devices * block
    turned = jnp.transpose(pieces[...].reshape(width, LANES))
    now = jnp.concatenate([turned[q * share : (q + 1) * share] for q in range(groups)], axis=1)
    wind = turned[groups * share :, 0:1]
    push = 1.0 + source_dt * (rates[0:1] * wind)
    drag = source_dt * rates[1:2]
    for repeat in range(SRC):
        linear = dot(now.astype(bf16), weights[...])
        mean = jnp.sum(now * now, axis=1, keepdims=True) * (1.0 / total_bins)
        spread = jnp.sqrt(mean + tiny_add)
        now = (now * push + source_dt * linear) / (1.0 + drag * spread)
    back = [now[:, q * width : (q + 1) * width] for q in range(groups)]
    back.append(jnp.zeros((share, width), f32))
    out[...] = jnp.transpose(jnp.concatenate(back, axis=0)).reshape(devices, block, LANES)


def spread_kernel(share, pieces, place, out, columns):
    devices, block, _ = pieces.shape
    per = LANES // share
    sea_count = devices * share
    points = place.shape[1]
    rows_count, cols_count = grid_shape(points)
    lane_group = lax.broadcasted_iota(jnp.int32, (block, LANES), 1) // share

    def unfold(tile):
        for q in range(per - 1):
            part = jnp.zeros((block, LANES), f32)
            for j in range(per):
                piece = pieces[tile * per + j]
                if j != q:
                    piece = pltpu.roll(piece, ((j - q) % per) * share, 1)
                part = jnp.where(lane_group == j, piece, part)
            columns[q * block : (q + 1) * block, span(tile, LANES)] = part

    each(sea_count // LANES, unfold)
    terms = split(columns[...])

    def scatter(row):
        picks = one_hot(sea_count, place[0:1, span(row, cols_count)] - 1)
        out[:, span(row, cols_count)] = joined(dot(terms, picks))

    each(rows_count, scatter)


def call(kernel, outs, scratch, operands, flops, apart=(), scalar=None):
    held = sum(x.size * x.dtype.itemsize for x in operands)
    single = not isinstance(outs, list)
    shapes = [jax.ShapeDtypeStruct(*out) for out in ([outs] if single else outs)]
    held += sum(x.size * x.dtype.itemsize for x in shapes)
    own = sum(4 * math.prod(getattr(x, "shape", ())) for x in scratch)
    in_vmem = pl.BlockSpec(memory_space=pltpu.VMEM)
    places = [pl.BlockSpec(memory_space=pltpu.HBM) if x in apart else in_vmem for x in range(len(operands))]
    if scalar is not None:
        places[scalar] = pl.BlockSpec(memory_space=pltpu.SMEM)
    operands = [
        x if which == scalar else pltpu.with_memory_space_constraint(x, places[which].memory_space)
        for which, x in enumerate(operands)
    ]
    return pl.pallas_call(
        kernel,
        out_shape=shapes[0] if single else shapes,
        in_specs=places,
        out_specs=in_vmem if single else [in_vmem] * len(shapes),
        scratch_shapes=scratch,
        compiler_params=pltpu.CompilerParams(vmem_limit_bytes=min(60 << 20, (4 << 20) + held + own)),
        cost_estimate=pl.CostEstimate(flops=flops, bytes_accessed=held, transcendentals=0),
    )(*operands)


def local(
    spectra,
    courant,
    coupling,
    growth,
    dissipation,
    wind,
    neighbours,
    wet_mask,
    send_list,
    recv_list,
    substep_count,
):
    devices = lax.axis_size("bin")
    field = spectra[0]
    bins_here, points = field.shape
    rows_count, cols_count = grid_shape(points)
    sea_count = points // 2
    listed = send_list.shape[1]
    share = sea_count // devices
    groups = LANES // share - 1
    bins = up_to(bins_here, SUBLANES * groups)
    block = bins // groups
    size = devices * bins_here
    extra = bins - bins_here
    rates_in = jnp.stack([growth, dissipation]).reshape(2, devices, bins_here)
    if extra:
        field = jnp.pad(field, ((0, extra), (0, 0)))
        courant = jnp.pad(courant, ((0, 0), (0, extra)))
        rates_in = jnp.pad(rates_in, ((0, 0), (0, 0), (0, extra)))
    rates_in = rates_in.reshape(2, devices, groups, block).swapaxes(1, 2).reshape(2, devices * bins)

    def swap(array):
        return lax.ppermute(array, "nest", [(0, 1), (1, 0)])

    spectra_b, send_b = swap(field), swap(send_list)
    grid = (rows_count, bins, cols_count)
    by_point = (rows_count, cols_count, cols_count)
    row_of = (rows_count, 1, cols_count)
    early = (
        field,
        courant,
        neighbours[0],
        wet_mask,
        send_list,
        recv_list,
        substep_count.reshape(1, 1),
    )
    kept_into = rows_count if points * listed <= 1 << 22 else 1
    order, base, into, sea, taken, rates, lists = call(
        prepare_kernel,
        [
            (by_point, bf16),
            (grid, f32),
            ((kept_into, listed, cols_count), bf16),
            (row_of, f32),
            (row_of, f32),
            ((4, bins, cols_count), f32),
            ((2, listed), jnp.int32),
        ],
        [
            *(pltpu.VMEM(x.shape, x.dtype) for x in early[:4]),
            pltpu.SemaphoreType.DMA((6,)),
        ],
        early,
        10**9,
        range(6),
        6,
    )
    field, outgoing = call(
        first_kernel,
        [(grid, f32), ((bins, listed), f32)],
        [pltpu.VMEM(grid, f32)] * 2,
        (base, into, order, sea, rates, lists, spectra_b, send_b),
        10**9,
    )
    incoming = swap(outgoing)
    kept = rows_count if points * sea_count <= 1 << 22 else 1
    ranks, picks, place, blown = call(
        places_kernel,
        [
            (row_of, f32),
            ((kept, cols_count, sea_count), bf16),
            ((1, points), jnp.int32),
            ((SUBLANES, sea_count), f32),
        ],
        [],
        (order, sea, wind),
        10**9,
    )
    pieces = call(
        functools.partial(second_kernel, share),
        ((devices, block, LANES), f32),
        [*[pltpu.VMEM(grid, f32)] * 3, pltpu.VMEM((bins, sea_count), f32)],
        (field, incoming, into, order, lists, taken, sea, rates, ranks, picks, blown),
        10**9,
    )
    pieces = lax.all_to_all(pieces, "bin", split_axis=0, concat_axis=0)
    weights = call(
        functools.partial(weights_kernel, devices, bins_here),
        ((devices * bins, devices * bins), bf16),
        [
            pltpu.VMEM((size, size), bf16),
            pltpu.VMEM((size + block, LANES), f32),
            pltpu.VMEM((devices * bins, LANES), f32),
            pltpu.VMEM((size, devices * bins), f32),
            pltpu.SemaphoreType.DMA,
        ],
        (coupling,),
        10**9,
        (0,),
    )
    pieces = call(
        functools.partial(integrate_kernel, share, size),
        ((devices, block, LANES), f32),
        [],
        (pieces, weights, rates_in),
        10**9,
    )
    pieces = lax.all_to_all(pieces, "bin", split_axis=0, concat_axis=0)
    result = call(
        functools.partial(spread_kernel, share),
        ((bins, points), f32),
        [pltpu.VMEM((bins, sea_count), f32)],
        (pieces, place),
        10**8,
    )
    return result[None, :bins_here]


def solution(mesh):
    in_specs = (
        P("nest", "bin", None),
        P(None, "bin"),
        P(),
        P(),
        P(),
        P("nest", None),
        P("nest", None, None),
        P("nest", None),
        P("nest", None),
        P("nest", None),
        P("nest"),
    )
    out_specs = P("nest", "bin", None)
    return jax.shard_map(local, mesh=mesh, in_specs=in_specs, out_specs=out_specs, check_vma=False)
```

time: 59.7 us -> 42.2 us (0.71)
  Pallas kernels: 21.7 us -> 14.1 us
  local copies, waits for them, and re-layouts: 5.11 us -> 0.29 us
  waiting for transfers between devices: 10.4 us -> 6.19 us
  starting transfers between devices: 10 us -> 9.14 us
    pallas_call x3 -> x7, Pallas kernels: 21.7 us -> 14.1 us  [call(): pl.pallas_call(kernel, out_shape=shapes[0] if single else shapes, in_spec...]
    unnamed x22 -> x6, local copies, waits for them, and re-layouts: 5.1 us -> 0.01 us
    all_to_all x1, waiting for transfers between devices: 8.99 us -> 6.17 us  [local(): pieces = lax.all_to_all(pieces, 'bin', split_axis=0, concat_axis=0)]
    ppermute x6 -> x3, waiting for transfers between devices: 1.37 us -> 0.02 us  [swap(): return lax.ppermute(array, 'nest', [(0, 1), (1, 0)])]
    ppermute x6 -> x3, starting transfers between devices: 1.75 us -> 1.03 us  [swap(): return lax.ppermute(array, 'nest', [(0, 1), (1, 0)])]
  transfers between devices with their start and end apart: 7 -> 4, of which waited for: 3 -> 1; matrix products, arithmetic and copies ran while one was open for 0% -> 1% of each run, Pallas kernels for 0% -> 18%
where the time goes in v2:
time: 42.2 us; the launch traced here: 41.8 us
  Pallas kernels  14.1 us (33%)
  blocking collectives  11.3 us (27%)
  starting transfers between devices  9.14 us (22%)
  waiting for transfers between devices  6.19 us (15%)
  between operations  0.77 us (2%)
    pallas_call x7, Pallas kernels, call(): pl.pallas_call(kernel, out_shape=shapes[0] if single else shapes, in_spec...  14.1 us
    all_to_all x1, blocking collectives, local(): pieces = lax.all_to_all(pieces, 'bin', split_axis=0, concat_axis=0)  11.3 us
    all_to_all x1, starting transfers between devices, local(): pieces = lax.all_to_all(pieces, 'bin', split_axis=0, concat_axis=0)  8.11 us
    all_to_all x1, waiting for transfers between devices, local(): pieces = lax.all_to_all(pieces, 'bin', split_axis=0, concat_axis=0)  6.17 us
    ppermute x3, starting transfers between devices, swap(): return lax.ppermute(array, 'nest', [(0, 1), (1, 0)])  1.03 us
  transfers between devices with their start and end apart: 4, of which 1 were waited for; matrix products, arithmetic and copies ran while one was open for 1% of the time, Pallas kernels for 18%

profile of v2, /device:TPU:0, one launch (start us, length us, event | category | flops | bytes accessed | tf_op | source)
XLA Modules:
  0.0 41.8 jit_solution(7670874744046164791)
XLA Ops:
  0.0 0.5 %collective-permute-start = (f32[72,1024]{1,0:T(8,128)}, f32[72,1024]{1,0:T(8,128)S(1)}, u32[]{:S(2)}, u32[]{:S(2)}) collective-permute-start(f32[72,1024]{1,0:T(8,128)} %bitcast.9), channel_id=1, source_target_pairs={{0,16},{16,0},{1,17},{17,1},{2,18},{18,2},{3,19},{19,3},{4,20},{20... | collective-permute-start | bytes 884744 | tf_op jit(solution)/shard_map/ppermute | solution.py:497
  0.5 0.1 collective-permute-start.1
  1.2 3.9 %shard_map.109 = (bf16[4,256,256]{2,1,0:T(8,128)(2,1)S(1)}, f32[4,72,256]{2,1,0:T(8,128)S(1)}, bf16[4,256,256]{2,1,0:T(8,128)(2,1)S(1)}, f32[4,1,256]{2,1,0:T(1,...) custom-call(f32[72,1024]{1,0:T(8,128)} %bitcast.10, f32[2,72]{1,0:T(2,128)} %courant_in.1, ...), custom_call_target="tpu_custom_call" | custom-call | flops 1000000000 | bytes 1966660 | tf_op jit(solution)/shard_map/pallas_call | solution.py:453
  5.1 0.0 copy-start
  5.1 0.0 collective-permute-done.1.send_b
  5.1 0.0 collective-permute-done.spectra_b
  5.1 1.4 %shard_map.110 = (f32[4,72,256]{2,1,0:T(8,128)S(1)}, f32[72,256]{1,0:T(8,128)S(1)}) custom-call(f32[4,72,256]{2,1,0:T(8,128)S(1)} %get-tuple-element.18.base, bf16[4,256,256]{2,1,0:T(8,128)(2,1)S(1)} %get-tuple-element.19.into, bf16[4,256,256]{2,1,0:T(8,128)(2,1)S(1)} %get-tuple-element.20.order, f32[4,1,256]{2,1,0:T(1,128)S(1)} %get-tuple-element.21.sea, ...), custom_call_target="tpu_custom_call" | custom-call | flops 1000000000 | bytes 2309120 | tf_op jit(solution)/shard_map/pallas_call | solution.py:453
  6.5 0.5 %collective-permute-start.2 = (f32[72,256]{1,0:T(8,128)S(1)}, f32[72,256]{1,0:T(8,128)S(1)}, u32[]{:S(2)}, u32[]{:S(2)}) collective-permute-start(f32[72,256]{1,0:T(8,128)S(1)} %get-tuple-element.25), channel_id=1, source_target_pairs={{0,16},{16,0},{1,17},{17,1},{2,18},{18,2},{3,19},{19,3},{4,20},{20... | collective-permute-start | bytes 221192 | tf_op jit(solution)/shard_map/ppermute | solution.py:497
  7.1 0.0 copy-done
  7.1 1.0 %shard_map.111 = (f32[4,1,256]{2,1,0:T(1,128)S(1)}, bf16[4,256,512]{2,1,0:T(8,128)(2,1)S(1)}, s32[1,1024]{1,0:T(1,128)S(1)}, f32[8,512]{1,0:T(8,128)S(1)}) custom-call(bf16[4,256,256]{2,1,0:T(8,128)(2,1)S(1)} %get-tuple-element.20.order, f32[4,1,256]{2,1,0:T(1,128)S(1)} %get-tuple-element.21.sea, f32[1,1024]{1,0:T(1,128)S(1)} %copy-done), custom_call_target="tpu_custom_call" | custom-call | flops 1000000000 | bytes 1605632 | tf_op jit(solution)/shard_map/pallas_call | solution.py:453
  8.0 0.0 copy-start.1
  8.0 0.0 copy-start.2
  8.0 0.0 collective-permute-done.2.incoming
  8.1 1.8 %shard_map.112 = f32[16,24,128]{2,1,0:T(8,128)} custom-call(f32[4,72,256]{2,1,0:T(8,128)S(1)} %get-tuple-element.24.field_in, f32[72,256]{1,0:T(8,128)S(1)} %collective-permute-done.2.incoming, bf16[4,256,256]{2,1,0:T(8,128)(2,1)S(1)} %get-tuple-element.19.into, bf16[4,256,256]{2,1,0:T(8,128)(2,1)S(1)} %get-tuple-element.20.order, ...), custom_call_target="tpu_custom_call" | custom-call | flops 1000000000 | bytes 2988032 | tf_op jit(solution)/shard_map/pallas_call | solution.py:453
  9.9 8.1 %all-to-all-start = ((f32[16,24,128]{2,1,0:T(8,128)}), f32[16,24,128]{2,1,0:T(8,128)S(1)}, u32[]{:S(2)}, u32[]{:S(2)}) async-start(f32[16,24,128]{2,1,0:T(8,128)} %shard_map.112), calls=%async_computation | async-start | bytes 393216 | tf_op jit(solution)/shard_map/all_to_all | solution.py:561
  18.0 0.0 copy-done.1
  18.0 0.1 stack.9
  18.1 0.0 copy-done.2
  18.1 0.1 stack.10
  18.2 0.1 reshape.11.rates
  18.3 2.5 %shard_map.113.weights = bf16[1152,1152]{1,0:T(8,128)(2,1)S(1)} custom-call(bf16[1152,1152]{1,0:T(8,128)(2,1)} %coupling_in.1), custom_call_target="tpu_custom_call" | custom-call | flops 1000000000 | bytes 5308416 | tf_op jit(solution)/shard_map/pallas_call | solution.py:453
  20.9 6.2 %all-to-all-done.pieces = f32[16,24,128]{2,1,0:T(8,128)S(1)} async-done(((f32[16,24,128]{2,1,0:T(8,128)}), f32[16,24,128]{2,1,0:T(8,128)S(1)}, u32[]{:S(2)}, u32[]{:S(2)}) %all-to-all-start) | async-done | bytes 196640 | tf_op jit(solution)/shard_map/all_to_all | solution.py:561
  27.1 2.3 %shard_map.114 = f32[16,24,128]{2,1,0:T(8,128)S(1)} custom-call(f32[16,24,128]{2,1,0:T(8,128)S(1)} %all-to-all-done.pieces, bf16[1152,1152]{1,0:T(8,128)(2,1)S(1)} %shard_map.113.weights, f32[2,1152]{1,0:T(2,128)S(1)} %reshape.11.rates), custom_call_target="tpu_custom_call" | custom-call | flops 1000000000 | bytes 3056640 | tf_op jit(solution)/shard_map/pallas_call | solution.py:453
  29.4 11.3 %all_to_all.10.pieces = f32[16,24,128]{2,1,0:T(8,128)S(1)} all-to-all(f32[16,24,128]{2,1,0:T(8,128)S(1)} %shard_map.114), channel_id=1, replica_groups=mesh['nest'=2,'bin'=16] {'bin'}, dimensions={0} | all-to-all | bytes 393216 | tf_op jit(solution)/shard_map/all_to_all | solution.py:583
  40.6 1.2 %shard_map.115 = f32[72,1024]{1,0:T(8,128)} custom-call(f32[16,24,128]{2,1,0:T(8,128)S(1)} %all_to_all.10.pieces, s32[1,1024]{1,0:T(1,128)S(1)} %get-tuple-element.30.place), custom_call_target="tpu_custom_call" | custom-call | flops 100000000 | bytes 495616 | tf_op jit(solution)/shard_map/pallas_call | solution.py:453
  (2 shorter events, 0.0 us)
Async XLA Ops:
  0.0 5.1 %collective-permute-start = (f32[72,1024]{1,0:T(8,128)}, f32[72,1024]{1,0:T(8,128)S(1)}, u32[]{:S(2)}, u32[]{:S(2)}) collective-permute-start(f32[72,1024]{1,0:T(8,128)} %bitcast.9), channel_id=1, source_target_pairs={{0,16},{16,0},{1,17},{17,1},{2,18},{18,2},{3,19},{19,3},{4,20},{20... | collective-permute-start | bytes 884744 | tf_op jit(solution)/shard_map/ppermute | solution.py:497
  0.5 4.6 %collective-permute-start.1 = (s32[1,256]{1,0:T(1,128)}, s32[1,256]{1,0:T(1,128)S(1)}, u32[]{:S(2)}, u32[]{:S(2)}) collective-permute-start(s32[1,256]{1,0:T(1,128)} %send_in.1), channel_id=1, source_target_pairs={{0,16},{16,0},{1,17},{17,1},{2,18},{18,2},{3,19},{19,3},{4,20},{20... | collective-permute-start | bytes 3080 | tf_op jit(solution)/shard_map/ppermute | solution.py:497
  5.1 2.0 %copy-start = (f32[1,1024]{1,0:T(1,128)S(1)}, f32[1,1024]{1,0:T(1,128)}, u32[]{:S(2)}) copy-start(f32[1,1024]{1,0:T(1,128)} %wind.1) | copy-start | bytes 12292
  6.5 1.5 %collective-permute-start.2 = (f32[72,256]{1,0:T(8,128)S(1)}, f32[72,256]{1,0:T(8,128)S(1)}, u32[]{:S(2)}, u32[]{:S(2)}) collective-permute-start(f32[72,256]{1,0:T(8,128)S(1)} %get-tuple-element.25), channel_id=1, source_target_pairs={{0,16},{16,0},{1,17},{17,1},{2,18},{18,2},{3,19},{19,3},{4,20},{20... | collective-permute-start | bytes 221192 | tf_op jit(solution)/shard_map/ppermute | solution.py:497
  8.0 10.0 %copy-start.1 = (f32[1152]{0:T(1024)S(1)}, f32[1152]{0:T(1024)}, u32[]{:S(2)}) copy-start(f32[1152]{0:T(1024)} %param.14) | copy-start | bytes 13828
  8.0 10.1 %copy-start.2 = (f32[1152]{0:T(1024)S(1)}, f32[1152]{0:T(1024)}, u32[]{:S(2)}) copy-start(f32[1152]{0:T(1024)} %param.15) | copy-start | bytes 13828
  9.9 17.2 %all-to-all-start = ((f32[16,24,128]{2,1,0:T(8,128)}), f32[16,24,128]{2,1,0:T(8,128)S(1)}, u32[]{:S(2)}, u32[]{:S(2)}) async-start(f32[16,24,128]{2,1,0:T(8,128)} %shard_map.112), calls=%async_computation | async-start | bytes 393216 | tf_op jit(solution)/shard_map/all_to_all | solution.py:561

commit v3 on v2

--- a/solution.py
+++ b/solution.py
@@ -79,6 +79,10 @@
     if isinstance(start, int):
         return pl.ds(start * size, size)
     return pl.ds(pl.multiple_of(start * size, size), size)
+
+
+def rows_of(start, size):
+    return pl.ds(start * size, size)
 
 
 def walk(tables, order):
@@ -167,21 +171,17 @@
 
 def prepare_kernel(
     spectra_in,
-    courant_in,
     tables_in,
     wet_in,
     send_in,
     recv_in,
-    steps,
     order,
     base,
     into,
     sea,
     taken,
-    rates,
     lists,
     spectra,
-    courant,
     tables,
     wet,
     arrived,
@@ -194,7 +194,6 @@
                 (send_in, lists.at[0:1]),
                 (recv_in, lists.at[1:2]),
                 (wet_in, wet),
-                (courant_in, courant),
                 (spectra_in, spectra),
             )
         )
@@ -208,8 +207,6 @@
     for copy in copies[1:]:
         copy.wait()
     recv_down = down(lists[1:2])
-    count = steps[0, 0]
-    second = jnp.where(count > 1, 1.0, 0.0)
 
     def place(row):
         own = order[row]
@@ -217,24 +214,39 @@
         if into.shape[0] == rows_count:
             into[row] = dot(here, own).astype(bf16)
         got = dot(jnp.ones((SUBLANES, listed), bf16), here)[0:1]
-        taken[row] = dot(eight(got).astype(bf16), own)[0:1] * second
+        taken[row] = dot(eight(got).astype(bf16), own)[0:1]
         covered = wet[0:1, span(row, cols_count)].astype(f32)
         sea[row] = dot(eight(covered).astype(bf16), own)[0:1]
         values = spectra[:, span(row, cols_count)] * (covered * (1.0 - got))
         base[row] = joined(dot(split(values), own))
 
     each(rows_count, place)
-    for which in range(2):
-        rate = column(courant[which : which + 1, :]) / count.astype(f32)
-        rates[which] = jnp.broadcast_to(rate, (bins, cols_count))
-        rates[2 + which] = jnp.broadcast_to(rate * second, (bins, cols_count))
 
 
 def first_kernel(
-    base, into, order, sea, rates, lists, spectra_b, send_b, field, outgoing, moved, faces
+    base,
+    into,
+    order,
+    sea,
+    lists,
+    spectra_b,
+    send_b,
+    courant,
+    steps,
+    field,
+    outgoing,
+    rates,
+    moved,
+    faces,
 ):
     rows_count, bins, cols_count = base.shape
     listed = lists.shape[1]
+    second = jnp.where(steps[...] > 1, 1.0, 0.0)
+    for which in range(2):
+        rate = column(courant[which : which + 1, :]) / steps[...].astype(f32)
+        rates[which] = jnp.broadcast_to(rate, (bins, cols_count))
+        rates[2 + which] = jnp.broadcast_to(rate * second, (bins, cols_count))
+    rates[4] = jnp.broadcast_to(second, (bins, cols_count))
 
     def sent(row):
         own = one_hot(cols_count, send_b[...] - row * cols_count)
@@ -309,7 +321,6 @@
     rates,
     ranks,
     picks,
-    blown,
     pieces,
     field,
     moved,
@@ -317,12 +328,13 @@
     columns,
 ):
     rows_count, bins, cols_count = field.shape
-    sea_count = blown.shape[1]
+    tiles, _, _ = columns.shape
+    sea_count = tiles * LANES
     terms = split(incoming[...])
 
     def take(row):
         got = joined(dot(terms, landing(row, into, order, lists)))
-        field[row] = jnp.where(taken[row] > 0.5, got, field_in[row])
+        field[row] = jnp.where(taken[row] * rates[4, 0:1] > 0.5, got, field_in[row])
 
     each(rows_count, take)
     advance(field, moved, faces, sea, rates[2], rates[3])
@@ -330,73 +342,107 @@
     def at_sea(row):
         return dot(split(field[row]), picked(row, ranks, picks, sea_count))
 
-    columns[...] = joined(total_of(rows_count, (2 * bins, sea_count), at_sea))
-    per = LANES // share
-    block = bins // (per - 1)
+    total = joined(total_of(rows_count, (2 * bins, sea_count), at_sea))
+    for tile in range(tiles):
+        columns[tile] = total[:, tile * LANES : (tile + 1) * LANES]
+    groups = LANES // share
+    block = pieces.shape[0] // (tiles * groups)
     lane_group = lax.broadcasted_iota(jnp.int32, (block, LANES), 1) // share
 
     def fold(tile):
-        winds = jnp.broadcast_to(blown[0:1, span(tile, LANES)], (block, LANES))
-        for j in range(per):
-            piece = pltpu.roll(winds, (per - 1 - j) * share, 1)
-            for q in range(per - 1):
-                part = columns[q * block : (q + 1) * block, span(tile, LANES)]
+        parts = [columns[tile, pl.ds(q, block, stride=groups)] for q in range(groups)]
+        for j in range(groups):
+            piece = parts[j]
+            for q in range(groups):
                 if q != j:
-                    part = pltpu.roll(part, ((q - j) % per) * share, 1)
-                piece = jnp.where(lane_group == q, part, piece)
-            pieces[tile * per + j] = piece
-
-    each(sea_count // LANES, fold)
-
-
-def weights_kernel(devices, bins, coupling_in, weights, coupling, rows, sorted_rows, turned, arrived):
+                    part = pltpu.roll(parts[q], ((q - j) % groups) * share, 1)
+                    piece = jnp.where(lane_group == q, part, piece)
+            pieces[rows_of(tile * groups + j, block)] = piece
+
+    each(tiles, fold)
+
+
+def weights_kernel(
+    devices,
+    bins,
+    share,
+    coupling_in,
+    growth,
+    dissipation,
+    blown,
+    weights,
+    rates,
+    wind,
+    coupling,
+    rows,
+    sorted_rows,
+    turned,
+    arrived,
+):
     copy = pltpu.make_async_copy(coupling_in, coupling, arrived)
     copy.start()
-    copy.wait()
     size = coupling.shape[0]
-    block = rows.shape[0] - size
-    groups = sorted_rows.shape[0] // (devices * block)
-    at = lax.broadcasted_iota(jnp.int32, (block, LANES), 0)
-    rows[size:] = jnp.zeros((block, LANES), f32)
-
-    def sort(tile):
-        rows[0:size] = tile
+    lane_tiles = size // LANES
+    groups = LANES // share
+    block = sorted_rows.shape[0] // (devices * groups)
+    mine = pltpu.roll(blown[...], blown.shape[1] - lax.axis_index("bin") * share, 1)
+    wind[...] = jnp.broadcast_to(column(mine[0:1, 0:share]), wind.shape)
+    rows[size:] = jnp.zeros((rows.shape[0] - size, LANES), f32)
+
+    def sort():
+        if groups * block == bins:
+            every = devices * block
+            taken = [rows[pl.ds(q, every, stride=groups)] for q in range(groups)]
+            return jnp.concatenate(taken, axis=0)
+        at = groups * lax.broadcasted_iota(jnp.int32, (block, LANES), 0)
         for q in range(groups):
-            if q * block >= bins:
-                none = jnp.zeros((devices * block, LANES), f32)
-                sorted_rows[q * devices * block : (q + 1) * devices * block] = none
-                continue
 
             def move(device, q=q):
-                start = device * bins + q * block
-                if not isinstance(start, int):
-                    start = pl.multiple_of(start, bins & -bins)
-                taken = rows[pl.ds(start, block)]
-                if (q + 1) * block > bins:
-                    taken = jnp.where(at < bins - q * block, taken, 0.0)
-                sorted_rows[span(q * devices + device, block)] = taken
+                taken = rows[pl.ds(device * bins + q, block, stride=groups)]
+                taken = jnp.where(at + q < bins, taken, 0.0)
+                sorted_rows[rows_of(q * devices + device, block)] = taken
 
             each(devices, move)
         return sorted_rows[...]
 
+    at = lax.broadcasted_iota(jnp.int32, (LANES, LANES), 0)
+
+    def lift(tile):
+        here = span(tile, LANES)
+        both = jnp.where(at == 0, growth[0:1, here], jnp.where(at == 1, dissipation[0:1, here], 0.0))
+        rows[here] = jnp.transpose(both)
+
+    each(lane_tiles, lift)
+    rates[...] = jnp.transpose(sort())[0:SUBLANES]
+    copy.wait()
+
     def turn(tile):
-        turned[span(tile, LANES)] = jnp.transpose(sort(coupling[:, span(tile, LANES)].astype(f32)))
+        rows[0:size] = coupling[:, span(tile, LANES)].astype(f32)
+        turned[span(tile, LANES)] = jnp.transpose(sort())
 
     def lay(tile):
-        weights[:, span(tile, LANES)] = sort(turned[:, span(tile, LANES)]).astype(bf16)
-
-    each(size // LANES, turn)
+        rows[0:size] = turned[:, span(tile, LANES)]
+        weights[:, span(tile, LANES)] = sort().astype(bf16)
+
+    each(lane_tiles, turn)
     each(weights.shape[1] // LANES, lay)
 
 
-def integrate_kernel(share, total_bins, pieces, weights, rates, out):
-    devices, block, _ = pieces.shape
-    groups = LANES // share - 1
-    width = devices * block
-    turned = jnp.transpose(pieces[...].reshape(width, LANES))
-    now = jnp.concatenate([turned[q * share : (q + 1) * share] for q in range(groups)], axis=1)
-    wind = turned[groups * share :, 0:1]
-    push = 1.0 + source_dt * (rates[0:1] * wind)
+def padded_transpose(array):
+    rows_count, cols_count = array.shape
+    full = up_to(rows_count, LANES)
+    if full > rows_count:
+        array = jnp.concatenate([array, jnp.zeros((full - rows_count, cols_count), f32)], axis=0)
+    return jnp.transpose(array)
+
+
+def integrate_kernel(share, total_bins, pieces, weights, rates, wind, out):
+    width = pieces.shape[0]
+    groups = LANES // share
+    turned = padded_transpose(pieces[...])
+    now = [turned[q * share : (q + 1) * share, 0:width] for q in range(groups)]
+    now = jnp.concatenate(now, axis=1)
+    push = 1.0 + source_dt * (rates[0:1] * wind[:, 0:1])
     drag = source_dt * rates[1:2]
     for repeat in range(SRC):
         linear = dot(now.astype(bf16), weights[...])
@@ -404,30 +450,36 @@
         spread = jnp.sqrt(mean + tiny_add)
         now = (now * push + source_dt * linear) / (1.0 + drag * spread)
     back = [now[:, q * width : (q + 1) * width] for q in range(groups)]
-    back.append(jnp.zeros((share, width), f32))
-    out[...] = jnp.transpose(jnp.concatenate(back, axis=0)).reshape(devices, block, LANES)
+    back = jnp.concatenate(back, axis=0)
+    full = up_to(width, LANES)
+    if full > width:
+        back = jnp.concatenate([back, jnp.zeros((LANES, full - width), f32)], axis=1)
+    out[...] = jnp.transpose(back)[0:width]
 
 
 def spread_kernel(share, pieces, place, out, columns):
-    devices, block, _ = pieces.shape
-    per = LANES // share
-    sea_count = devices * share
+    tiles, bins, _ = columns.shape
+    groups = LANES // share
+    block = pieces.shape[0] // (tiles * groups)
+    sea_count = tiles * LANES
     points = place.shape[1]
     rows_count, cols_count = grid_shape(points)
     lane_group = lax.broadcasted_iota(jnp.int32, (block, LANES), 1) // share
+    if groups * block < bins:
+        columns[:, groups * block :] = jnp.zeros((tiles, bins - groups * block, LANES), f32)
 
     def unfold(tile):
-        for q in range(per - 1):
-            part = jnp.zeros((block, LANES), f32)
-            for j in range(per):
-                piece = pieces[tile * per + j]
+        parts = [pieces[rows_of(tile * groups + j, block)] for j in range(groups)]
+        for q in range(groups):
+            part = parts[q]
+            for j in range(groups):
                 if j != q:
-                    piece = pltpu.roll(piece, ((j - q) % per) * share, 1)
-                part = jnp.where(lane_group == j, piece, part)
-            columns[q * block : (q + 1) * block, span(tile, LANES)] = part
-
-    each(sea_count // LANES, unfold)
-    terms = split(columns[...])
+                    other = pltpu.roll(parts[j], ((j - q) % groups) * share, 1)
+                    part = jnp.where(lane_group == j, other, part)
+            columns[tile, pl.ds(q, block, stride=groups)] = part
+
+    each(tiles, unfold)
+    terms = jnp.concatenate([split(columns[tile]) for tile in range(tiles)], axis=1)
 
     def scatter(row):
         picks = one_hot(sea_count, place[0:1, span(row, cols_count)] - 1)
@@ -436,7 +488,7 @@
     each(rows_count, scatter)
 
 
-def call(kernel, outs, scratch, operands, flops, apart=(), scalar=None):
+def call(kernel, outs, scratch, operands, flops, apart=()):
     held = sum(x.size * x.dtype.itemsize for x in operands)
     single = not isinstance(outs, list)
     shapes = [jax.ShapeDtypeStruct(*out) for out in ([outs] if single else outs)]
@@ -444,11 +496,9 @@
     own = sum(4 * math.prod(getattr(x, "shape", ())) for x in scratch)
     in_vmem = pl.BlockSpec(memory_space=pltpu.VMEM)
     places = [pl.BlockSpec(memory_space=pltpu.HBM) if x in apart else in_vmem for x in range(len(operands))]
-    if scalar is not None:
-        places[scalar] = pl.BlockSpec(memory_space=pltpu.SMEM)
     operands = [
-        x if which == scalar else pltpu.with_memory_space_constraint(x, places[which].memory_space)
-        for which, x in enumerate(operands)
+        x if x.size == 1 else pltpu.with_memory_space_constraint(x, place.memory_space)
+        for x, place in zip(operands, places)
     ]
     return pl.pallas_call(
         kernel,
@@ -481,17 +531,19 @@
     sea_count = points // 2
     listed = send_list.shape[1]
     share = sea_count // devices
-    groups = LANES // share - 1
-    bins = up_to(bins_here, SUBLANES * groups)
-    block = bins // groups
+    groups = LANES // share
+    block = -(-bins_here // groups)
+    bins = up_to(groups * block, SUBLANES)
     size = devices * bins_here
+    sorted_size = devices * groups * block
     extra = bins - bins_here
-    rates_in = jnp.stack([growth, dissipation]).reshape(2, devices, bins_here)
     if extra:
         field = jnp.pad(field, ((0, extra), (0, 0)))
         courant = jnp.pad(courant, ((0, 0), (0, extra)))
-        rates_in = jnp.pad(rates_in, ((0, 0), (0, 0), (0, extra)))
-    rates_in = rates_in.reshape(2, devices, groups, block).swapaxes(1, 2).reshape(2, devices * bins)
+    def transpose_all(pieces):
+        pieces = pieces.reshape(devices, 1, block * LANES)
+        pieces = lax.all_to_all(pieces, "bin", split_axis=0, concat_axis=0)
+        return pieces.reshape(devices * block, LANES)
 
     def swap(array):
         return lax.ppermute(array, "nest", [(0, 1), (1, 0)])
@@ -502,15 +554,13 @@
     row_of = (rows_count, 1, cols_count)
     early = (
         field,
-        courant,
         neighbours[0],
         wet_mask,
         send_list,
         recv_list,
-        substep_count.reshape(1, 1),
     )
     kept_into = rows_count if points * listed <= 1 << 22 else 1
-    order, base, into, sea, taken, rates, lists = call(
+    order, base, into, sea, taken, lists = call(
         prepare_kernel,
         [
             (by_point, bf16),
@@ -518,23 +568,21 @@
             ((kept_into, listed, cols_count), bf16),
             (row_of, f32),
             (row_of, f32),
-            ((4, bins, cols_count), f32),
             ((2, listed), jnp.int32),
         ],
         [
-            *(pltpu.VMEM(x.shape, x.dtype) for x in early[:4]),
-            pltpu.SemaphoreType.DMA((6,)),
+            *(pltpu.VMEM(x.shape, x.dtype) for x in early[:3]),
+            pltpu.SemaphoreType.DMA((5,)),
         ],
         early,
         10**9,
-        range(6),
-        6,
-    )
-    field, outgoing = call(
+        range(5),
+    )
+    field, outgoing, rates = call(
         first_kernel,
-        [(grid, f32), ((bins, listed), f32)],
+        [(grid, f32), ((bins, listed), f32), ((5, bins, cols_count), f32)],
         [pltpu.VMEM(grid, f32)] * 2,
-        (base, into, order, sea, rates, lists, spectra_b, send_b),
+        (base, into, order, sea, lists, spectra_b, send_b, courant, substep_count.reshape(1, 1)),
         10**9,
     )
     incoming = swap(outgoing)
@@ -551,40 +599,41 @@
         (order, sea, wind),
         10**9,
     )
+    tiles = sea_count // LANES
     pieces = call(
         functools.partial(second_kernel, share),
-        ((devices, block, LANES), f32),
-        [*[pltpu.VMEM(grid, f32)] * 3, pltpu.VMEM((bins, sea_count), f32)],
-        (field, incoming, into, order, lists, taken, sea, rates, ranks, picks, blown),
+        ((devices * block, LANES), f32),
+        [*[pltpu.VMEM(grid, f32)] * 3, pltpu.VMEM((tiles, bins, LANES), f32)],
+        (field, incoming, into, order, lists, taken, sea, rates, ranks, picks),
         10**9,
     )
-    pieces = lax.all_to_all(pieces, "bin", split_axis=0, concat_axis=0)
-    weights = call(
-        functools.partial(weights_kernel, devices, bins_here),
-        ((devices * bins, devices * bins), bf16),
+    pieces = transpose_all(pieces)
+    weights, sorted_rates, wind_here = call(
+        functools.partial(weights_kernel, devices, bins_here, share),
+        [((sorted_size, sorted_size), bf16), ((SUBLANES, sorted_size), f32), ((share, LANES), f32)],
         [
             pltpu.VMEM((size, size), bf16),
-            pltpu.VMEM((size + block, LANES), f32),
-            pltpu.VMEM((devices * bins, LANES), f32),
-            pltpu.VMEM((size, devices * bins), f32),
+            pltpu.VMEM((size + up_to(groups * block, SUBLANES), LANES), f32),
+            pltpu.VMEM((sorted_size, LANES), f32),
+            pltpu.VMEM((size, sorted_size), f32),
             pltpu.SemaphoreType.DMA,
         ],
-        (coupling,),
+        (coupling, growth.reshape(1, size), dissipation.reshape(1, size), blown),
         10**9,
         (0,),
     )
     pieces = call(
         functools.partial(integrate_kernel, share, size),
-        ((devices, block, LANES), f32),
+        ((devices * block, LANES), f32),
         [],
-        (pieces, weights, rates_in),
+        (pieces, weights, sorted_rates, wind_here),
         10**9,
     )
-    pieces = lax.all_to_all(pieces, "bin", split_axis=0, concat_axis=0)
+    pieces = transpose_all(pieces)
     result = call(
         functools.partial(spread_kernel, share),
         ((bins, points), f32),
-        [pltpu.VMEM((bins, sea_count), f32)],
+        [pltpu.VMEM((tiles, bins, LANES), f32)],
         (pieces, place),
         10**8,
     )

time: 42.2 us -> 41.2 us (0.976)
  waiting for transfers between devices: 6.19 us -> 4.23 us
  Pallas kernels: 14.1 us -> 15.7 us
    all_to_all x1, waiting for transfers between devices: 6.17 us -> 4.21 us  [transpose_all(): pieces = lax.all_to_all(pieces, 'bin', split_axis=0, concat_axis=0)]
    pallas_call x7, Pallas kernels: 14.1 us -> 15.7 us  [call(): pl.pallas_call(kernel, out_shape=shapes[0] if single else shapes, in_spec...]
  transfers between devices with their start and end apart: 4 -> 4, of which waited for: 1 -> 1; matrix products, arithmetic and copies ran while one was open for 1% -> 0% of each run, Pallas kernels for 18% -> 21%
where the time goes in v3:
time: 41.2 us; the launch traced here: 40.8 us
  Pallas kernels  15.7 us (38%)
  blocking collectives  11 us (27%)
  starting transfers between devices  9.14 us (22%)
  waiting for transfers between devices  4.23 us (10%)
  between operations  0.78 us (2%)
    pallas_call x7, Pallas kernels, call(): pl.pallas_call(kernel, out_shape=shapes[0] if single else shapes, in_spec...  15.7 us
    all_to_all x1, blocking collectives, transpose_all(): pieces = lax.all_to_all(pieces, 'bin', split_axis=0, concat_axis=0)  11 us
    all_to_all x1, starting transfers between devices, transpose_all(): pieces = lax.all_to_all(pieces, 'bin', split_axis=0, concat_axis=0)  8.11 us
    all_to_all x1, waiting for transfers between devices, transpose_all(): pieces = lax.all_to_all(pieces, 'bin', split_axis=0, concat_axis=0)  4.21 us
    ppermute x3, starting transfers between devices, swap(): return lax.ppermute(array, 'nest', [(0, 1), (1, 0)])  1.03 us
  transfers between devices with their start and end apart: 4, of which 1 were waited for; matrix products, arithmetic and copies ran while one was open for 0% of the time, Pallas kernels for 21%

profile of v3, /device:TPU:0, one launch (start us, length us, event | category | flops | bytes accessed | tf_op | source)
XLA Modules:
  0.0 40.8 jit_solution(16020252277982602431)
XLA Ops:
  0.0 0.0 copy-start.1
  0.0 0.5 %collective-permute-start = (f32[72,1024]{1,0:T(8,128)}, f32[72,1024]{1,0:T(8,128)S(1)}, u32[]{:S(2)}, u32[]{:S(2)}) collective-permute-start(f32[72,1024]{1,0:T(8,128)} %bitcast.12), channel_id=1, source_target_pairs={{0,16},{16,0},{1,17},{17,1},{2,18},{18,2},{3,19},{19,3},{4,20},{20... | collective-permute-start | bytes 884744 | tf_op jit(solution)/shard_map/ppermute | solution.py:549
  0.5 0.1 collective-permute-start.1
  0.5 3.9 %shard_map.109 = (bf16[4,256,256]{2,1,0:T(8,128)(2,1)S(1)}, f32[4,72,256]{2,1,0:T(8,128)S(1)}, bf16[4,256,256]{2,1,0:T(8,128)(2,1)S(1)}, f32[4,1,256]{2,1,0:T(1,...) custom-call(f32[72,1024]{1,0:T(8,128)} %bitcast.13, s32[4,1024]{1,0:T(4,128)} %bitcast.14, s32[1,1024]{1,0:T(1,128)} %wet_in.1, ...), custom_call_target="tpu_custom_call" | custom-call | flops 1000000000 | bytes 1671168 | tf_op jit(solution)/shard_map/pallas_call | solution.py:503
  4.4 0.0 copy-start
  5.1 0.0 collective-permute-done.1.send_b
  5.1 0.0 collective-permute-done.spectra_b
  5.1 0.0 copy-done.1
  5.1 1.5 %shard_map.110 = (f32[4,72,256]{2,1,0:T(8,128)S(1)}, f32[72,256]{1,0:T(8,128)S(1)}, f32[5,72,256]{2,1,0:T(8,128)S(1)}) custom-call(f32[4,72,256]{2,1,0:T(8,128)S(1)} %get-tuple-element.21.base, bf16[4,256,256]{2,1,0:T(8,128)(2,1)S(1)} %get-tuple-element.22.into, bf16[4,256,256]{2,1,0:T(8,128)(2,1)S(1)} %get-tuple-element.23.order, ...), custom_call_target="tpu_custom_call" | custom-call | flops 1000000000 | bytes 2383428 | tf_op jit(solution)/shard_map/pallas_call | solution.py:503
  6.6 0.5 %collective-permute-start.2 = (f32[72,256]{1,0:T(8,128)S(1)}, f32[72,256]{1,0:T(8,128)S(1)}, u32[]{:S(2)}, u32[]{:S(2)}) collective-permute-start(f32[72,256]{1,0:T(8,128)S(1)} %get-tuple-element.27), channel_id=1, source_target_pairs={{0,16},{16,0},{1,17},{17,1},{2,18},{18,2},{3,19},{19,3},{4,20},{20... | collective-permute-start | bytes 221192 | tf_op jit(solution)/shard_map/ppermute | solution.py:549
  7.1 0.0 copy-done
  7.1 1.0 %shard_map.111 = (f32[4,1,256]{2,1,0:T(1,128)S(1)}, bf16[4,256,512]{2,1,0:T(8,128)(2,1)S(1)}, s32[1,1024]{1,0:T(1,128)S(1)}, f32[8,512]{1,0:T(8,128)S(1)}) custom-call(bf16[4,256,256]{2,1,0:T(8,128)(2,1)S(1)} %get-tuple-element.23.order, f32[4,1,256]{2,1,0:T(1,128)S(1)} %get-tuple-element.24.sea, f32[1,1024]{1,0:T(1,128)S(1)} %copy-done), custom_call_target="tpu_custom_call" | custom-call | flops 1000000000 | bytes 1605632 | tf_op jit(solution)/shard_map/pallas_call | solution.py:503
  8.1 0.0 copy-start.2
  8.1 0.0 copy-start.3
  8.1 0.0 collective-permute-done.2.incoming
  8.1 1.8 %shard_map.112 = f32[288,128]{1,0:T(8,128)} custom-call(f32[4,72,256]{2,1,0:T(8,128)S(1)} %get-tuple-element.26.field_in, f32[72,256]{1,0:T(8,128)S(1)} %collective-permute-done.2.incoming, bf16[4,256,256]{2,1,0:T(8,128)(2,1)S(1)} %get-tuple-element.22.into, bf16[4,256,256]{2,1,0:T(8,128)(2,1)S(1)} %get-tuple-element.23.order, ...), custom_call_target="tpu_custom_call" | custom-call | flops 1000000000 | bytes 2996224 | tf_op jit(solution)/shard_map/pallas_call | solution.py:503
  9.9 8.1 %all-to-all-start = ((f32[16,1,2304]{2,1,0:T(1,128)}), f32[16,1,2304]{2,1,0:T(1,128)S(1)}, u32[]{:S(2)}, u32[]{:S(2)}) async-start(f32[16,1,2304]{2,1,0:T(1,128)} %bitcast.3), calls=%async_computation | async-start | bytes 294912 | tf_op jit(solution)/shard_map/all_to_all | solution.py:545
  18.0 0.0 copy-done.2
  18.1 0.0 copy-done.3
  18.1 3.8 %shard_map.113 = (bf16[1152,1152]{1,0:T(8,128)(2,1)S(1)}, f32[8,1152]{1,0:T(8,128)S(1)}, f32[32,128]{1,0:T(8,128)S(1)}) custom-call(bf16[1152,1152]{1,0:T(8,128)(2,1)} %coupling_in.1, f32[1,1152]{1,0:T(1,128)S(1)} %reshape.24.growth, f32[1,1152]{1,0:T(1,128)S(1)} %reshape.25.dissipation, f32[8,512]{1,0:T(8,128)S(1)} %get-tuple-element.32.blown), custom_call_target="tpu_custom_call" | custom-call | flops 1000000000 | bytes 5387264 | tf_op jit(solution)/shard_map/pallas_call | solution.py:503
  21.9 4.2 %all-to-all-done = f32[16,1,2304]{2,1,0:T(1,128)S(1)} async-done(((f32[16,1,2304]{2,1,0:T(1,128)}), f32[16,1,2304]{2,1,0:T(1,128)S(1)}, u32[]{:S(2)}, u32[]{:S(2)}) %all-to-all-start) | async-done | bytes 147488 | tf_op jit(solution)/shard_map/all_to_all | solution.py:545
  26.1 2.5 %shard_map.114 = f32[288,128]{1,0:T(8,128)S(1)} custom-call(f32[288,128]{1,0:T(8,128)S(1)} %bitcast.10, bf16[1152,1152]{1,0:T(8,128)(2,1)S(1)} %get-tuple-element.33.weights, f32[8,1152]{1,0:T(8,128)S(1)} %get-tuple-element.34.rates, f32[32,128]{1,0:T(8,128)S(1)} %get-tuple-element.35.wind), custom_call_target="tpu_custom_call" | custom-call | flops 1000000000 | bytes 3002368 | tf_op jit(solution)/shard_map/pallas_call | solution.py:503
  28.6 11.0 %all_to_all.10 = f32[16,1,2304]{2,1,0:T(1,128)S(1)} all-to-all(f32[16,1,2304]{2,1,0:T(1,128)S(1)} %bitcast.11), channel_id=1, replica_groups=mesh['nest'=2,'bin'=16] {'bin'}, dimensions={0} | all-to-all | bytes 294912 | tf_op jit(solution)/shard_map/all_to_all | solution.py:545
  39.6 1.3 %shard_map.115 = f32[72,1024]{1,0:T(8,128)} custom-call(f32[288,128]{1,0:T(8,128)S(1)} %bitcast.9, s32[1,1024]{1,0:T(1,128)S(1)} %get-tuple-element.36.place), custom_call_target="tpu_custom_call" | custom-call | flops 100000000 | bytes 446464 | tf_op jit(solution)/shard_map/pallas_call | solution.py:503
  (2 shorter events, 0.0 us)
Async XLA Ops:
  0.0 5.1 %copy-start.1 = (f32[2,72]{1,0:T(2,128)S(1)}, f32[2,72]{1,0:T(2,128)}, u32[]{:S(2)}) copy-start(f32[2,72]{1,0:T(2,128)} %courant.1) | copy-start | bytes 1732
  0.0 5.1 %collective-permute-start = (f32[72,1024]{1,0:T(8,128)}, f32[72,1024]{1,0:T(8,128)S(1)}, u32[]{:S(2)}, u32[]{:S(2)}) collective-permute-start(f32[72,1024]{1,0:T(8,128)} %bitcast.12), channel_id=1, source_target_pairs={{0,16},{16,0},{1,17},{17,1},{2,18},{18,2},{3,19},{19,3},{4,20},{20... | collective-permute-start | bytes 884744 | tf_op jit(solution)/shard_map/ppermute | solution.py:549
  0.5 4.6 %collective-permute-start.1 = (s32[1,256]{1,0:T(1,128)}, s32[1,256]{1,0:T(1,128)S(1)}, u32[]{:S(2)}, u32[]{:S(2)}) collective-permute-start(s32[1,256]{1,0:T(1,128)} %send_in.1), channel_id=1, source_target_pairs={{0,16},{16,0},{1,17},{17,1},{2,18},{18,2},{3,19},{19,3},{4,20},{20... | collective-permute-start | bytes 3080 | tf_op jit(solution)/shard_map/ppermute | solution.py:549
  4.4 2.7 %copy-start = (f32[1,1024]{1,0:T(1,128)S(1)}, f32[1,1024]{1,0:T(1,128)}, u32[]{:S(2)}) copy-start(f32[1,1024]{1,0:T(1,128)} %wind.1) | copy-start | bytes 12292
  6.6 1.5 %collective-permute-start.2 = (f32[72,256]{1,0:T(8,128)S(1)}, f32[72,256]{1,0:T(8,128)S(1)}, u32[]{:S(2)}, u32[]{:S(2)}) collective-permute-start(f32[72,256]{1,0:T(8,128)S(1)} %get-tuple-element.27), channel_id=1, source_target_pairs={{0,16},{16,0},{1,17},{17,1},{2,18},{18,2},{3,19},{19,3},{4,20},{20... | collective-permute-start | bytes 221192 | tf_op jit(solution)/shard_map/ppermute | solution.py:549
  8.1 10.0 %copy-start.2 = (f32[1152]{0:T(1024)S(1)}, f32[1152]{0:T(1024)}, u32[]{:S(2)}) copy-start(f32[1152]{0:T(1024)} %param.14) | copy-start | bytes 13828
  8.1 10.0 %copy-start.3 = (f32[1152]{0:T(1024)S(1)}, f32[1152]{0:T(1024)}, u32[]{:S(2)}) copy-start(f32[1152]{0:T(1024)} %param.15) | copy-start | bytes 13828
  9.9 16.2 %all-to-all-start = ((f32[16,1,2304]{2,1,0:T(1,128)}), f32[16,1,2304]{2,1,0:T(1,128)S(1)}, u32[]{:S(2)}, u32[]{:S(2)}) async-start(f32[16,1,2304]{2,1,0:T(1,128)} %bitcast.3), calls=%async_computation | async-start | bytes 294912 | tf_op jit(solution)/shard_map/all_to_all | solution.py:545

commit v4 on v3

--- a/solution.py
+++ b/solution.py
@@ -85,25 +85,85 @@
     return pl.ds(start * size, size)
 
 
-def walk(tables, order):
-    rows_count, cols_count, _ = order.shape
-    step = one_hot(cols_count, tables[0:1, 0:cols_count])
-    across = lax.broadcasted_iota(jnp.int32, (cols_count, cols_count), 1)
-    at = lax.broadcasted_iota(jnp.int32, (cols_count, cols_count), 0)
-    found = jnp.where(at == 0, 1.0, 0.0)
+def rows_stacked(tiles):
+    at = lax.broadcasted_iota(jnp.int32, (SUBLANES, LANES), 0)
+    stacked = eight(tiles[0])
+    for k in range(1, len(tiles)):
+        stacked = jnp.where(at == k, eight(tiles[k]), stacked)
+    return stacked
+
+
+def tiles_of(row):
+    return [row[:, k * LANES : (k + 1) * LANES] for k in range(row.shape[1] // LANES)]
+
+
+def taken_from(tables, index):
+    lane, tile = index & (LANES - 1), index >> (LANES - 1).bit_length()
+    found = None
+    for k, table in enumerate(tables):
+        here = jnp.take_along_axis(eight(table), lane, axis=1, mode="promise_in_bounds")
+        found = here if k == 0 else jnp.where(tile == k, here, found)
+    return found
+
+
+def look_up(table, index):
+    count = index.shape[1] // LANES
+    found = taken_from(tiles_of(table), rows_stacked(tiles_of(index)))
+    return jnp.concatenate([found[k : k + 1] for k in range(count)], axis=1)
+
+
+def walk(tables, order, rank):
+    rows_count, _, cols_count = order.shape
+    count = cols_count // LANES
     bits = (cols_count - 1).bit_length()
+    at = lax.broadcasted_iota(jnp.int32, (SUBLANES, LANES), 0)
+    place = (at % count) * LANES + lax.broadcasted_iota(jnp.int32, (SUBLANES, LANES), 1)
+
+    first = tables[0:1, 0:cols_count]
+    ahead = jnp.where(at < count, rows_stacked(tiles_of(first)), 0)
+    behind = rows_stacked(tiles_of(tables[1:2, 0:cols_count]))
+    behind = jnp.where(place == 0, 0, behind)
+    steps = jnp.where(place == 0, 0, 1)
     for bit in range(bits):
-        moved = dot(step, found.astype(bf16))
-        found = jnp.where((across >> bit) & 1 == 1, moved, found)
-        if bit < bits - 1:
-            step = dot(step, step).astype(bf16)
-    order[0] = found.astype(bf16)
+        far = taken_from([ahead[k : k + 1] for k in range(count)], ahead)
+        both = (steps << bits) + behind
+        back = taken_from([both[k : k + 1] for k in range(count)], behind)
+        ahead = jnp.where((at >= count) & ((place >> bit) & 1 == 0), ahead, far)
+        steps = steps + (back >> bits)
+        behind = back & ((1 << bits) - 1)
+    order[0] = jnp.concatenate([ahead[count + k : count + k + 1] for k in range(count)], axis=1)
+    rank[0] = jnp.concatenate([steps[k : k + 1] for k in range(count)], axis=1)
 
     def next_row(row):
         north = tables[2:3, span(row, cols_count)] - (row + 1) * cols_count
-        order[row + 1] = dot(one_hot(cols_count, north), order[row]).astype(bf16)
+        south = tables[3:4, span(row + 1, cols_count)] - row * cols_count
+        order[row + 1] = look_up(north, order[row])
+        rank[row + 1] = look_up(rank[row], south)
 
     each(rows_count - 1, next_row)
+
+
+def grid_places(listed, rank):
+    rows_count, _, cols_count = rank.shape
+    tiles = tiles_of(listed)
+    found = []
+    for tile in tiles:
+        index = eight(tile)
+
+        def column_in(row, best):
+            first = row * cols_count
+            within = jnp.clip(index - first, 0, cols_count - 1)
+            here = taken_from(tiles_of(rank[row]), within)
+            return jnp.where(index - first == within, here + first, best)
+
+        best = jnp.zeros((SUBLANES, LANES), jnp.int32)
+        if rows_count <= 16:
+            for row in range(rows_count):
+                best = column_in(row, best)
+        else:
+            best = lax.fori_loop(0, rows_count, column_in, best)
+        found.append(best[0:1])
+    return jnp.concatenate(found, axis=1)
 
 
 def down(row):
@@ -161,12 +221,10 @@
     each(rows_count, north)
 
 
-def landing(row, into, order, lists):
-    if into.shape[0] == order.shape[0]:
+def landing(row, into, lists, cols_count):
+    if into.shape[0] > 1:
         return into[row]
-    cols_count = order.shape[2]
-    here = one_hot_across(down(lists[1:2]), row * cols_count, cols_count)
-    return dot(here, order[row]).astype(bf16)
+    return one_hot_across(down(lists[1:2]), row * cols_count, cols_count)
 
 
 def prepare_kernel(
@@ -176,6 +234,7 @@
     send_in,
     recv_in,
     order,
+    rank,
     base,
     into,
     sea,
@@ -184,6 +243,8 @@
     spectra,
     tables,
     wet,
+    send,
+    recv,
     arrived,
 ):
     copies = [
@@ -191,8 +252,8 @@
         for which, (source, target) in enumerate(
             (
                 (tables_in, tables),
-                (send_in, lists.at[0:1]),
-                (recv_in, lists.at[1:2]),
+                (send_in, send),
+                (recv_in, recv),
                 (wet_in, wet),
                 (spectra_in, spectra),
             )
@@ -201,24 +262,26 @@
     for copy in copies:
         copy.start()
     rows_count, bins, cols_count = base.shape
-    listed = lists.shape[1]
-    copies[0].wait()
-    walk(tables, order)
-    for copy in copies[1:]:
+    listed = send.shape[1]
+    for copy in copies[:-1]:
         copy.wait()
+    walk(tables, order, rank)
+    lists[0:1] = grid_places(send[...], rank)
+    lists[1:2] = grid_places(recv[...], rank)
     recv_down = down(lists[1:2])
+    copies[-1].wait()
 
     def place(row):
-        own = order[row]
+        own = one_hot(cols_count, order[row])
         here = one_hot_across(recv_down, row * cols_count, cols_count)
-        if into.shape[0] == rows_count:
-            into[row] = dot(here, own).astype(bf16)
+        if into.shape[0] > 1:
+            into[row] = here
         got = dot(jnp.ones((SUBLANES, listed), bf16), here)[0:1]
-        taken[row] = dot(eight(got).astype(bf16), own)[0:1]
-        covered = wet[0:1, span(row, cols_count)].astype(f32)
-        sea[row] = dot(eight(covered).astype(bf16), own)[0:1]
-        values = spectra[:, span(row, cols_count)] * (covered * (1.0 - got))
-        base[row] = joined(dot(split(values), own))
+        taken[row] = got
+        covered = look_up(wet[0:1, span(row, cols_count)], order[row]).astype(f32)
+        sea[row] = covered
+        values = joined(dot(split(spectra[:, span(row, cols_count)]), own))
+        base[row] = values * (covered * (1.0 - got))
 
     each(rows_count, place)
 
@@ -226,7 +289,6 @@
 def first_kernel(
     base,
     into,
-    order,
     sea,
     lists,
     spectra_b,
@@ -255,14 +317,13 @@
     incoming = total_of(rows_count, (2 * bins, listed), sent).astype(bf16)
 
     def take(row):
-        field[row] = base[row] + joined(dot(incoming, landing(row, into, order, lists)))
+        field[row] = base[row] + joined(dot(incoming, landing(row, into, lists, cols_count)))
 
     each(rows_count, take)
     advance(field, moved, faces, sea, rates[0], rates[1])
 
     def sending(row):
-        plain = dot_t(split(field[row]), order[row]).astype(bf16)
-        return dot(plain, one_hot(cols_count, lists[0:1] - row * cols_count))
+        return dot(split(field[row]), one_hot(cols_count, lists[0:1] - row * cols_count))
 
     outgoing[...] = joined(total_of(rows_count, (2 * bins, listed), sending))
 
@@ -273,8 +334,8 @@
     return one_hot_across(down(ranks[row] - 1.0), 0, sea_count)
 
 
-def places_kernel(order, sea, wind, ranks, picks, place, blown):
-    rows_count, cols_count, _ = order.shape
+def places_kernel(order, rank, sea, wind, ranks, picks, place, blown):
+    rows_count, _, cols_count = order.shape
     sea_count = blown.shape[1]
     at = lax.broadcasted_iota(jnp.int32, (cols_count, cols_count), 0)
     across = lax.broadcasted_iota(jnp.int32, (cols_count, cols_count), 1)
@@ -282,16 +343,12 @@
 
     def number(row, before):
         here = sea[row]
-        rank = dot(eight(here).astype(bf16), upper)[0:1] + before
-        rank = jnp.where(here > 0.0, rank, 0.0)
-        ranks[row] = rank
+        number_of = dot(eight(here).astype(bf16), upper)[0:1] + before
+        number_of = jnp.where(here > 0.0, number_of, 0.0)
+        ranks[row] = number_of
         if picks.shape[0] == rows_count:
-            picks[row] = one_hot_across(down(rank - 1.0), 0, sea_count)
-        high = jnp.floor(rank * (1.0 / cols_count))
-        digits = jnp.concatenate([eight(high), eight(rank - high * cols_count)], axis=0)
-        plain = dot_t(digits.astype(bf16), order[row])
-        plain = plain[0:1] * cols_count + plain[SUBLANES : SUBLANES + 1]
-        place[0:1, span(row, cols_count)] = plain.astype(jnp.int32)
+            picks[row] = one_hot_across(down(number_of - 1.0), 0, sea_count)
+        place[0:1, span(row, cols_count)] = look_up(number_of.astype(jnp.int32), rank[row])
         return before + jnp.sum(here, axis=1, keepdims=True)
 
     before = jnp.zeros((1, 1), f32)
@@ -302,9 +359,8 @@
         lax.fori_loop(0, rows_count, number, before)
 
     def there(row):
-        terms = split(eight(wind[0:1, span(row, cols_count)]))
-        by_grid = dot(terms, order[row]).astype(bf16)
-        return dot(by_grid, picked(row, ranks, picks, sea_count))
+        by_grid = look_up(wind[0:1, span(row, cols_count)], order[row])
+        return dot(split(eight(by_grid)), picked(row, ranks, picks, sea_count))
 
     blown[...] = joined(total_of(rows_count, (2 * SUBLANES, sea_count), there))
 
@@ -314,7 +370,6 @@
     field_in,
     incoming,
     into,
-    order,
     lists,
     taken,
     sea,
@@ -333,7 +388,7 @@
     terms = split(incoming[...])
 
     def take(row):
-        got = joined(dot(terms, landing(row, into, order, lists)))
+        got = joined(dot(terms, landing(row, into, lists, cols_count)))
         field[row] = jnp.where(taken[row] * rates[4, 0:1] > 0.5, got, field_in[row])
 
     each(rows_count, take)
@@ -550,7 +605,6 @@
 
     spectra_b, send_b = swap(field), swap(send_list)
     grid = (rows_count, bins, cols_count)
-    by_point = (rows_count, cols_count, cols_count)
     row_of = (rows_count, 1, cols_count)
     early = (
         field,
@@ -560,10 +614,11 @@
         recv_list,
     )
     kept_into = rows_count if points * listed <= 1 << 22 else 1
-    order, base, into, sea, taken, lists = call(
+    order, rank, base, into, sea, taken, lists = call(
         prepare_kernel,
         [
-            (by_point, bf16),
+            (row_of, jnp.int32),
+            (row_of, jnp.int32),
             (grid, f32),
             ((kept_into, listed, cols_count), bf16),
             (row_of, f32),
@@ -571,7 +626,7 @@
             ((2, listed), jnp.int32),
         ],
         [
-            *(pltpu.VMEM(x.shape, x.dtype) for x in early[:3]),
+            *(pltpu.VMEM(x.shape, x.dtype) for x in early),
             pltpu.SemaphoreType.DMA((5,)),
         ],
         early,
@@ -582,7 +637,7 @@
         first_kernel,
         [(grid, f32), ((bins, listed), f32), ((5, bins, cols_count), f32)],
         [pltpu.VMEM(grid, f32)] * 2,
-        (base, into, order, sea, lists, spectra_b, send_b, courant, substep_count.reshape(1, 1)),
+        (base, into, sea, lists, spectra_b, send_b, courant, substep_count.reshape(1, 1)),
         10**9,
     )
     incoming = swap(outgoing)
@@ -596,7 +651,7 @@
             ((SUBLANES, sea_count), f32),
         ],
         [],
-        (order, sea, wind),
+        (order, rank, sea, wind),
         10**9,
     )
     tiles = sea_count // LANES
@@ -604,7 +659,7 @@
         functools.partial(second_kernel, share),
         ((devices * block, LANES), f32),
         [*[pltpu.VMEM(grid, f32)] * 3, pltpu.VMEM((tiles, bins, LANES), f32)],
-        (field, incoming, into, order, lists, taken, sea, rates, ranks, picks),
+        (field, incoming, into, lists, taken, sea, rates, ranks, picks),
         10**9,
     )
     pieces = transpose_all(pieces)

time: 41.2 us -> 39.3 us (0.954)
  Pallas kernels: 15.7 us -> 13.6 us
    pallas_call x7, Pallas kernels: 15.7 us -> 13.6 us  [call(): pl.pallas_call(kernel, out_shape=shapes[0] if single else shapes, in_spec...]
  transfers between devices with their start and end apart: 4 -> 4, of which waited for: 1 -> 2; matrix products, arithmetic and copies ran while one was open for 0% -> 0% of each run, Pallas kernels for 21% -> 17%
where the time goes in v4:
time: 39.3 us; the launch traced here: 39 us
  Pallas kernels  13.6 us (35%)
  blocking collectives  11 us (28%)
  starting transfers between devices  9.24 us (24%)
  waiting for transfers between devices  4.34 us (11%)
  between operations  0.77 us (2%)
    pallas_call x7, Pallas kernels, call(): pl.pallas_call(kernel, out_shape=shapes[0] if single else shapes, in_spec...  13.6 us
    all_to_all x1, blocking collectives, transpose_all(): pieces = lax.all_to_all(pieces, 'bin', split_axis=0, concat_axis=0)  11 us
    all_to_all x1, starting transfers between devices, transpose_all(): pieces = lax.all_to_all(pieces, 'bin', split_axis=0, concat_axis=0)  8.22 us
    all_to_all x1, waiting for transfers between devices, transpose_all(): pieces = lax.all_to_all(pieces, 'bin', split_axis=0, concat_axis=0)  4.11 us
    ppermute x3, starting transfers between devices, swap(): return lax.ppermute(array, 'nest', [(0, 1), (1, 0)])  1.03 us
  transfers between devices with their start and end apart: 4, of which 2 were waited for; matrix products, arithmetic and copies ran while one was open for 0% of the time, Pallas kernels for 17%

profile of v4, /device:TPU:0, one launch (start us, length us, event | category | flops | bytes accessed | tf_op | source)
XLA Modules:
  0.0 39.0 jit_solution(7292608056257002995)
XLA Ops:
  0.0 0.0 copy-start.1
  0.0 0.5 %collective-permute-start = (f32[72,1024]{1,0:T(8,128)}, f32[72,1024]{1,0:T(8,128)S(1)}, u32[]{:S(2)}, u32[]{:S(2)}) collective-permute-start(f32[72,1024]{1,0:T(8,128)} %bitcast.12), channel_id=1, source_target_pairs={{0,16},{16,0},{1,17},{17,1},{2,18},{18,2},{3,19},{19,3},{4,20},{20... | collective-permute-start | bytes 884744 | tf_op jit(solution)/shard_map/ppermute | solution.py:604
  0.5 0.1 collective-permute-start.1
  0.5 2.4 %shard_map.109 = (s32[4,1,256]{2,1,0:T(1,128)S(1)}, s32[4,1,256]{2,1,0:T(1,128)S(1)}, f32[4,72,256]{2,1,0:T(8,128)S(1)}, bf16[4,256,256]{2,1,0:T(8,128)(2,1)S(1)...) custom-call(f32[72,1024]{1,0:T(8,128)} %bitcast.13, s32[4,1024]{1,0:T(4,128)} %bitcast.14, ...), custom_call_target="tpu_custom_call" | custom-call | flops 1000000000 | bytes 1155072 | tf_op jit(solution)/shard_map/pallas_call | solution.py:558
  2.9 0.0 copy-start
  3.6 0.0 collective-permute-done.1.send_b
  3.6 0.0 collective-permute-done.spectra_b
  3.6 0.0 copy-done.1
  3.6 1.2 %shard_map.110 = (f32[4,72,256]{2,1,0:T(8,128)S(1)}, f32[72,256]{1,0:T(8,128)S(1)}, f32[5,72,256]{2,1,0:T(8,128)S(1)}) custom-call(f32[4,72,256]{2,1,0:T(8,128)S(1)} %get-tuple-element.22.base, bf16[4,256,256]{2,1,0:T(8,128)(2,1)S(1)} %get-tuple-element.23.into, f32[4,1,256]{2,1,0:T(1,128)S(1)} %get-tuple-element.24.sea, ...), custom_call_target="tpu_custom_call" | custom-call | flops 1000000000 | bytes 1859140 | tf_op jit(solution)/shard_map/pallas_call | solution.py:558
  4.8 0.5 %collective-permute-start.2 = (f32[72,256]{1,0:T(8,128)S(1)}, f32[72,256]{1,0:T(8,128)S(1)}, u32[]{:S(2)}, u32[]{:S(2)}) collective-permute-start(f32[72,256]{1,0:T(8,128)S(1)} %get-tuple-element.27), channel_id=1, source_target_pairs={{0,16},{16,0},{1,17},{17,1},{2,18},{18,2},{3,19},{19,3},{4,20},{20... | collective-permute-start | bytes 221192 | tf_op jit(solution)/shard_map/ppermute | solution.py:604
  5.3 0.0 copy-done
  5.3 0.7 %shard_map.111 = (f32[4,1,256]{2,1,0:T(1,128)S(1)}, bf16[4,256,512]{2,1,0:T(8,128)(2,1)S(1)}, s32[1,1024]{1,0:T(1,128)S(1)}, f32[8,512]{1,0:T(8,128)S(1)}) custom-call(s32[4,1,256]{2,1,0:T(1,128)S(1)} %get-tuple-element.30.order, s32[4,1,256]{2,1,0:T(1,128)S(1)} %get-tuple-element.31.rank, f32[4,1,256]{2,1,0:T(1,128)S(1)} %get-tuple-element.24.sea, ...), custom_call_target="tpu_custom_call" | custom-call | flops 1000000000 | bytes 1089536 | tf_op jit(solution)/shard_map/pallas_call | solution.py:558
  6.0 0.0 copy-start.2
  6.0 0.0 copy-start.3
  6.0 0.2 collective-permute-done.2.incoming
  6.2 1.8 %shard_map.112 = f32[288,128]{1,0:T(8,128)} custom-call(f32[4,72,256]{2,1,0:T(8,128)S(1)} %get-tuple-element.26.field_in, f32[72,256]{1,0:T(8,128)S(1)} %collective-permute-done.2.incoming, bf16[4,256,256]{2,1,0:T(8,128)(2,1)S(1)} %get-tuple-element.23.into, s32[2,256]{1,0:T(2,128)S(1)} %get-tuple-element.25.lists, ...), custom_call_target="tpu_custom_call" | custom-call | flops 1000000000 | bytes 2471936 | tf_op jit(solution)/shard_map/pallas_call | solution.py:558
  8.1 8.2 %all-to-all-start = ((f32[16,1,2304]{2,1,0:T(1,128)}), f32[16,1,2304]{2,1,0:T(1,128)S(1)}, u32[]{:S(2)}, u32[]{:S(2)}) async-start(f32[16,1,2304]{2,1,0:T(1,128)} %bitcast.3), calls=%async_computation | async-start | bytes 294912 | tf_op jit(solution)/shard_map/all_to_all | solution.py:600
  16.3 0.0 copy-done.2
  16.3 0.0 copy-done.3
  16.3 3.8 %shard_map.113 = (bf16[1152,1152]{1,0:T(8,128)(2,1)S(1)}, f32[8,1152]{1,0:T(8,128)S(1)}, f32[32,128]{1,0:T(8,128)S(1)}) custom-call(bf16[1152,1152]{1,0:T(8,128)(2,1)} %coupling_in.1, f32[1,1152]{1,0:T(1,128)S(1)} %reshape.24.growth, f32[1,1152]{1,0:T(1,128)S(1)} %reshape.25.dissipation, f32[8,512]{1,0:T(8,128)S(1)} %get-tuple-element.34.blown), custom_call_target="tpu_custom_call" | custom-call | flops 1000000000 | bytes 5387264 | tf_op jit(solution)/shard_map/pallas_call | solution.py:558
  20.1 4.1 %all-to-all-done = f32[16,1,2304]{2,1,0:T(1,128)S(1)} async-done(((f32[16,1,2304]{2,1,0:T(1,128)}), f32[16,1,2304]{2,1,0:T(1,128)S(1)}, u32[]{:S(2)}, u32[]{:S(2)}) %all-to-all-start) | async-done | bytes 147488 | tf_op jit(solution)/shard_map/all_to_all | solution.py:600
  24.2 2.5 %shard_map.114 = f32[288,128]{1,0:T(8,128)S(1)} custom-call(f32[288,128]{1,0:T(8,128)S(1)} %bitcast.10, bf16[1152,1152]{1,0:T(8,128)(2,1)S(1)} %get-tuple-element.35.weights, f32[8,1152]{1,0:T(8,128)S(1)} %get-tuple-element.36.rates, f32[32,128]{1,0:T(8,128)S(1)} %get-tuple-element.37.wind), custom_call_target="tpu_custom_call" | custom-call | flops 1000000000 | bytes 3002368 | tf_op jit(solution)/shard_map/pallas_call | solution.py:558
  26.7 11.0 %all_to_all.10 = f32[16,1,2304]{2,1,0:T(1,128)S(1)} all-to-all(f32[16,1,2304]{2,1,0:T(1,128)S(1)} %bitcast.11), channel_id=1, replica_groups=mesh['nest'=2,'bin'=16] {'bin'}, dimensions={0} | all-to-all | bytes 294912 | tf_op jit(solution)/shard_map/all_to_all | solution.py:600
  37.7 1.3 %shard_map.115 = f32[72,1024]{1,0:T(8,128)} custom-call(f32[288,128]{1,0:T(8,128)S(1)} %bitcast.9, s32[1,1024]{1,0:T(1,128)S(1)} %get-tuple-element.38.place), custom_call_target="tpu_custom_call" | custom-call | flops 100000000 | bytes 446464 | tf_op jit(solution)/shard_map/pallas_call | solution.py:558
  (2 shorter events, 0.0 us)
Async XLA Ops:
  0.0 3.6 %copy-start.1 = (f32[2,72]{1,0:T(2,128)S(1)}, f32[2,72]{1,0:T(2,128)}, u32[]{:S(2)}) copy-start(f32[2,72]{1,0:T(2,128)} %courant.1) | copy-start | bytes 1732
  0.0 3.6 %collective-permute-start = (f32[72,1024]{1,0:T(8,128)}, f32[72,1024]{1,0:T(8,128)S(1)}, u32[]{:S(2)}, u32[]{:S(2)}) collective-permute-start(f32[72,1024]{1,0:T(8,128)} %bitcast.12), channel_id=1, source_target_pairs={{0,16},{16,0},{1,17},{17,1},{2,18},{18,2},{3,19},{19,3},{4,20},{20... | collective-permute-start | bytes 884744 | tf_op jit(solution)/shard_map/ppermute | solution.py:604
  0.5 3.1 %collective-permute-start.1 = (s32[1,256]{1,0:T(1,128)}, s32[1,256]{1,0:T(1,128)S(1)}, u32[]{:S(2)}, u32[]{:S(2)}) collective-permute-start(s32[1,256]{1,0:T(1,128)} %send_in.1), channel_id=1, source_target_pairs={{0,16},{16,0},{1,17},{17,1},{2,18},{18,2},{3,19},{19,3},{4,20},{20... | collective-permute-start | bytes 3080 | tf_op jit(solution)/shard_map/ppermute | solution.py:604
  2.9 2.4 %copy-start = (f32[1,1024]{1,0:T(1,128)S(1)}, f32[1,1024]{1,0:T(1,128)}, u32[]{:S(2)}) copy-start(f32[1,1024]{1,0:T(1,128)} %wind.1) | copy-start | bytes 12292
  4.8 1.4 %collective-permute-start.2 = (f32[72,256]{1,0:T(8,128)S(1)}, f32[72,256]{1,0:T(8,128)S(1)}, u32[]{:S(2)}, u32[]{:S(2)}) collective-permute-start(f32[72,256]{1,0:T(8,128)S(1)} %get-tuple-element.27), channel_id=1, source_target_pairs={{0,16},{16,0},{1,17},{17,1},{2,18},{18,2},{3,19},{19,3},{4,20},{20... | collective-permute-start | bytes 221192 | tf_op jit(solution)/shard_map/ppermute | solution.py:604
  6.0 10.3 %copy-start.2 = (f32[1152]{0:T(1024)S(1)}, f32[1152]{0:T(1024)}, u32[]{:S(2)}) copy-start(f32[1152]{0:T(1024)} %param.14) | copy-start | bytes 13828
  6.0 10.3 %copy-start.3 = (f32[1152]{0:T(1024)S(1)}, f32[1152]{0:T(1024)}, u32[]{:S(2)}) copy-start(f32[1152]{0:T(1024)} %param.15) | copy-start | bytes 13828
  8.1 16.2 %all-to-all-start = ((f32[16,1,2304]{2,1,0:T(1,128)}), f32[16,1,2304]{2,1,0:T(1,128)S(1)}, u32[]{:S(2)}, u32[]{:S(2)}) async-start(f32[16,1,2304]{2,1,0:T(1,128)} %bitcast.3), calls=%async_computation | async-start | bytes 294912 | tf_op jit(solution)/shard_map/all_to_all | solution.py:600

commit v5 on v4

--- a/solution.py
+++ b/solution.py
@@ -227,12 +227,16 @@
     return one_hot_across(down(lists[1:2]), row * cols_count, cols_count)
 
 
+def count_kernel(steps_in, steps):
+    steps[...] = jnp.broadcast_to(steps_in[...].astype(f32), steps.shape)
+
+
 def prepare_kernel(
-    spectra_in,
-    tables_in,
-    wet_in,
-    send_in,
-    recv_in,
+    spectra,
+    tables,
+    wet,
+    send,
+    recv,
     order,
     rank,
     base,
@@ -240,36 +244,13 @@
     sea,
     taken,
     lists,
-    spectra,
-    tables,
-    wet,
-    send,
-    recv,
-    arrived,
 ):
-    copies = [
-        pltpu.make_async_copy(source, target, arrived.at[which])
-        for which, (source, target) in enumerate(
-            (
-                (tables_in, tables),
-                (send_in, send),
-                (recv_in, recv),
-                (wet_in, wet),
-                (spectra_in, spectra),
-            )
-        )
-    ]
-    for copy in copies:
-        copy.start()
     rows_count, bins, cols_count = base.shape
     listed = send.shape[1]
-    for copy in copies[:-1]:
-        copy.wait()
     walk(tables, order, rank)
     lists[0:1] = grid_places(send[...], rank)
     lists[1:2] = grid_places(recv[...], rank)
     recv_down = down(lists[1:2])
-    copies[-1].wait()
 
     def place(row):
         own = one_hot(cols_count, order[row])
@@ -303,9 +284,9 @@
 ):
     rows_count, bins, cols_count = base.shape
     listed = lists.shape[1]
-    second = jnp.where(steps[...] > 1, 1.0, 0.0)
+    second = jnp.where(steps[0:1] > 1.0, 1.0, 0.0)
     for which in range(2):
-        rate = column(courant[which : which + 1, :]) / steps[...].astype(f32)
+        rate = column(courant[which : which + 1, :]) / steps[0:1]
         rates[which] = jnp.broadcast_to(rate, (bins, cols_count))
         rates[2 + which] = jnp.broadcast_to(rate * second, (bins, cols_count))
     rates[4] = jnp.broadcast_to(second, (bins, cols_count))
@@ -606,6 +587,9 @@
     spectra_b, send_b = swap(field), swap(send_list)
     grid = (rows_count, bins, cols_count)
     row_of = (rows_count, 1, cols_count)
+    steps = call(
+        count_kernel, ((SUBLANES, cols_count), f32), [], (substep_count.reshape(1, 1),), 10**9
+    )
     early = (
         field,
         neighbours[0],
@@ -625,19 +609,15 @@
             (row_of, f32),
             ((2, listed), jnp.int32),
         ],
-        [
-            *(pltpu.VMEM(x.shape, x.dtype) for x in early),
-            pltpu.SemaphoreType.DMA((5,)),
-        ],
+        [],
         early,
         10**9,
-        range(5),
     )
     field, outgoing, rates = call(
         first_kernel,
         [(grid, f32), ((bins, listed), f32), ((5, bins, cols_count), f32)],
         [pltpu.VMEM(grid, f32)] * 2,
-        (base, into, sea, lists, spectra_b, send_b, courant, substep_count.reshape(1, 1)),
+        (base, into, sea, lists, spectra_b, send_b, courant, steps),
         10**9,
     )
     incoming = swap(outgoing)

time: 39.3 us -> 38.7 us (0.985)
  Pallas kernels: 13.6 us -> 12.9 us
    pallas_call x7 -> x8, Pallas kernels: 13.6 us -> 12.9 us  [call(): pl.pallas_call(kernel, out_shape=shapes[0] if single else shapes, in_spec...]
  transfers between devices with their start and end apart: 4 -> 4, of which waited for: 2 -> 2; matrix products, arithmetic and copies ran while one was open for 0% -> 0% of each run, Pallas kernels for 17% -> 16%
where the time goes in v5:
time: 38.7 us; the launch traced here: 38.4 us
  Pallas kernels  12.9 us (33%)
  blocking collectives  11 us (28%)
  starting transfers between devices  9.32 us (24%)
  waiting for transfers between devices  4.34 us (11%)
  between operations  0.79 us (2%)
    pallas_call x8, Pallas kernels, call(): pl.pallas_call(kernel, out_shape=shapes[0] if single else shapes, in_spec...  12.9 us
    all_to_all x1, blocking collectives, transpose_all(): pieces = lax.all_to_all(pieces, 'bin', split_axis=0, concat_axis=0)  11 us
    all_to_all x1, starting transfers between devices, transpose_all(): pieces = lax.all_to_all(pieces, 'bin', split_axis=0, concat_axis=0)  8.21 us
    all_to_all x1, waiting for transfers between devices, transpose_all(): pieces = lax.all_to_all(pieces, 'bin', split_axis=0, concat_axis=0)  4.11 us
    ppermute x3, starting transfers between devices, swap(): return lax.ppermute(array, 'nest', [(0, 1), (1, 0)])  1.11 us
  transfers between devices with their start and end apart: 4, of which 2 were waited for; matrix products, arithmetic and copies ran while one was open for 0% of the time, Pallas kernels for 16%

profile of v5, /device:TPU:0, one launch (start us, length us, event | category | flops | bytes accessed | tf_op | source)
XLA Modules:
  0.0 38.4 jit_solution(16809112456589127241)
XLA Ops:
  0.0 0.0 copy-start
  0.0 0.0 copy-start.5
  0.0 0.0 copy-start.4
  0.0 0.0 copy-start.2
  0.0 0.0 copy-start.1
  0.0 0.5 %collective-permute-start = (f32[72,1024]{1,0:T(8,128)}, f32[72,1024]{1,0:T(8,128)S(1)}, u32[]{:S(2)}, u32[]{:S(2)}) collective-permute-start(f32[72,1024]{1,0:T(8,128)} %bitcast.12), channel_id=1, source_target_pairs={{0,16},{16,0},{1,17},{17,1},{2,18},{18,2},{3,19},{19,3},{4,20},{20... | collective-permute-start | bytes 884744 | tf_op jit(solution)/shard_map/ppermute | solution.py:585
  0.5 0.1 collective-permute-start.1
  1.3 0.1 shard_map.110.steps
  1.4 0.0 copy-start.6
  1.4 0.0 copy-done
  1.4 0.0 copy-done.5
  1.4 0.0 copy-done.4
  1.4 0.0 copy-done.2
  1.4 0.0 copy-done.1
  1.4 1.5 %shard_map.109 = (s32[4,1,256]{2,1,0:T(1,128)S(1)}, s32[4,1,256]{2,1,0:T(1,128)S(1)}, f32[4,72,256]{2,1,0:T(8,128)S(1)}, bf16[4,256,256]{2,1,0:T(8,128)(2,1)S(1)...) custom-call(f32[72,1024]{1,0:T(8,128)S(1)} %bitcast.13, s32[4,1024]{1,0:T(4,128)S(1)} %bitcast.14, ...), custom_call_target="tpu_custom_call" | custom-call | flops 1000000000 | bytes 1155072 | tf_op jit(solution)/shard_map/pallas_call | solution.py:539
  2.9 0.0 copy-start.3
  2.9 0.0 collective-permute-done.1.send_b
  3.0 0.0 collective-permute-done.spectra_b
  3.0 0.0 copy-done.6
  3.0 1.2 %shard_map.111 = (f32[4,72,256]{2,1,0:T(8,128)S(1)}, f32[72,256]{1,0:T(8,128)S(1)}, f32[5,72,256]{2,1,0:T(8,128)S(1)}) custom-call(f32[4,72,256]{2,1,0:T(8,128)S(1)} %get-tuple-element.22.base, bf16[4,256,256]{2,1,0:T(8,128)(2,1)S(1)} %get-tuple-element.23.into, f32[4,1,256]{2,1,0:T(1,128)S(1)} %get-tuple-element.24.sea, ...), custom_call_target="tpu_custom_call" | custom-call | flops 1000000000 | bytes 1867328 | tf_op jit(solution)/shard_map/pallas_call | solution.py:539
  4.2 0.5 %collective-permute-start.2 = (f32[72,256]{1,0:T(8,128)S(1)}, f32[72,256]{1,0:T(8,128)S(1)}, u32[]{:S(2)}, u32[]{:S(2)}) collective-permute-start(f32[72,256]{1,0:T(8,128)S(1)} %get-tuple-element.27), channel_id=1, source_target_pairs={{0,16},{16,0},{1,17},{17,1},{2,18},{18,2},{3,19},{19,3},{4,20},{20... | collective-permute-start | bytes 221192 | tf_op jit(solution)/shard_map/ppermute | solution.py:585
  4.7 0.0 copy-done.3
  4.7 0.7 %shard_map.112 = (f32[4,1,256]{2,1,0:T(1,128)S(1)}, bf16[4,256,512]{2,1,0:T(8,128)(2,1)S(1)}, s32[1,1024]{1,0:T(1,128)S(1)}, f32[8,512]{1,0:T(8,128)S(1)}) custom-call(s32[4,1,256]{2,1,0:T(1,128)S(1)} %get-tuple-element.30.order, s32[4,1,256]{2,1,0:T(1,128)S(1)} %get-tuple-element.31.rank, f32[4,1,256]{2,1,0:T(1,128)S(1)} %get-tuple-element.24.sea, ...), custom_call_target="tpu_custom_call" | custom-call | flops 1000000000 | bytes 1089536 | tf_op jit(solution)/shard_map/pallas_call | solution.py:539
  5.4 0.0 copy-start.7
  5.4 0.0 copy-start.8
  5.4 0.2 collective-permute-done.2.incoming
  5.6 1.8 %shard_map.113 = f32[288,128]{1,0:T(8,128)} custom-call(f32[4,72,256]{2,1,0:T(8,128)S(1)} %get-tuple-element.26.field_in, f32[72,256]{1,0:T(8,128)S(1)} %collective-permute-done.2.incoming, bf16[4,256,256]{2,1,0:T(8,128)(2,1)S(1)} %get-tuple-element.23.into, s32[2,256]{1,0:T(2,128)S(1)} %get-tuple-element.25.lists, ...), custom_call_target="tpu_custom_call" | custom-call | flops 1000000000 | bytes 2471936 | tf_op jit(solution)/shard_map/pallas_call | solution.py:539
  7.5 8.2 %all-to-all-start = ((f32[16,1,2304]{2,1,0:T(1,128)}), f32[16,1,2304]{2,1,0:T(1,128)S(1)}, u32[]{:S(2)}, u32[]{:S(2)}) async-start(f32[16,1,2304]{2,1,0:T(1,128)} %bitcast.3), calls=%async_computation | async-start | bytes 294912 | tf_op jit(solution)/shard_map/all_to_all | solution.py:581
  15.7 0.0 copy-done.7
  15.7 0.0 copy-done.8
  15.7 3.8 %shard_map.114 = (bf16[1152,1152]{1,0:T(8,128)(2,1)S(1)}, f32[8,1152]{1,0:T(8,128)S(1)}, f32[32,128]{1,0:T(8,128)S(1)}) custom-call(bf16[1152,1152]{1,0:T(8,128)(2,1)} %coupling_in.1, f32[1,1152]{1,0:T(1,128)S(1)} %reshape.24.growth, f32[1,1152]{1,0:T(1,128)S(1)} %reshape.25.dissipation, f32[8,512]{1,0:T(8,128)S(1)} %get-tuple-element.34.blown), custom_call_target="tpu_custom_call" | custom-call | flops 1000000000 | bytes 5387264 | tf_op jit(solution)/shard_map/pallas_call | solution.py:539
  19.5 4.1 %all-to-all-done = f32[16,1,2304]{2,1,0:T(1,128)S(1)} async-done(((f32[16,1,2304]{2,1,0:T(1,128)}), f32[16,1,2304]{2,1,0:T(1,128)S(1)}, u32[]{:S(2)}, u32[]{:S(2)}) %all-to-all-start) | async-done | bytes 147488 | tf_op jit(solution)/shard_map/all_to_all | solution.py:581
  23.6 2.5 %shard_map.115 = f32[288,128]{1,0:T(8,128)S(1)} custom-call(f32[288,128]{1,0:T(8,128)S(1)} %bitcast.10, bf16[1152,1152]{1,0:T(8,128)(2,1)S(1)} %get-tuple-element.35.weights, f32[8,1152]{1,0:T(8,128)S(1)} %get-tuple-element.36.rates, f32[32,128]{1,0:T(8,128)S(1)} %get-tuple-element.37.wind), custom_call_target="tpu_custom_call" | custom-call | flops 1000000000 | bytes 3002368 | tf_op jit(solution)/shard_map/pallas_call | solution.py:539
  26.1 11.0 %all_to_all.10 = f32[16,1,2304]{2,1,0:T(1,128)S(1)} all-to-all(f32[16,1,2304]{2,1,0:T(1,128)S(1)} %bitcast.11), channel_id=1, replica_groups=mesh['nest'=2,'bin'=16] {'bin'}, dimensions={0} | all-to-all | bytes 294912 | tf_op jit(solution)/shard_map/all_to_all | solution.py:581
  37.1 1.3 %shard_map.116 = f32[72,1024]{1,0:T(8,128)} custom-call(f32[288,128]{1,0:T(8,128)S(1)} %bitcast.9, s32[1,1024]{1,0:T(1,128)S(1)} %get-tuple-element.38.place), custom_call_target="tpu_custom_call" | custom-call | flops 100000000 | bytes 446464 | tf_op jit(solution)/shard_map/pallas_call | solution.py:539
  (2 shorter events, 0.0 us)
Async XLA Ops:
  0.0 1.4 %copy-start = (f32[1,72,1024]{2,1,0:T(8,128)S(1)}, f32[1,72,1024]{2,1,0:T(8,128)}, u32[]{:S(2)}) copy-start(f32[1,72,1024]{2,1,0:T(8,128)} %param.11) | copy-start | bytes 884740
  0.0 1.4 %copy-start.5 = (s32[1,256]{1,0:T(1,128)S(1)}, s32[1,256]{1,0:T(1,128)}, u32[]{:S(2)}) copy-start(s32[1,256]{1,0:T(1,128)} %send.1) | copy-start | bytes 3076
  0.0 1.4 %copy-start.4 = (s32[1,256]{1,0:T(1,128)S(1)}, s32[1,256]{1,0:T(1,128)}, u32[]{:S(2)}) copy-start(s32[1,256]{1,0:T(1,128)} %recv.1) | copy-start | bytes 3076
  0.0 1.4 %copy-start.2 = (s32[1,1024]{1,0:T(1,128)S(1)}, s32[1,1024]{1,0:T(1,128)}, u32[]{:S(2)}) copy-start(s32[1,1024]{1,0:T(1,128)} %wet.1) | copy-start | bytes 12292
  0.0 1.4 %copy-start.1 = (s32[1,4,1024]{2,1,0:T(4,128)S(1)}, s32[1,4,1024]{2,1,0:T(4,128)}, u32[]{:S(2)}) copy-start(s32[1,4,1024]{2,1,0:T(4,128)} %param.17) | copy-start | bytes 49156
  0.0 2.9 %collective-permute-start = (f32[72,1024]{1,0:T(8,128)}, f32[72,1024]{1,0:T(8,128)S(1)}, u32[]{:S(2)}, u32[]{:S(2)}) collective-permute-start(f32[72,1024]{1,0:T(8,128)} %bitcast.12), channel_id=1, source_target_pairs={{0,16},{16,0},{1,17},{17,1},{2,18},{18,2},{3,19},{19,3},{4,20},{20... | collective-permute-start | bytes 884744 | tf_op jit(solution)/shard_map/ppermute | solution.py:585
  0.5 2.4 %collective-permute-start.1 = (s32[1,256]{1,0:T(1,128)}, s32[1,256]{1,0:T(1,128)S(1)}, u32[]{:S(2)}, u32[]{:S(2)}) collective-permute-start(s32[1,256]{1,0:T(1,128)} %send.1), channel_id=1, source_target_pairs={{0,16},{16,0},{1,17},{17,1},{2,18},{18,2},{3,19},{19,3},{4,20},{20... | collective-permute-start | bytes 3080 | tf_op jit(solution)/shard_map/ppermute | solution.py:585
  1.4 1.6 %copy-start.6 = (f32[2,72]{1,0:T(2,128)S(1)}, f32[2,72]{1,0:T(2,128)}, u32[]{:S(2)}) copy-start(f32[2,72]{1,0:T(2,128)} %courant.1) | copy-start | bytes 1732
  2.9 1.8 %copy-start.3 = (f32[1,1024]{1,0:T(1,128)S(1)}, f32[1,1024]{1,0:T(1,128)}, u32[]{:S(2)}) copy-start(f32[1,1024]{1,0:T(1,128)} %wind.1) | copy-start | bytes 12292
  4.2 1.4 %collective-permute-start.2 = (f32[72,256]{1,0:T(8,128)S(1)}, f32[72,256]{1,0:T(8,128)S(1)}, u32[]{:S(2)}, u32[]{:S(2)}) collective-permute-start(f32[72,256]{1,0:T(8,128)S(1)} %get-tuple-element.27), channel_id=1, source_target_pairs={{0,16},{16,0},{1,17},{17,1},{2,18},{18,2},{3,19},{19,3},{4,20},{20... | collective-permute-start | bytes 221192 | tf_op jit(solution)/shard_map/ppermute | solution.py:585
  5.4 10.3 %copy-start.7 = (f32[1152]{0:T(1024)S(1)}, f32[1152]{0:T(1024)}, u32[]{:S(2)}) copy-start(f32[1152]{0:T(1024)} %param.14) | copy-start | bytes 13828
  5.4 10.3 %copy-start.8 = (f32[1152]{0:T(1024)S(1)}, f32[1152]{0:T(1024)}, u32[]{:S(2)}) copy-start(f32[1152]{0:T(1024)} %param.15) | copy-start | bytes 13828
  7.5 16.2 %all-to-all-start = ((f32[16,1,2304]{2,1,0:T(1,128)}), f32[16,1,2304]{2,1,0:T(1,128)S(1)}, u32[]{:S(2)}, u32[]{:S(2)}) async-start(f32[16,1,2304]{2,1,0:T(1,128)} %bitcast.3), calls=%async_computation | async-start | bytes 294912 | tf_op jit(solution)/shard_map/all_to_all | solution.py:581

commit v6 on v5

--- a/solution.py
+++ b/solution.py
@@ -134,13 +134,26 @@
     order[0] = jnp.concatenate([ahead[count + k : count + k + 1] for k in range(count)], axis=1)
     rank[0] = jnp.concatenate([steps[k : k + 1] for k in range(count)], axis=1)
 
-    def next_row(row):
-        north = tables[2:3, span(row, cols_count)] - (row + 1) * cols_count
-        south = tables[3:4, span(row + 1, cols_count)] - row * cols_count
-        order[row + 1] = look_up(north, order[row])
-        rank[row + 1] = look_up(rank[row], south)
-
-    each(rows_count - 1, next_row)
+    def north(row):
+        return tables[2:3, span(row, cols_count)] - (row + 1) * cols_count
+
+    def south(row):
+        return tables[3:4, span(row, cols_count)] - (row - 1) * cols_count
+
+    if rows_count <= 16:
+        there, back = north(0), south(1)
+        for row in range(1, rows_count):
+            order[row] = look_up(there, order[0])
+            rank[row] = look_up(rank[0], back)
+            if row + 1 < rows_count:
+                there, back = look_up(north(row), there), look_up(back, south(row + 1))
+    else:
+
+        def next_row(row):
+            order[row + 1] = look_up(north(row), order[row])
+            rank[row + 1] = look_up(rank[row], south(row + 1))
+
+        each(rows_count - 1, next_row)
 
 
 def grid_places(listed, rank):
@@ -184,41 +197,71 @@
     return jnp.broadcast_to(row, (SUBLANES, row.shape[1]))
 
 
-def face_at(cell, onward, curve, rate):
-    estimate = cell + (0.5 - 0.5 * rate) * (onward - cell) - (1.0 - rate * rate) / 6.0 * curve
+def face_at(cell, slope, onward, curve, coefs):
+    _, lean, bend = coefs
+    estimate = cell + lean * slope - bend * curve
     return jnp.clip(estimate, jnp.minimum(cell, onward), jnp.maximum(cell, onward))
 
 
-def advance(field, moved, faces, sea, rate_east, rate_north):
-    rows_count, _, cols_count = field.shape
-
-    def east(row):
-        cell = field[row]
-        onward = pltpu.roll(cell, cols_count - 1, 1)
-        slope = onward - cell
-        bent = slope - pltpu.roll(slope, 1, 1)
-        curve = jnp.where(rate_east >= 0.0, bent, pltpu.roll(bent, cols_count - 1, 1))
-        face = face_at(cell, onward, curve, rate_east)
-        moved[row] = cell - rate_east * (face - pltpu.roll(face, 1, 1))
-
-    each(rows_count, east)
-
-    def face(row):
+def moved_east(cell, coefs):
+    size = cell.shape[1]
+    rate = coefs[0]
+    onward = pltpu.roll(cell, size - 1, 1)
+    slope = onward - cell
+    bent = slope - pltpu.roll(slope, 1, 1)
+    curve = jnp.where(rate >= 0.0, bent, pltpu.roll(bent, size - 1, 1))
+    face = face_at(cell, slope, onward, curve, coefs)
+    return cell - rate * (face - pltpu.roll(face, 1, 1))
+
+
+def advance(field, moved, faces, sea, east, north):
+    rows_count, bins, cols_count = field.shape
+    if rows_count <= 16:
+        for first in range(0, bins, SUBLANES):
+            here = slice(first, first + SUBLANES)
+            to_east, to_north = ([x[here] for x in coefs] for coefs in (east, north))
+            cells = [moved_east(field[row, here], to_east) for row in range(rows_count)]
+            onward = cells[1:] + cells[:1]
+            slopes = [b - a for a, b in zip(cells, onward)]
+            bents = [slopes[row] - slopes[row - 1] for row in range(rows_count)]
+            forward = to_north[0] >= 0.0
+            over = [
+                face_at(
+                    cells[row],
+                    slopes[row],
+                    onward[row],
+                    jnp.where(forward, bents[row], bents[(row + 1) % rows_count]),
+                    to_north,
+                )
+                for row in range(rows_count)
+            ]
+            for row in range(rows_count):
+                change = to_north[0] * (over[row] - over[row - 1])
+                field[row, here] = (cells[row] - change) * sea[row]
+        return
+
+    def to_east(row):
+        moved[row] = moved_east(field[row], east)
+
+    def over_row(row):
         ahead, second, behind = ((row + k + rows_count) % rows_count for k in (1, 2, -1))
         cell, onward = moved[row], moved[ahead]
         slope = onward - cell
         curve = jnp.where(
-            rate_north >= 0.0, slope - (cell - moved[behind]), (moved[second] - onward) - slope
+            north[0] >= 0.0, slope - (cell - moved[behind]), (moved[second] - onward) - slope
         )
-        faces[row] = face_at(cell, onward, curve, rate_north)
-
-    each(rows_count, face)
-
-    def north(row):
+        faces[row] = face_at(cell, slope, onward, curve, north)
+
+    def to_north(row):
         behind = (row - 1 + rows_count) % rows_count
-        field[row] = (moved[row] - rate_north * (faces[row] - faces[behind])) * sea[row]
-
-    each(rows_count, north)
+        field[row] = (moved[row] - north[0] * (faces[row] - faces[behind])) * sea[row]
+
+    for step in (to_east, over_row, to_north):
+        each(rows_count, step)
+
+
+def coefs_of(rates, which):
+    return [rates[3 * which + k] for k in range(3)]
 
 
 def landing(row, into, lists, cols_count):
@@ -287,9 +330,12 @@
     second = jnp.where(steps[0:1] > 1.0, 1.0, 0.0)
     for which in range(2):
         rate = column(courant[which : which + 1, :]) / steps[0:1]
-        rates[which] = jnp.broadcast_to(rate, (bins, cols_count))
-        rates[2 + which] = jnp.broadcast_to(rate * second, (bins, cols_count))
-    rates[4] = jnp.broadcast_to(second, (bins, cols_count))
+        for k, value in enumerate((rate, rate * second)):
+            at = 3 * (2 * k + which)
+            rates[at] = jnp.broadcast_to(value, (bins, cols_count))
+            rates[at + 1] = 0.5 - 0.5 * rates[at]
+            rates[at + 2] = (1.0 - rates[at] * rates[at]) * (1.0 / 6.0)
+    rates[12] = jnp.broadcast_to(second, (bins, cols_count))
 
     def sent(row):
         own = one_hot(cols_count, send_b[...] - row * cols_count)
@@ -301,7 +347,7 @@
         field[row] = base[row] + joined(dot(incoming, landing(row, into, lists, cols_count)))
 
     each(rows_count, take)
-    advance(field, moved, faces, sea, rates[0], rates[1])
+    advance(field, moved, faces, sea, coefs_of(rates, 0), coefs_of(rates, 1))
 
     def sending(row):
         return dot(split(field[row]), one_hot(cols_count, lists[0:1] - row * cols_count))
@@ -315,9 +361,9 @@
     return one_hot_across(down(ranks[row] - 1.0), 0, sea_count)
 
 
-def places_kernel(order, rank, sea, wind, ranks, picks, place, blown):
-    rows_count, _, cols_count = order.shape
-    sea_count = blown.shape[1]
+def places_kernel(rank, sea, coupling, growth, dissipation, ranks, picks, place, weights, rates):
+    rows_count, _, cols_count = rank.shape
+    sea_count = picks.shape[2]
     at = lax.broadcasted_iota(jnp.int32, (cols_count, cols_count), 0)
     across = lax.broadcasted_iota(jnp.int32, (cols_count, cols_count), 1)
     upper = jnp.where(at <= across, 1.0, 0.0).astype(bf16)
@@ -338,12 +384,9 @@
             before = number(row, before)
     else:
         lax.fori_loop(0, rows_count, number, before)
-
-    def there(row):
-        by_grid = look_up(wind[0:1, span(row, cols_count)], order[row])
-        return dot(split(eight(by_grid)), picked(row, ranks, picks, sea_count))
-
-    blown[...] = joined(total_of(rows_count, (2 * SUBLANES, sea_count), there))
+    weights[...] = jnp.transpose(coupling[...])
+    rates[0:1] = growth[...]
+    rates[1:2] = dissipation[...]
 
 
 def second_kernel(
@@ -357,7 +400,10 @@
     rates,
     ranks,
     picks,
+    order,
+    wind,
     pieces,
+    blown,
     field,
     moved,
     faces,
@@ -370,15 +416,19 @@
 
     def take(row):
         got = joined(dot(terms, landing(row, into, lists, cols_count)))
-        field[row] = jnp.where(taken[row] * rates[4, 0:1] > 0.5, got, field_in[row])
+        field[row] = jnp.where(taken[row] * rates[12, 0:1] > 0.5, got, field_in[row])
 
     each(rows_count, take)
-    advance(field, moved, faces, sea, rates[2], rates[3])
+    advance(field, moved, faces, sea, coefs_of(rates, 2), coefs_of(rates, 3))
 
     def at_sea(row):
-        return dot(split(field[row]), picked(row, ranks, picks, sea_count))
-
-    total = joined(total_of(rows_count, (2 * bins, sea_count), at_sea))
+        by_grid = look_up(wind[0:1, span(row, cols_count)], order[row])
+        terms = jnp.concatenate([split(field[row]), split(eight(by_grid))], axis=0)
+        return dot(terms, picked(row, ranks, picks, sea_count))
+
+    total = total_of(rows_count, (2 * bins + 2 * SUBLANES, sea_count), at_sea)
+    blown[...] = joined(total[2 * bins :])
+    total = joined(total[: 2 * bins])
     for tile in range(tiles):
         columns[tile] = total[:, tile * LANES : (tile + 1) * LANES]
     groups = LANES // share
@@ -398,102 +448,60 @@
     each(tiles, fold)
 
 
-def weights_kernel(
-    devices,
-    bins,
-    share,
-    coupling_in,
-    growth,
-    dissipation,
-    blown,
-    weights,
-    rates,
-    wind,
-    coupling,
-    rows,
-    sorted_rows,
-    turned,
-    arrived,
-):
-    copy = pltpu.make_async_copy(coupling_in, coupling, arrived)
-    copy.start()
-    size = coupling.shape[0]
-    lane_tiles = size // LANES
+def integrate_kernel(share, pieces, weights, rates, blown, out, values, rolled):
+    size = weights.shape[0]
+    devices = blown.shape[1] // share
     groups = LANES // share
-    block = sorted_rows.shape[0] // (devices * groups)
+    block = pieces.shape[0] // devices
+    bins = size // devices
+    even = bins == groups * block
+
+    def bins_of(device, q):
+        return pl.ds(device * bins + q, block, stride=groups)
+
+    for q in range(groups):
+        part = pieces[...]
+        if q:
+            part = pltpu.roll(part, LANES - q * share, 1)
+        if even:
+            values[pl.ds(q, devices * block, stride=groups)] = part
+        else:
+            rolled[q] = part
+    if not even:
+
+        def unfold(device):
+            for q in range(groups):
+                values[bins_of(device, q)] = rolled[q, rows_of(device, block)]
+
+        pl.loop(0, devices)(unfold)
+    now = jnp.transpose(values[0:size])[0:share]
     mine = pltpu.roll(blown[...], blown.shape[1] - lax.axis_index("bin") * share, 1)
-    wind[...] = jnp.broadcast_to(column(mine[0:1, 0:share]), wind.shape)
-    rows[size:] = jnp.zeros((rows.shape[0] - size, LANES), f32)
-
-    def sort():
-        if groups * block == bins:
-            every = devices * block
-            taken = [rows[pl.ds(q, every, stride=groups)] for q in range(groups)]
-            return jnp.concatenate(taken, axis=0)
-        at = groups * lax.broadcasted_iota(jnp.int32, (block, LANES), 0)
-        for q in range(groups):
-
-            def move(device, q=q):
-                taken = rows[pl.ds(device * bins + q, block, stride=groups)]
-                taken = jnp.where(at + q < bins, taken, 0.0)
-                sorted_rows[rows_of(q * devices + device, block)] = taken
-
-            each(devices, move)
-        return sorted_rows[...]
-
-    at = lax.broadcasted_iota(jnp.int32, (LANES, LANES), 0)
-
-    def lift(tile):
-        here = span(tile, LANES)
-        both = jnp.where(at == 0, growth[0:1, here], jnp.where(at == 1, dissipation[0:1, here], 0.0))
-        rows[here] = jnp.transpose(both)
-
-    each(lane_tiles, lift)
-    rates[...] = jnp.transpose(sort())[0:SUBLANES]
-    copy.wait()
-
-    def turn(tile):
-        rows[0:size] = coupling[:, span(tile, LANES)].astype(f32)
-        turned[span(tile, LANES)] = jnp.transpose(sort())
-
-    def lay(tile):
-        rows[0:size] = turned[:, span(tile, LANES)]
-        weights[:, span(tile, LANES)] = sort().astype(bf16)
-
-    each(lane_tiles, turn)
-    each(weights.shape[1] // LANES, lay)
-
-
-def padded_transpose(array):
-    rows_count, cols_count = array.shape
-    full = up_to(rows_count, LANES)
-    if full > rows_count:
-        array = jnp.concatenate([array, jnp.zeros((full - rows_count, cols_count), f32)], axis=0)
-    return jnp.transpose(array)
-
-
-def integrate_kernel(share, total_bins, pieces, weights, rates, wind, out):
-    width = pieces.shape[0]
-    groups = LANES // share
-    turned = padded_transpose(pieces[...])
-    now = [turned[q * share : (q + 1) * share, 0:width] for q in range(groups)]
-    now = jnp.concatenate(now, axis=1)
-    push = 1.0 + source_dt * (rates[0:1] * wind[:, 0:1])
+    push = 1.0 + source_dt * (rates[0:1] * column(mine[0:1, 0:share]))
     drag = source_dt * rates[1:2]
     for repeat in range(SRC):
         linear = dot(now.astype(bf16), weights[...])
-        mean = jnp.sum(now * now, axis=1, keepdims=True) * (1.0 / total_bins)
+        mean = jnp.sum(now * now, axis=1, keepdims=True) * (1.0 / size)
         spread = jnp.sqrt(mean + tiny_add)
         now = (now * push + source_dt * linear) / (1.0 + drag * spread)
-    back = [now[:, q * width : (q + 1) * width] for q in range(groups)]
-    back = jnp.concatenate(back, axis=0)
-    full = up_to(width, LANES)
-    if full > width:
-        back = jnp.concatenate([back, jnp.zeros((LANES, full - width), f32)], axis=1)
-    out[...] = jnp.transpose(back)[0:width]
-
-
-def spread_kernel(share, pieces, place, out, columns):
+    values[0:size] = jnp.transpose(jnp.concatenate([now, jnp.zeros((LANES - share, size), f32)], axis=0))
+    if not even:
+
+        def fold(device):
+            for q in range(groups):
+                rolled[q, rows_of(device, block)] = values[bins_of(device, q)]
+
+        pl.loop(0, devices)(fold)
+    lane_group = lax.broadcasted_iota(jnp.int32, out.shape, 1) // share
+    result = None
+    for q in range(groups):
+        part = values[pl.ds(q, devices * block, stride=groups)] if even else rolled[q]
+        if q:
+            part = pltpu.roll(part, q * share, 1)
+        result = part if q == 0 else jnp.where(lane_group == q, part, result)
+    out[...] = result
+
+
+def spread_kernel(share, pieces, place, out, columns, done, left):
     tiles, bins, _ = columns.shape
     groups = LANES // share
     block = pieces.shape[0] // (tiles * groups)
@@ -518,13 +526,20 @@
     terms = jnp.concatenate([split(columns[tile]) for tile in range(tiles)], axis=1)
 
     def scatter(row):
-        picks = one_hot(sea_count, place[0:1, span(row, cols_count)] - 1)
-        out[:, span(row, cols_count)] = joined(dot(terms, picks))
+        here = span(row, cols_count)
+        picks = one_hot(sea_count, place[0:1, here] - 1)
+        done[:, here] = joined(dot(terms, picks))
+        leave(row).start()
+
+    def leave(row):
+        here = span(row, cols_count)
+        return pltpu.make_async_copy(done.at[:, here], out.at[:, here], left.at[row])
 
     each(rows_count, scatter)
-
-
-def call(kernel, outs, scratch, operands, flops, apart=()):
+    each(rows_count, lambda row: leave(row).wait())
+
+
+def call(kernel, outs, scratch, operands, flops, apart=(), direct=False):
     held = sum(x.size * x.dtype.itemsize for x in operands)
     single = not isinstance(outs, list)
     shapes = [jax.ShapeDtypeStruct(*out) for out in ([outs] if single else outs)]
@@ -540,7 +555,7 @@
         kernel,
         out_shape=shapes[0] if single else shapes,
         in_specs=places,
-        out_specs=in_vmem if single else [in_vmem] * len(shapes),
+        out_specs=(pl.BlockSpec(memory_space=pltpu.HBM) if direct else in_vmem) if single else [in_vmem] * len(shapes),
         scratch_shapes=scratch,
         compiler_params=pltpu.CompilerParams(vmem_limit_bytes=min(60 << 20, (4 << 20) + held + own)),
         cost_estimate=pl.CostEstimate(flops=flops, bytes_accessed=held, transcendentals=0),
@@ -571,7 +586,6 @@
     block = -(-bins_here // groups)
     bins = up_to(groups * block, SUBLANES)
     size = devices * bins_here
-    sorted_size = devices * groups * block
     extra = bins - bins_here
     if extra:
         field = jnp.pad(field, ((0, extra), (0, 0)))
@@ -615,62 +629,57 @@
     )
     field, outgoing, rates = call(
         first_kernel,
-        [(grid, f32), ((bins, listed), f32), ((5, bins, cols_count), f32)],
+        [(grid, f32), ((bins, listed), f32), ((13, bins, cols_count), f32)],
         [pltpu.VMEM(grid, f32)] * 2,
         (base, into, sea, lists, spectra_b, send_b, courant, steps),
         10**9,
     )
     incoming = swap(outgoing)
     kept = rows_count if points * sea_count <= 1 << 22 else 1
-    ranks, picks, place, blown = call(
+    ranks, picks, place, weights, source_rates = call(
         places_kernel,
         [
             (row_of, f32),
             ((kept, cols_count, sea_count), bf16),
             ((1, points), jnp.int32),
-            ((SUBLANES, sea_count), f32),
+            ((size, size), bf16),
+            ((2, size), f32),
         ],
         [],
-        (order, rank, sea, wind),
+        (rank, sea, coupling, growth.reshape(1, size), dissipation.reshape(1, size)),
         10**9,
     )
     tiles = sea_count // LANES
+    pieces, blown = call(
+        functools.partial(second_kernel, share),
+        [((devices * block, LANES), f32), ((SUBLANES, sea_count), f32)],
+        [*[pltpu.VMEM(grid, f32)] * 3, pltpu.VMEM((tiles, bins, LANES), f32)],
+        (field, incoming, into, lists, taken, sea, rates, ranks, picks, order, wind),
+        10**9,
+    )
+    pieces = transpose_all(pieces)
     pieces = call(
-        functools.partial(second_kernel, share),
+        functools.partial(integrate_kernel, share),
         ((devices * block, LANES), f32),
-        [*[pltpu.VMEM(grid, f32)] * 3, pltpu.VMEM((tiles, bins, LANES), f32)],
-        (field, incoming, into, lists, taken, sea, rates, ranks, picks),
-        10**9,
-    )
-    pieces = transpose_all(pieces)
-    weights, sorted_rates, wind_here = call(
-        functools.partial(weights_kernel, devices, bins_here, share),
-        [((sorted_size, sorted_size), bf16), ((SUBLANES, sorted_size), f32), ((share, LANES), f32)],
         [
-            pltpu.VMEM((size, size), bf16),
             pltpu.VMEM((size + up_to(groups * block, SUBLANES), LANES), f32),
-            pltpu.VMEM((sorted_size, LANES), f32),
-            pltpu.VMEM((size, sorted_size), f32),
-            pltpu.SemaphoreType.DMA,
+            pltpu.VMEM((groups, devices * block, LANES), f32),
         ],
-        (coupling, growth.reshape(1, size), dissipation.reshape(1, size), blown),
-        10**9,
-        (0,),
-    )
-    pieces = call(
-        functools.partial(integrate_kernel, share, size),
-        ((devices * block, LANES), f32),
-        [],
-        (pieces, weights, sorted_rates, wind_here),
+        (pieces, weights, source_rates, blown),
         10**9,
     )
     pieces = transpose_all(pieces)
     result = call(
         functools.partial(spread_kernel, share),
         ((bins, points), f32),
-        [pltpu.VMEM((tiles, bins, LANES), f32)],
+        [
+            pltpu.VMEM((tiles, bins, LANES), f32),
+            pltpu.VMEM((bins, points), f32),
+            pltpu.SemaphoreType.DMA((rows_count,)),
+        ],
         (pieces, place),
         10**8,
+        direct=True,
     )
     return result[None, :bins_here]
 

time: 38.7 us -> 38.2 us (0.987)
  blocking collectives: 11 us -> 27 us
  starting transfers between devices: 9.32 us -> 1.11 us
  waiting for transfers between devices: 4.34 us -> 0.01 us
  Pallas kernels: 12.9 us -> 9.04 us
    all_to_all x1 -> x2, blocking collectives: 11 us -> 27 us  [transpose_all(): pieces = lax.all_to_all(pieces, 'bin', split_axis=0, concat_axis=0)]
    all_to_all x1 -> x0, starting transfers between devices: 8.21 us -> none  [transpose_all(): pieces = lax.all_to_all(pieces, 'bin', split_axis=0, concat_axis=0)]
    all_to_all x1 -> x0, waiting for transfers between devices: 4.11 us -> none  [transpose_all(): pieces = lax.all_to_all(pieces, 'bin', split_axis=0, concat_axis=0)]
    pallas_call x8 -> x7, Pallas kernels: 12.9 us -> 9.04 us  [call(): pl.pallas_call(kernel, out_shape=shapes[0] if single else shapes, in_spec...]
  transfers between devices with their start and end apart: 4 -> 3, of which waited for: 2 -> 0; matrix products, arithmetic and copies ran while one was open for 0% -> 0% of each run, Pallas kernels for 16% -> 7%
where the time goes in v6:
time: 38.2 us; the launch traced here: 38 us
  blocking collectives  27 us (71%)
  Pallas kernels  9.04 us (24%)
  starting transfers between devices  1.11 us (3%)
  between operations  0.81 us (2%)
    all_to_all x2, blocking collectives, transpose_all(): pieces = lax.all_to_all(pieces, 'bin', split_axis=0, concat_axis=0)  27 us
    pallas_call x7, Pallas kernels, call(): pl.pallas_call(kernel, out_shape=shapes[0] if single else shapes, in_spec...  9.04 us
    ppermute x3, starting transfers between devices, swap(): return lax.ppermute(array, 'nest', [(0, 1), (1, 0)])  1.11 us
  transfers between devices with their start and end apart: 3, of which 0 were waited for; matrix products, arithmetic and copies ran while one was open for 0% of the time, Pallas kernels for 7%

profile of v6, /device:TPU:0, one launch (start us, length us, event | category | flops | bytes accessed | tf_op | source)
XLA Modules:
  0.0 38.0 jit_solution(15216823887654008405)
XLA Ops:
  0.0 0.0 copy-start.1
  0.0 0.0 copy-start.6
  0.0 0.0 copy-start.5
  0.0 0.0 copy-start.3
  0.0 0.0 copy-start.2
  0.0 0.5 %collective-permute-start = (f32[72,1024]{1,0:T(8,128)}, f32[72,1024]{1,0:T(8,128)S(1)}, u32[]{:S(2)}, u32[]{:S(2)}) collective-permute-start(f32[72,1024]{1,0:T(8,128)} %bitcast.13), channel_id=1, source_target_pairs={{0,16},{16,0},{1,17},{17,1},{2,18},{18,2},{3,19},{19,3},{4,20},{20... | collective-permute-start | bytes 884744 | tf_op jit(solution)/shard_map/ppermute | solution.py:599
  0.5 0.1 collective-permute-start.1
  1.3 0.1 shard_map.110.steps
  1.4 0.0 copy-start.8
  1.4 0.0 copy-start.9
  1.4 0.0 copy-start.7
  1.4 0.0 copy-done.1
  1.4 0.0 copy-done.6
  1.4 0.0 copy-done.5
  1.4 0.0 copy-done.3
  1.4 0.0 copy-done.2
  1.4 1.4 %shard_map.109 = (s32[4,1,256]{2,1,0:T(1,128)S(1)}, s32[4,1,256]{2,1,0:T(1,128)S(1)}, f32[4,72,256]{2,1,0:T(8,128)S(1)}, bf16[4,256,256]{2,1,0:T(8,128)(2,1)S(1)...) custom-call(f32[72,1024]{1,0:T(8,128)S(1)} %bitcast.14, s32[4,1024]{1,0:T(4,128)S(1)} %bitcast.15, ...), custom_call_target="tpu_custom_call" | custom-call | flops 1000000000 | bytes 1155072 | tf_op jit(solution)/shard_map/pallas_call | solution.py:554
  2.8 0.0 copy-done.8
  2.8 0.0 copy-start
  2.8 0.0 copy-done.9
  2.9 0.0 collective-permute-done.1.send_b
  2.9 0.0 collective-permute-done.spectra_b
  2.9 0.0 copy-done.7
  2.9 1.2 %shard_map.111 = (f32[4,72,256]{2,1,0:T(8,128)S(1)}, f32[72,256]{1,0:T(8,128)S(1)}, f32[13,72,256]{2,1,0:T(8,128)S(1)}) custom-call(f32[4,72,256]{2,1,0:T(8,128)S(1)} %get-tuple-element.22.base, bf16[4,256,256]{2,1,0:T(8,128)(2,1)S(1)} %get-tuple-element.23.into, f32[4,1,256]{2,1,0:T(1,128)S(1)} %get-tuple-element.24.sea, ...), custom_call_target="tpu_custom_call" | custom-call | flops 1000000000 | bytes 2457152 | tf_op jit(solution)/shard_map/pallas_call | solution.py:554
  4.1 0.0 copy-start.4
  4.1 0.5 %collective-permute-start.2 = (f32[72,256]{1,0:T(8,128)S(1)}, f32[72,256]{1,0:T(8,128)S(1)}, u32[]{:S(2)}, u32[]{:S(2)}) collective-permute-start(f32[72,256]{1,0:T(8,128)S(1)} %get-tuple-element.27), channel_id=1, source_target_pairs={{0,16},{16,0},{1,17},{17,1},{2,18},{18,2},{3,19},{19,3},{4,20},{20... | collective-permute-start | bytes 221192 | tf_op jit(solution)/shard_map/ppermute | solution.py:599
  4.6 0.0 copy-done
  4.6 1.1 %shard_map.112 = (f32[4,1,256]{2,1,0:T(1,128)S(1)}, bf16[4,256,512]{2,1,0:T(8,128)(2,1)S(1)}, s32[1,1024]{1,0:T(1,128)S(1)}, bf16[1152,1152]{1,0:T(8,128)(2,1)S(1)}, f32[2,1152]{1,0:T(2,128)S(1)}) custom-call(s32[4,1,256]{2,1,0:T(1,128)S(1)} %get-tuple-element.30.rank, f32[4,1,256]{2,1,0:T(1,128)S(1)} %get-tuple-element.24.sea, ...), custom_call_target="tpu_custom_call" | custom-call | flops 1000000000 | bytes 6391808 | tf_op jit(solution)/shard_map/pallas_call | solution.py:554
  5.7 0.0 collective-permute-done.2.incoming
  5.8 0.0 copy-done.4
  5.8 1.2 %shard_map.113 = (f32[288,128]{1,0:T(8,128)S(1)}, f32[8,512]{1,0:T(8,128)S(1)}) custom-call(f32[4,72,256]{2,1,0:T(8,128)S(1)} %get-tuple-element.26.field_in, f32[72,256]{1,0:T(8,128)S(1)} %collective-permute-done.2.incoming, bf16[4,256,256]{2,1,0:T(8,128)(2,1)S(1)} %get-tuple-element.23.into, s32[2,256]{1,0:T(2,128)S(1)} %get-tuple-element.25.lists, ...), custom_call_target="tpu_custom_call" | custom-call | flops 1000000000 | bytes 3086336 | tf_op jit(solution)/shard_map/pallas_call | solution.py:554
  7.0 16.0 %all_to_all.10 = f32[16,1,2304]{2,1,0:T(1,128)S(1)} all-to-all(f32[16,1,2304]{2,1,0:T(1,128)S(1)} %bitcast.10), channel_id=1, replica_groups=mesh['nest'=2,'bin'=16] {'bin'}, dimensions={0} | all-to-all | bytes 294912 | tf_op jit(solution)/shard_map/all_to_all | solution.py:595
  22.9 2.8 %shard_map.114 = f32[288,128]{1,0:T(8,128)S(1)} custom-call(f32[288,128]{1,0:T(8,128)S(1)} %bitcast.11, bf16[1152,1152]{1,0:T(8,128)(2,1)S(1)} %get-tuple-element.35.weights, f32[2,1152]{1,0:T(2,128)S(1)} %get-tuple-element.36.rates, f32[8,512]{1,0:T(8,128)S(1)} %get-tuple-element.37.blown), custom_call_target="tpu_custom_call" | custom-call | flops 1000000000 | bytes 2974720 | tf_op jit(solution)/shard_map/pallas_call | solution.py:554
  25.7 11.0 %all_to_all.11 = f32[16,1,2304]{2,1,0:T(1,128)S(1)} all-to-all(f32[16,1,2304]{2,1,0:T(1,128)S(1)} %bitcast.12), channel_id=1, replica_groups=mesh['nest'=2,'bin'=16] {'bin'}, dimensions={0} | all-to-all | bytes 294912 | tf_op jit(solution)/shard_map/all_to_all | solution.py:595
  36.7 1.2 %shard_map.115 = f32[72,1024]{1,0:T(8,128)} custom-call(f32[288,128]{1,0:T(8,128)S(1)} %bitcast.9, s32[1,1024]{1,0:T(1,128)S(1)} %get-tuple-element.38.place), custom_call_target="tpu_custom_call" | custom-call | flops 100000000 | bytes 446464 | tf_op jit(solution)/shard_map/pallas_call | solution.py:554
  (2 shorter events, 0.0 us)
Async XLA Ops:
  0.0 1.4 %copy-start.1 = (f32[1,72,1024]{2,1,0:T(8,128)S(1)}, f32[1,72,1024]{2,1,0:T(8,128)}, u32[]{:S(2)}) copy-start(f32[1,72,1024]{2,1,0:T(8,128)} %param.11) | copy-start | bytes 884740
  0.0 1.4 %copy-start.6 = (s32[1,256]{1,0:T(1,128)S(1)}, s32[1,256]{1,0:T(1,128)}, u32[]{:S(2)}) copy-start(s32[1,256]{1,0:T(1,128)} %send.1) | copy-start | bytes 3076
  0.0 1.4 %copy-start.5 = (s32[1,256]{1,0:T(1,128)S(1)}, s32[1,256]{1,0:T(1,128)}, u32[]{:S(2)}) copy-start(s32[1,256]{1,0:T(1,128)} %recv.1) | copy-start | bytes 3076
  0.0 1.4 %copy-start.3 = (s32[1,1024]{1,0:T(1,128)S(1)}, s32[1,1024]{1,0:T(1,128)}, u32[]{:S(2)}) copy-start(s32[1,1024]{1,0:T(1,128)} %wet.1) | copy-start | bytes 12292
  0.0 1.4 %copy-start.2 = (s32[1,4,1024]{2,1,0:T(4,128)S(1)}, s32[1,4,1024]{2,1,0:T(4,128)}, u32[]{:S(2)}) copy-start(s32[1,4,1024]{2,1,0:T(4,128)} %param.17) | copy-start | bytes 49156
  0.0 2.9 %collective-permute-start = (f32[72,1024]{1,0:T(8,128)}, f32[72,1024]{1,0:T(8,128)S(1)}, u32[]{:S(2)}, u32[]{:S(2)}) collective-permute-start(f32[72,1024]{1,0:T(8,128)} %bitcast.13), channel_id=1, source_target_pairs={{0,16},{16,0},{1,17},{17,1},{2,18},{18,2},{3,19},{19,3},{4,20},{20... | collective-permute-start | bytes 884744 | tf_op jit(solution)/shard_map/ppermute | solution.py:599
  0.5 2.3 %collective-permute-start.1 = (s32[1,256]{1,0:T(1,128)}, s32[1,256]{1,0:T(1,128)S(1)}, u32[]{:S(2)}, u32[]{:S(2)}) collective-permute-start(s32[1,256]{1,0:T(1,128)} %send.1), channel_id=1, source_target_pairs={{0,16},{16,0},{1,17},{17,1},{2,18},{18,2},{3,19},{19,3},{4,20},{20... | collective-permute-start | bytes 3080 | tf_op jit(solution)/shard_map/ppermute | solution.py:599
  1.4 1.4 %copy-start.8 = (f32[1152]{0:T(1024)S(1)}, f32[1152]{0:T(1024)}, u32[]{:S(2)}) copy-start(f32[1152]{0:T(1024)} %param.14) | copy-start | bytes 13828
  1.4 1.5 %copy-start.9 = (f32[1152]{0:T(1024)S(1)}, f32[1152]{0:T(1024)}, u32[]{:S(2)}) copy-start(f32[1152]{0:T(1024)} %param.15) | copy-start | bytes 13828
  1.4 1.5 %copy-start.7 = (f32[2,72]{1,0:T(2,128)S(1)}, f32[2,72]{1,0:T(2,128)}, u32[]{:S(2)}) copy-start(f32[2,72]{1,0:T(2,128)} %courant.1) | copy-start | bytes 1732
  2.8 1.8 %copy-start = (bf16[1152,1152]{1,0:T(8,128)(2,1)S(1)}, bf16[1152,1152]{1,0:T(8,128)(2,1)}, u32[]{:S(2)}) copy-start(bf16[1152,1152]{1,0:T(8,128)(2,1)} %coupling.1) | copy-start | bytes 7962628
  4.1 1.6 %copy-start.4 = (f32[1,1024]{1,0:T(1,128)S(1)}, f32[1,1024]{1,0:T(1,128)}, u32[]{:S(2)}) copy-start(f32[1,1024]{1,0:T(1,128)} %wind.1) | copy-start | bytes 12292
  4.1 1.6 %collective-permute-start.2 = (f32[72,256]{1,0:T(8,128)S(1)}, f32[72,256]{1,0:T(8,128)S(1)}, u32[]{:S(2)}, u32[]{:S(2)}) collective-permute-start(f32[72,256]{1,0:T(8,128)S(1)} %get-tuple-element.27), channel_id=1, source_target_pairs={{0,16},{16,0},{1,17},{17,1},{2,18},{18,2},{3,19},{19,3},{4,20},{20... | collective-permute-start | bytes 221192 | tf_op jit(solution)/shard_map/ppermute | solution.py:599

commit v7 on v6

--- a/solution.py
+++ b/solution.py
@@ -448,7 +448,7 @@
     each(tiles, fold)
 
 
-def integrate_kernel(share, pieces, weights, rates, blown, out, values, rolled):
+def integrate_kernel(share, pieces, weights, rates, blown, out, values, parts):
     size = weights.shape[0]
     devices = blown.shape[1] // share
     groups = LANES // share
@@ -459,22 +459,20 @@
     def bins_of(device, q):
         return pl.ds(device * bins + q, block, stride=groups)
 
-    for q in range(groups):
-        part = pieces[...]
-        if q:
-            part = pltpu.roll(part, LANES - q * share, 1)
-        if even:
-            values[pl.ds(q, devices * block, stride=groups)] = part
-        else:
-            rolled[q] = part
-    if not even:
-
-        def unfold(device):
-            for q in range(groups):
-                values[bins_of(device, q)] = rolled[q, rows_of(device, block)]
-
+    def unfold(device):
+        for q in range(groups):
+            values[bins_of(device, q)] = pieces[rows_of(device, block)]
+
+    if even:
+        for q in range(groups):
+            values[pl.ds(q, devices * block, stride=groups)] = pieces[...]
+    else:
         pl.loop(0, devices)(unfold)
-    now = jnp.transpose(values[0:size])[0:share]
+    turned = jnp.transpose(values[0:size])
+    group = lax.broadcasted_iota(jnp.int32, (share, size), 1) % bins % groups
+    now = turned[0:share]
+    for q in range(1, groups):
+        now = jnp.where(group == q, turned[q * share : (q + 1) * share], now)
     mine = pltpu.roll(blown[...], blown.shape[1] - lax.axis_index("bin") * share, 1)
     push = 1.0 + source_dt * (rates[0:1] * column(mine[0:1, 0:share]))
     drag = source_dt * rates[1:2]
@@ -483,20 +481,18 @@
         mean = jnp.sum(now * now, axis=1, keepdims=True) * (1.0 / size)
         spread = jnp.sqrt(mean + tiny_add)
         now = (now * push + source_dt * linear) / (1.0 + drag * spread)
-    values[0:size] = jnp.transpose(jnp.concatenate([now, jnp.zeros((LANES - share, size), f32)], axis=0))
+    values[0:size] = jnp.transpose(jnp.concatenate([now] * groups, axis=0))
+
+    def fold(device):
+        for q in range(groups):
+            parts[q, rows_of(device, block)] = values[bins_of(device, q)]
+
     if not even:
-
-        def fold(device):
-            for q in range(groups):
-                rolled[q, rows_of(device, block)] = values[bins_of(device, q)]
-
         pl.loop(0, devices)(fold)
     lane_group = lax.broadcasted_iota(jnp.int32, out.shape, 1) // share
     result = None
     for q in range(groups):
-        part = values[pl.ds(q, devices * block, stride=groups)] if even else rolled[q]
-        if q:
-            part = pltpu.roll(part, q * share, 1)
+        part = values[pl.ds(q, devices * block, stride=groups)] if even else parts[q]
         result = part if q == 0 else jnp.where(lane_group == q, part, result)
     out[...] = result
 

time: 38.2 us -> 37.8 us (0.990)
  no operation moved by 1% of the time
where the time goes in v7:
time: 37.8 us; the launch traced here: 37.6 us
  blocking collectives  27 us (71%)
  Pallas kernels  8.69 us (23%)
  starting transfers between devices  1.11 us (3%)
  between operations  0.81 us (2%)
    all_to_all x2, blocking collectives, transpose_all(): pieces = lax.all_to_all(pieces, 'bin', split_axis=0, concat_axis=0)  27 us
    pallas_call x7, Pallas kernels, call(): pl.pallas_call(kernel, out_shape=shapes[0] if single else shapes, in_spec...  8.69 us
    ppermute x3, starting transfers between devices, swap(): return lax.ppermute(array, 'nest', [(0, 1), (1, 0)])  1.11 us
  transfers between devices with their start and end apart: 3, of which 0 were waited for; matrix products, arithmetic and copies ran while one was open for 0% of the time, Pallas kernels for 7%

profile of v7, /device:TPU:0, one launch (start us, length us, event | category | flops | bytes accessed | tf_op | source)
XLA Modules:
  0.0 37.6 jit_solution(8721778459377033513)
XLA Ops:
  0.0 0.0 copy-start.1
  0.0 0.0 copy-start.6
  0.0 0.0 copy-start.5
  0.0 0.0 copy-start.3
  0.0 0.0 copy-start.2
  0.0 0.5 %collective-permute-start = (f32[72,1024]{1,0:T(8,128)}, f32[72,1024]{1,0:T(8,128)S(1)}, u32[]{:S(2)}, u32[]{:S(2)}) collective-permute-start(f32[72,1024]{1,0:T(8,128)} %bitcast.13), channel_id=1, source_target_pairs={{0,16},{16,0},{1,17},{17,1},{2,18},{18,2},{3,19},{19,3},{4,20},{20... | collective-permute-start | bytes 884744 | tf_op jit(solution)/shard_map/ppermute | solution.py:595
  0.5 0.1 collective-permute-start.1
  1.3 0.1 shard_map.110.steps
  1.4 0.0 copy-start.8
  1.4 0.0 copy-start.9
  1.4 0.0 copy-start.7
  1.4 0.0 copy-done.1
  1.4 0.0 copy-done.6
  1.4 0.0 copy-done.5
  1.4 0.0 copy-done.3
  1.4 0.0 copy-done.2
  1.4 1.4 %shard_map.109 = (s32[4,1,256]{2,1,0:T(1,128)S(1)}, s32[4,1,256]{2,1,0:T(1,128)S(1)}, f32[4,72,256]{2,1,0:T(8,128)S(1)}, bf16[4,256,256]{2,1,0:T(8,128)(2,1)S(1)...) custom-call(f32[72,1024]{1,0:T(8,128)S(1)} %bitcast.14, s32[4,1024]{1,0:T(4,128)S(1)} %bitcast.15, ...), custom_call_target="tpu_custom_call" | custom-call | flops 1000000000 | bytes 1155072 | tf_op jit(solution)/shard_map/pallas_call | solution.py:550
  2.8 0.0 copy-done.8
  2.8 0.0 copy-start
  2.8 0.0 copy-done.9
  2.9 0.0 collective-permute-done.1.send_b
  2.9 0.0 collective-permute-done.spectra_b
  2.9 0.0 copy-done.7
  2.9 1.2 %shard_map.111 = (f32[4,72,256]{2,1,0:T(8,128)S(1)}, f32[72,256]{1,0:T(8,128)S(1)}, f32[13,72,256]{2,1,0:T(8,128)S(1)}) custom-call(f32[4,72,256]{2,1,0:T(8,128)S(1)} %get-tuple-element.22.base, bf16[4,256,256]{2,1,0:T(8,128)(2,1)S(1)} %get-tuple-element.23.into, f32[4,1,256]{2,1,0:T(1,128)S(1)} %get-tuple-element.24.sea, ...), custom_call_target="tpu_custom_call" | custom-call | flops 1000000000 | bytes 2457152 | tf_op jit(solution)/shard_map/pallas_call | solution.py:550
  4.1 0.0 copy-start.4
  4.1 0.5 %collective-permute-start.2 = (f32[72,256]{1,0:T(8,128)S(1)}, f32[72,256]{1,0:T(8,128)S(1)}, u32[]{:S(2)}, u32[]{:S(2)}) collective-permute-start(f32[72,256]{1,0:T(8,128)S(1)} %get-tuple-element.27), channel_id=1, source_target_pairs={{0,16},{16,0},{1,17},{17,1},{2,18},{18,2},{3,19},{19,3},{4,20},{20... | collective-permute-start | bytes 221192 | tf_op jit(solution)/shard_map/ppermute | solution.py:595
  4.6 0.0 copy-done
  4.6 1.1 %shard_map.112 = (f32[4,1,256]{2,1,0:T(1,128)S(1)}, bf16[4,256,512]{2,1,0:T(8,128)(2,1)S(1)}, s32[1,1024]{1,0:T(1,128)S(1)}, bf16[1152,1152]{1,0:T(8,128)(2,1)S(1)}, f32[2,1152]{1,0:T(2,128)S(1)}) custom-call(s32[4,1,256]{2,1,0:T(1,128)S(1)} %get-tuple-element.30.rank, f32[4,1,256]{2,1,0:T(1,128)S(1)} %get-tuple-element.24.sea, ...), custom_call_target="tpu_custom_call" | custom-call | flops 1000000000 | bytes 6391808 | tf_op jit(solution)/shard_map/pallas_call | solution.py:550
  5.7 0.0 collective-permute-done.2.incoming
  5.8 0.0 copy-done.4
  5.8 1.2 %shard_map.113 = (f32[288,128]{1,0:T(8,128)S(1)}, f32[8,512]{1,0:T(8,128)S(1)}) custom-call(f32[4,72,256]{2,1,0:T(8,128)S(1)} %get-tuple-element.26.field_in, f32[72,256]{1,0:T(8,128)S(1)} %collective-permute-done.2.incoming, bf16[4,256,256]{2,1,0:T(8,128)(2,1)S(1)} %get-tuple-element.23.into, s32[2,256]{1,0:T(2,128)S(1)} %get-tuple-element.25.lists, ...), custom_call_target="tpu_custom_call" | custom-call | flops 1000000000 | bytes 3086336 | tf_op jit(solution)/shard_map/pallas_call | solution.py:550
  7.0 16.0 %all_to_all.10 = f32[16,1,2304]{2,1,0:T(1,128)S(1)} all-to-all(f32[16,1,2304]{2,1,0:T(1,128)S(1)} %bitcast.10), channel_id=1, replica_groups=mesh['nest'=2,'bin'=16] {'bin'}, dimensions={0} | all-to-all | bytes 294912 | tf_op jit(solution)/shard_map/all_to_all | solution.py:591
  22.9 2.5 %shard_map.114 = f32[288,128]{1,0:T(8,128)S(1)} custom-call(f32[288,128]{1,0:T(8,128)S(1)} %bitcast.11, bf16[1152,1152]{1,0:T(8,128)(2,1)S(1)} %get-tuple-element.35.weights, f32[2,1152]{1,0:T(2,128)S(1)} %get-tuple-element.36.rates, f32[8,512]{1,0:T(8,128)S(1)} %get-tuple-element.37.blown), custom_call_target="tpu_custom_call" | custom-call | flops 1000000000 | bytes 2974720 | tf_op jit(solution)/shard_map/pallas_call | solution.py:550
  25.4 11.0 %all_to_all.11 = f32[16,1,2304]{2,1,0:T(1,128)S(1)} all-to-all(f32[16,1,2304]{2,1,0:T(1,128)S(1)} %bitcast.12), channel_id=1, replica_groups=mesh['nest'=2,'bin'=16] {'bin'}, dimensions={0} | all-to-all | bytes 294912 | tf_op jit(solution)/shard_map/all_to_all | solution.py:591
  36.4 1.2 %shard_map.115 = f32[72,1024]{1,0:T(8,128)} custom-call(f32[288,128]{1,0:T(8,128)S(1)} %bitcast.9, s32[1,1024]{1,0:T(1,128)S(1)} %get-tuple-element.38.place), custom_call_target="tpu_custom_call" | custom-call | flops 100000000 | bytes 446464 | tf_op jit(solution)/shard_map/pallas_call | solution.py:550
  (2 shorter events, 0.0 us)
Async XLA Ops:
  0.0 1.4 %copy-start.1 = (f32[1,72,1024]{2,1,0:T(8,128)S(1)}, f32[1,72,1024]{2,1,0:T(8,128)}, u32[]{:S(2)}) copy-start(f32[1,72,1024]{2,1,0:T(8,128)} %param.11) | copy-start | bytes 884740
  0.0 1.4 %copy-start.6 = (s32[1,256]{1,0:T(1,128)S(1)}, s32[1,256]{1,0:T(1,128)}, u32[]{:S(2)}) copy-start(s32[1,256]{1,0:T(1,128)} %send.1) | copy-start | bytes 3076
  0.0 1.4 %copy-start.5 = (s32[1,256]{1,0:T(1,128)S(1)}, s32[1,256]{1,0:T(1,128)}, u32[]{:S(2)}) copy-start(s32[1,256]{1,0:T(1,128)} %recv.1) | copy-start | bytes 3076
  0.0 1.4 %copy-start.3 = (s32[1,1024]{1,0:T(1,128)S(1)}, s32[1,1024]{1,0:T(1,128)}, u32[]{:S(2)}) copy-start(s32[1,1024]{1,0:T(1,128)} %wet.1) | copy-start | bytes 12292
  0.0 1.4 %copy-start.2 = (s32[1,4,1024]{2,1,0:T(4,128)S(1)}, s32[1,4,1024]{2,1,0:T(4,128)}, u32[]{:S(2)}) copy-start(s32[1,4,1024]{2,1,0:T(4,128)} %param.17) | copy-start | bytes 49156
  0.0 2.9 %collective-permute-start = (f32[72,1024]{1,0:T(8,128)}, f32[72,1024]{1,0:T(8,128)S(1)}, u32[]{:S(2)}, u32[]{:S(2)}) collective-permute-start(f32[72,1024]{1,0:T(8,128)} %bitcast.13), channel_id=1, source_target_pairs={{0,16},{16,0},{1,17},{17,1},{2,18},{18,2},{3,19},{19,3},{4,20},{20... | collective-permute-start | bytes 884744 | tf_op jit(solution)/shard_map/ppermute | solution.py:595
  0.5 2.3 %collective-permute-start.1 = (s32[1,256]{1,0:T(1,128)}, s32[1,256]{1,0:T(1,128)S(1)}, u32[]{:S(2)}, u32[]{:S(2)}) collective-permute-start(s32[1,256]{1,0:T(1,128)} %send.1), channel_id=1, source_target_pairs={{0,16},{16,0},{1,17},{17,1},{2,18},{18,2},{3,19},{19,3},{4,20},{20... | collective-permute-start | bytes 3080 | tf_op jit(solution)/shard_map/ppermute | solution.py:595
  1.4 1.4 %copy-start.8 = (f32[1152]{0:T(1024)S(1)}, f32[1152]{0:T(1024)}, u32[]{:S(2)}) copy-start(f32[1152]{0:T(1024)} %param.14) | copy-start | bytes 13828
  1.4 1.5 %copy-start.9 = (f32[1152]{0:T(1024)S(1)}, f32[1152]{0:T(1024)}, u32[]{:S(2)}) copy-start(f32[1152]{0:T(1024)} %param.15) | copy-start | bytes 13828
  1.4 1.5 %copy-start.7 = (f32[2,72]{1,0:T(2,128)S(1)}, f32[2,72]{1,0:T(2,128)}, u32[]{:S(2)}) copy-start(f32[2,72]{1,0:T(2,128)} %courant.1) | copy-start | bytes 1732
  2.8 1.8 %copy-start = (bf16[1152,1152]{1,0:T(8,128)(2,1)S(1)}, bf16[1152,1152]{1,0:T(8,128)(2,1)}, u32[]{:S(2)}) copy-start(bf16[1152,1152]{1,0:T(8,128)(2,1)} %coupling.1) | copy-start | bytes 7962628
  4.1 1.6 %copy-start.4 = (f32[1,1024]{1,0:T(1,128)S(1)}, f32[1,1024]{1,0:T(1,128)}, u32[]{:S(2)}) copy-start(f32[1,1024]{1,0:T(1,128)} %wind.1) | copy-start | bytes 12292
  4.1 1.6 %collective-permute-start.2 = (f32[72,256]{1,0:T(8,128)S(1)}, f32[72,256]{1,0:T(8,128)S(1)}, u32[]{:S(2)}, u32[]{:S(2)}) collective-permute-start(f32[72,256]{1,0:T(8,128)S(1)} %get-tuple-element.27), channel_id=1, source_target_pairs={{0,16},{16,0},{1,17},{17,1},{2,18},{18,2},{3,19},{19,3},{4,20},{20... | collective-permute-start | bytes 221192 | tf_op jit(solution)/shard_map/ppermute | solution.py:595

commit v8 on v7

--- a/solution.py
+++ b/solution.py
@@ -384,7 +384,12 @@
             before = number(row, before)
     else:
         lax.fori_loop(0, rows_count, number, before)
-    weights[...] = jnp.transpose(coupling[...])
+    turned = min(2 * cols_count, weights.shape[0])
+    unit = jnp.where(at == across, 1.0, 0.0).astype(bf16)
+    for first in range(0, turned, cols_count):
+        here = slice(first, first + cols_count)
+        weights[here] = dot_t(unit, coupling[:, here]).astype(bf16)
+    weights[turned:] = jnp.transpose(coupling[:, turned:])
     rates[0:1] = growth[...]
     rates[1:2] = dissipation[...]
 

time: 37.8 us -> 37.6 us (level)
  transfers between devices with their start and end apart: 3 -> 3, of which waited for: 0 -> 0; matrix products, arithmetic and copies ran while one was open for 0% -> 0% of each run, Pallas kernels for 7% -> 6%
where the time goes in v8:
time: 37.6 us; the launch traced here: 37.4 us
  blocking collectives  27 us (72%)
  Pallas kernels  8.45 us (22%)
  starting transfers between devices  1.11 us (3%)
  between operations  0.8 us (2%)
    all_to_all x2, blocking collectives, transpose_all(): pieces = lax.all_to_all(pieces, 'bin', split_axis=0, concat_axis=0)  27 us
    pallas_call x7, Pallas kernels, call(): pl.pallas_call(kernel, out_shape=shapes[0] if single else shapes, in_spec...  8.45 us
    ppermute x3, starting transfers between devices, swap(): return lax.ppermute(array, 'nest', [(0, 1), (1, 0)])  1.11 us
  transfers between devices with their start and end apart: 3, of which 0 were waited for; matrix products, arithmetic and copies ran while one was open for 0% of the time, Pallas kernels for 6%

profile of v8, /device:TPU:0, one launch (start us, length us, event | category | flops | bytes accessed | tf_op | source)
XLA Modules:
  0.0 37.4 jit_solution(14661254284428944311)
XLA Ops:
  0.0 0.0 copy-start.1
  0.0 0.0 copy-start.6
  0.0 0.0 copy-start.5
  0.0 0.0 copy-start.3
  0.0 0.0 copy-start.2
  0.0 0.5 %collective-permute-start = (f32[72,1024]{1,0:T(8,128)}, f32[72,1024]{1,0:T(8,128)S(1)}, u32[]{:S(2)}, u32[]{:S(2)}) collective-permute-start(f32[72,1024]{1,0:T(8,128)} %bitcast.13), channel_id=1, source_target_pairs={{0,16},{16,0},{1,17},{17,1},{2,18},{18,2},{3,19},{19,3},{4,20},{20... | collective-permute-start | bytes 884744 | tf_op jit(solution)/shard_map/ppermute | solution.py:600
  0.5 0.1 collective-permute-start.1
  1.3 0.1 shard_map.110.steps
  1.4 0.0 copy-start.8
  1.4 0.0 copy-start.9
  1.4 0.0 copy-start.7
  1.4 0.0 copy-done.1
  1.4 0.0 copy-done.6
  1.4 0.0 copy-done.5
  1.4 0.0 copy-done.3
  1.4 0.0 copy-done.2
  1.4 1.4 %shard_map.109 = (s32[4,1,256]{2,1,0:T(1,128)S(1)}, s32[4,1,256]{2,1,0:T(1,128)S(1)}, f32[4,72,256]{2,1,0:T(8,128)S(1)}, bf16[4,256,256]{2,1,0:T(8,128)(2,1)S(1)...) custom-call(f32[72,1024]{1,0:T(8,128)S(1)} %bitcast.14, s32[4,1024]{1,0:T(4,128)S(1)} %bitcast.15, ...), custom_call_target="tpu_custom_call" | custom-call | flops 1000000000 | bytes 1155072 | tf_op jit(solution)/shard_map/pallas_call | solution.py:555
  2.8 0.0 copy-done.8
  2.8 0.0 copy-start
  2.8 0.0 copy-done.9
  2.9 0.0 collective-permute-done.1.send_b
  2.9 0.0 collective-permute-done.spectra_b
  2.9 0.0 copy-done.7
  2.9 1.2 %shard_map.111 = (f32[4,72,256]{2,1,0:T(8,128)S(1)}, f32[72,256]{1,0:T(8,128)S(1)}, f32[13,72,256]{2,1,0:T(8,128)S(1)}) custom-call(f32[4,72,256]{2,1,0:T(8,128)S(1)} %get-tuple-element.22.base, bf16[4,256,256]{2,1,0:T(8,128)(2,1)S(1)} %get-tuple-element.23.into, f32[4,1,256]{2,1,0:T(1,128)S(1)} %get-tuple-element.24.sea, ...), custom_call_target="tpu_custom_call" | custom-call | flops 1000000000 | bytes 2457152 | tf_op jit(solution)/shard_map/pallas_call | solution.py:555
  4.1 0.0 copy-start.4
  4.1 0.5 %collective-permute-start.2 = (f32[72,256]{1,0:T(8,128)S(1)}, f32[72,256]{1,0:T(8,128)S(1)}, u32[]{:S(2)}, u32[]{:S(2)}) collective-permute-start(f32[72,256]{1,0:T(8,128)S(1)} %get-tuple-element.27), channel_id=1, source_target_pairs={{0,16},{16,0},{1,17},{17,1},{2,18},{18,2},{3,19},{19,3},{4,20},{20... | collective-permute-start | bytes 221192 | tf_op jit(solution)/shard_map/ppermute | solution.py:600
  4.6 0.0 copy-done
  4.6 0.9 %shard_map.112 = (f32[4,1,256]{2,1,0:T(1,128)S(1)}, bf16[4,256,512]{2,1,0:T(8,128)(2,1)S(1)}, s32[1,1024]{1,0:T(1,128)S(1)}, bf16[1152,1152]{1,0:T(8,128)(2,1)S(1)}, f32[2,1152]{1,0:T(2,128)S(1)}) custom-call(s32[4,1,256]{2,1,0:T(1,128)S(1)} %get-tuple-element.30.rank, f32[4,1,256]{2,1,0:T(1,128)S(1)} %get-tuple-element.24.sea, ...), custom_call_target="tpu_custom_call" | custom-call | flops 1000000000 | bytes 6391808 | tf_op jit(solution)/shard_map/pallas_call | solution.py:555
  5.5 0.0 collective-permute-done.2.incoming
  5.5 0.0 copy-done.4
  5.5 1.2 %shard_map.113 = (f32[288,128]{1,0:T(8,128)S(1)}, f32[8,512]{1,0:T(8,128)S(1)}) custom-call(f32[4,72,256]{2,1,0:T(8,128)S(1)} %get-tuple-element.26.field_in, f32[72,256]{1,0:T(8,128)S(1)} %collective-permute-done.2.incoming, bf16[4,256,256]{2,1,0:T(8,128)(2,1)S(1)} %get-tuple-element.23.into, s32[2,256]{1,0:T(2,128)S(1)} %get-tuple-element.25.lists, ...), custom_call_target="tpu_custom_call" | custom-call | flops 1000000000 | bytes 3086336 | tf_op jit(solution)/shard_map/pallas_call | solution.py:555
  6.7 16.0 %all_to_all.10 = f32[16,1,2304]{2,1,0:T(1,128)S(1)} all-to-all(f32[16,1,2304]{2,1,0:T(1,128)S(1)} %bitcast.10), channel_id=1, replica_groups=mesh['nest'=2,'bin'=16] {'bin'}, dimensions={0} | all-to-all | bytes 294912 | tf_op jit(solution)/shard_map/all_to_all | solution.py:596
  22.7 2.5 %shard_map.114 = f32[288,128]{1,0:T(8,128)S(1)} custom-call(f32[288,128]{1,0:T(8,128)S(1)} %bitcast.11, bf16[1152,1152]{1,0:T(8,128)(2,1)S(1)} %get-tuple-element.35.weights, f32[2,1152]{1,0:T(2,128)S(1)} %get-tuple-element.36.rates, f32[8,512]{1,0:T(8,128)S(1)} %get-tuple-element.37.blown), custom_call_target="tpu_custom_call" | custom-call | flops 1000000000 | bytes 2974720 | tf_op jit(solution)/shard_map/pallas_call | solution.py:555
  25.2 11.0 %all_to_all.11 = f32[16,1,2304]{2,1,0:T(1,128)S(1)} all-to-all(f32[16,1,2304]{2,1,0:T(1,128)S(1)} %bitcast.12), channel_id=1, replica_groups=mesh['nest'=2,'bin'=16] {'bin'}, dimensions={0} | all-to-all | bytes 294912 | tf_op jit(solution)/shard_map/all_to_all | solution.py:596
  36.2 1.2 %shard_map.115 = f32[72,1024]{1,0:T(8,128)} custom-call(f32[288,128]{1,0:T(8,128)S(1)} %bitcast.9, s32[1,1024]{1,0:T(1,128)S(1)} %get-tuple-element.38.place), custom_call_target="tpu_custom_call" | custom-call | flops 100000000 | bytes 446464 | tf_op jit(solution)/shard_map/pallas_call | solution.py:555
  (2 shorter events, 0.0 us)
Async XLA Ops:
  0.0 1.4 %copy-start.1 = (f32[1,72,1024]{2,1,0:T(8,128)S(1)}, f32[1,72,1024]{2,1,0:T(8,128)}, u32[]{:S(2)}) copy-start(f32[1,72,1024]{2,1,0:T(8,128)} %param.11) | copy-start | bytes 884740
  0.0 1.4 %copy-start.6 = (s32[1,256]{1,0:T(1,128)S(1)}, s32[1,256]{1,0:T(1,128)}, u32[]{:S(2)}) copy-start(s32[1,256]{1,0:T(1,128)} %send.1) | copy-start | bytes 3076
  0.0 1.4 %copy-start.5 = (s32[1,256]{1,0:T(1,128)S(1)}, s32[1,256]{1,0:T(1,128)}, u32[]{:S(2)}) copy-start(s32[1,256]{1,0:T(1,128)} %recv.1) | copy-start | bytes 3076
  0.0 1.4 %copy-start.3 = (s32[1,1024]{1,0:T(1,128)S(1)}, s32[1,1024]{1,0:T(1,128)}, u32[]{:S(2)}) copy-start(s32[1,1024]{1,0:T(1,128)} %wet.1) | copy-start | bytes 12292
  0.0 1.4 %copy-start.2 = (s32[1,4,1024]{2,1,0:T(4,128)S(1)}, s32[1,4,1024]{2,1,0:T(4,128)}, u32[]{:S(2)}) copy-start(s32[1,4,1024]{2,1,0:T(4,128)} %param.17) | copy-start | bytes 49156
  0.0 2.9 %collective-permute-start = (f32[72,1024]{1,0:T(8,128)}, f32[72,1024]{1,0:T(8,128)S(1)}, u32[]{:S(2)}, u32[]{:S(2)}) collective-permute-start(f32[72,1024]{1,0:T(8,128)} %bitcast.13), channel_id=1, source_target_pairs={{0,16},{16,0},{1,17},{17,1},{2,18},{18,2},{3,19},{19,3},{4,20},{20... | collective-permute-start | bytes 884744 | tf_op jit(solution)/shard_map/ppermute | solution.py:600
  0.5 2.3 %collective-permute-start.1 = (s32[1,256]{1,0:T(1,128)}, s32[1,256]{1,0:T(1,128)S(1)}, u32[]{:S(2)}, u32[]{:S(2)}) collective-permute-start(s32[1,256]{1,0:T(1,128)} %send.1), channel_id=1, source_target_pairs={{0,16},{16,0},{1,17},{17,1},{2,18},{18,2},{3,19},{19,3},{4,20},{20... | collective-permute-start | bytes 3080 | tf_op jit(solution)/shard_map/ppermute | solution.py:600
  1.4 1.4 %copy-start.8 = (f32[1152]{0:T(1024)S(1)}, f32[1152]{0:T(1024)}, u32[]{:S(2)}) copy-start(f32[1152]{0:T(1024)} %param.14) | copy-start | bytes 13828
  1.4 1.5 %copy-start.9 = (f32[1152]{0:T(1024)S(1)}, f32[1152]{0:T(1024)}, u32[]{:S(2)}) copy-start(f32[1152]{0:T(1024)} %param.15) | copy-start | bytes 13828
  1.4 1.5 %copy-start.7 = (f32[2,72]{1,0:T(2,128)S(1)}, f32[2,72]{1,0:T(2,128)}, u32[]{:S(2)}) copy-start(f32[2,72]{1,0:T(2,128)} %courant.1) | copy-start | bytes 1732
  2.8 1.8 %copy-start = (bf16[1152,1152]{1,0:T(8,128)(2,1)S(1)}, bf16[1152,1152]{1,0:T(8,128)(2,1)}, u32[]{:S(2)}) copy-start(bf16[1152,1152]{1,0:T(8,128)(2,1)} %coupling.1) | copy-start | bytes 7962628
  4.1 1.4 %copy-start.4 = (f32[1,1024]{1,0:T(1,128)S(1)}, f32[1,1024]{1,0:T(1,128)}, u32[]{:S(2)}) copy-start(f32[1,1024]{1,0:T(1,128)} %wind.1) | copy-start | bytes 12292
  4.1 1.4 %collective-permute-start.2 = (f32[72,256]{1,0:T(8,128)S(1)}, f32[72,256]{1,0:T(8,128)S(1)}, u32[]{:S(2)}, u32[]{:S(2)}) collective-permute-start(f32[72,256]{1,0:T(8,128)S(1)} %get-tuple-element.27), channel_id=1, source_target_pairs={{0,16},{16,0},{1,17},{17,1},{2,18},{18,2},{3,19},{19,3},{4,20},{20... | collective-permute-start | bytes 221192 | tf_op jit(solution)/shard_map/ppermute | solution.py:600

commit v9 on v8

--- a/solution.py
+++ b/solution.py
@@ -12,6 +12,7 @@
 SRC = 5
 LANES = 128
 SUBLANES = 8
+CHUNK = 640
 
 source_dt = 0.25
 tiny_add = 1e-06
@@ -117,21 +118,24 @@
     count = cols_count // LANES
     bits = (cols_count - 1).bit_length()
     at = lax.broadcasted_iota(jnp.int32, (SUBLANES, LANES), 0)
-    place = (at % count) * LANES + lax.broadcasted_iota(jnp.int32, (SUBLANES, LANES), 1)
+    lane = lax.broadcasted_iota(jnp.int32, (SUBLANES, LANES), 1)
+    point = (at % count) * LANES + lane
+    column_at = lane * count + at % count
 
     first = tables[0:1, 0:cols_count]
     ahead = jnp.where(at < count, rows_stacked(tiles_of(first)), 0)
     behind = rows_stacked(tiles_of(tables[1:2, 0:cols_count]))
-    behind = jnp.where(place == 0, 0, behind)
-    steps = jnp.where(place == 0, 0, 1)
+    behind = jnp.where(point == 0, 0, behind)
+    steps = jnp.where(point == 0, 0, 1)
     for bit in range(bits):
         far = taken_from([ahead[k : k + 1] for k in range(count)], ahead)
         both = (steps << bits) + behind
         back = taken_from([both[k : k + 1] for k in range(count)], behind)
-        ahead = jnp.where((at >= count) & ((place >> bit) & 1 == 0), ahead, far)
+        ahead = jnp.where((at >= count) & ((column_at >> bit) & 1 == 0), ahead, far)
         steps = steps + (back >> bits)
         behind = back & ((1 << bits) - 1)
     order[0] = jnp.concatenate([ahead[count + k : count + k + 1] for k in range(count)], axis=1)
+    steps = steps % count * LANES + steps // count
     rank[0] = jnp.concatenate([steps[k : k + 1] for k in range(count)], axis=1)
 
     def north(row):
@@ -197,21 +201,27 @@
     return jnp.broadcast_to(row, (SUBLANES, row.shape[1]))
 
 
-def face_at(cell, slope, onward, curve, coefs):
-    _, lean, bend = coefs
-    estimate = cell + lean * slope - bend * curve
+def face_at(cell, onward, slope, other, coefs):
+    _, near, far = coefs
+    estimate = cell + near * slope + far * other
     return jnp.clip(estimate, jnp.minimum(cell, onward), jnp.maximum(cell, onward))
 
 
-def moved_east(cell, coefs):
-    size = cell.shape[1]
+def ahead(tiles):
+    return tiles[1:] + [pltpu.roll(tiles[0], LANES - 1, 1)]
+
+
+def behind(tiles):
+    return [pltpu.roll(tiles[-1], 1, 1)] + tiles[:-1]
+
+
+def moved_east(cells, coefs):
     rate = coefs[0]
-    onward = pltpu.roll(cell, size - 1, 1)
-    slope = onward - cell
-    bent = slope - pltpu.roll(slope, 1, 1)
-    curve = jnp.where(rate >= 0.0, bent, pltpu.roll(bent, size - 1, 1))
-    face = face_at(cell, slope, onward, curve, coefs)
-    return cell - rate * (face - pltpu.roll(face, 1, 1))
+    onward = ahead(cells)
+    slopes = [b - a for a, b in zip(cells, onward)]
+    others = [jnp.where(rate >= 0.0, a, b) for a, b in zip(behind(slopes), ahead(slopes))]
+    faces = [face_at(*values, coefs) for values in zip(cells, onward, slopes, others)]
+    return [a - rate * (b - c) for a, b, c in zip(cells, faces, behind(faces))]
 
 
 def advance(field, moved, faces, sea, east, north):
@@ -219,42 +229,42 @@
     if rows_count <= 16:
         for first in range(0, bins, SUBLANES):
             here = slice(first, first + SUBLANES)
-            to_east, to_north = ([x[here] for x in coefs] for coefs in (east, north))
-            cells = [moved_east(field[row, here], to_east) for row in range(rows_count)]
-            onward = cells[1:] + cells[:1]
-            slopes = [b - a for a, b in zip(cells, onward)]
-            bents = [slopes[row] - slopes[row - 1] for row in range(rows_count)]
+            to_east, to_north = ([x[here, :LANES] for x in coefs] for coefs in (east, north))
             forward = to_north[0] >= 0.0
-            over = [
-                face_at(
-                    cells[row],
-                    slopes[row],
-                    onward[row],
-                    jnp.where(forward, bents[row], bents[(row + 1) % rows_count]),
-                    to_north,
-                )
-                for row in range(rows_count)
-            ]
-            for row in range(rows_count):
-                change = to_north[0] * (over[row] - over[row - 1])
-                field[row, here] = (cells[row] - change) * sea[row]
+            rows = [moved_east(tiles_of(field[row, here]), to_east) for row in range(rows_count)]
+            for k in range(cols_count // LANES):
+                cells = [tiles[k] for tiles in rows]
+                onward = cells[1:] + cells[:1]
+                slopes = [b - a for a, b in zip(cells, onward)]
+                over = [
+                    face_at(
+                        cells[row],
+                        onward[row],
+                        slopes[row],
+                        jnp.where(forward, slopes[row - 1], slopes[(row + 1) % rows_count]),
+                        to_north,
+                    )
+                    for row in range(rows_count)
+                ]
+                there = slice(k * LANES, (k + 1) * LANES)
+                for row in range(rows_count):
+                    change = to_north[0] * (over[row] - over[row - 1])
+                    field[row, here, there] = (cells[row] - change) * sea[row, :, there]
         return
 
     def to_east(row):
-        moved[row] = moved_east(field[row], east)
+        tiles = moved_east(tiles_of(field[row]), [x[:, :LANES] for x in east])
+        moved[row] = jnp.concatenate(tiles, axis=1)
 
     def over_row(row):
-        ahead, second, behind = ((row + k + rows_count) % rows_count for k in (1, 2, -1))
-        cell, onward = moved[row], moved[ahead]
-        slope = onward - cell
-        curve = jnp.where(
-            north[0] >= 0.0, slope - (cell - moved[behind]), (moved[second] - onward) - slope
-        )
-        faces[row] = face_at(cell, slope, onward, curve, north)
+        first, second, last = (moved[(row + k + rows_count) % rows_count] for k in (1, 2, -1))
+        cell = moved[row]
+        other = jnp.where(north[0] >= 0.0, cell - last, second - first)
+        faces[row] = face_at(cell, first, first - cell, other, north)
 
     def to_north(row):
-        behind = (row - 1 + rows_count) % rows_count
-        field[row] = (moved[row] - north[0] * (faces[row] - faces[behind])) * sea[row]
+        last = (row - 1 + rows_count) % rows_count
+        field[row] = (moved[row] - north[0] * (faces[row] - faces[last])) * sea[row]
 
     for step in (to_east, over_row, to_north):
         each(rows_count, step)
@@ -333,8 +343,10 @@
         for k, value in enumerate((rate, rate * second)):
             at = 3 * (2 * k + which)
             rates[at] = jnp.broadcast_to(value, (bins, cols_count))
-            rates[at + 1] = 0.5 - 0.5 * rates[at]
-            rates[at + 2] = (1.0 - rates[at] * rates[at]) * (1.0 / 6.0)
+            bend = (1.0 - rates[at] * rates[at]) * (1.0 / 6.0)
+            bend = jnp.where(rates[at] >= 0.0, bend, -bend)
+            rates[at + 1] = 0.5 - 0.5 * rates[at] - bend
+            rates[at + 2] = bend
     rates[12] = jnp.broadcast_to(second, (bins, cols_count))
 
     def sent(row):
@@ -384,7 +396,7 @@
             before = number(row, before)
     else:
         lax.fori_loop(0, rows_count, number, before)
-    turned = min(2 * cols_count, weights.shape[0])
+    turned = min(2, weights.shape[0] // cols_count) * cols_count
     unit = jnp.where(at == across, 1.0, 0.0).astype(bf16)
     for first in range(0, turned, cols_count):
         here = slice(first, first + cols_count)
@@ -482,7 +494,9 @@
     push = 1.0 + source_dt * (rates[0:1] * column(mine[0:1, 0:share]))
     drag = source_dt * rates[1:2]
     for repeat in range(SRC):
-        linear = dot(now.astype(bf16), weights[...])
+        terms = now.astype(bf16)
+        linear = [dot(terms, weights[:, at : at + CHUNK]) for at in range(0, size, CHUNK)]
+        linear = jnp.concatenate(linear, axis=1)
         mean = jnp.sum(now * now, axis=1, keepdims=True) * (1.0 / size)
         spread = jnp.sqrt(mean + tiny_add)
         now = (now * push + source_dt * linear) / (1.0 + drag * spread)

time: 37.6 us -> 37.2 us (0.989)
  Pallas kernels: 8.45 us -> 7.99 us
    pallas_call x7, Pallas kernels: 8.45 us -> 7.99 us  [call(): pl.pallas_call(kernel, out_shape=shapes[0] if single else shapes, in_spec...]
where the time goes in v9:
time: 37.2 us; the launch traced here: 37 us
  blocking collectives  26.9 us (72%)
  Pallas kernels  7.99 us (21%)
  starting transfers between devices  1.11 us (3%)
  between operations  0.81 us (2%)
    all_to_all x2, blocking collectives, transpose_all(): pieces = lax.all_to_all(pieces, 'bin', split_axis=0, concat_axis=0)  26.9 us
    pallas_call x7, Pallas kernels, call(): pl.pallas_call(kernel, out_shape=shapes[0] if single else shapes, in_spec...  7.99 us
    ppermute x3, starting transfers between devices, swap(): return lax.ppermute(array, 'nest', [(0, 1), (1, 0)])  1.11 us
  transfers between devices with their start and end apart: 3, of which 0 were waited for; matrix products, arithmetic and copies ran while one was open for 0% of the time, Pallas kernels for 6%

profile of v9, /device:TPU:0, one launch (start us, length us, event | category | flops | bytes accessed | tf_op | source)
XLA Modules:
  0.0 37.0 jit_solution(1758398602992798810)
XLA Ops:
  0.0 0.0 copy-start.1
  0.0 0.0 copy-start.6
  0.0 0.0 copy-start.5
  0.0 0.0 copy-start.3
  0.0 0.0 copy-start.2
  0.0 0.5 %collective-permute-start = (f32[72,1024]{1,0:T(8,128)}, f32[72,1024]{1,0:T(8,128)S(1)}, u32[]{:S(2)}, u32[]{:S(2)}) collective-permute-start(f32[72,1024]{1,0:T(8,128)} %bitcast.13), channel_id=1, source_target_pairs={{0,16},{16,0},{1,17},{17,1},{2,18},{18,2},{3,19},{19,3},{4,20},{20... | collective-permute-start | bytes 884744 | tf_op jit(solution)/shard_map/ppermute | solution.py:614
  0.5 0.1 collective-permute-start.1
  1.3 0.1 shard_map.110.steps
  1.4 0.0 copy-start.8
  1.4 0.0 copy-start.9
  1.4 0.0 copy-start.7
  1.4 0.0 copy-done.1
  1.4 0.0 copy-done.6
  1.4 0.0 copy-done.5
  1.4 0.0 copy-done.3
  1.4 0.0 copy-done.2
  1.4 1.4 %shard_map.109 = (s32[4,1,256]{2,1,0:T(1,128)S(1)}, s32[4,1,256]{2,1,0:T(1,128)S(1)}, f32[4,72,256]{2,1,0:T(8,128)S(1)}, bf16[4,256,256]{2,1,0:T(8,128)(2,1)S(1)...) custom-call(f32[72,1024]{1,0:T(8,128)S(1)} %bitcast.14, s32[4,1024]{1,0:T(4,128)S(1)} %bitcast.15, ...), custom_call_target="tpu_custom_call" | custom-call | flops 1000000000 | bytes 1155072 | tf_op jit(solution)/shard_map/pallas_call | solution.py:569
  2.8 0.0 copy-done.8
  2.8 0.0 copy-start
  2.8 0.0 copy-done.9
  2.9 0.0 collective-permute-done.1.send_b
  2.9 0.0 collective-permute-done.spectra_b
  2.9 0.0 copy-done.7
  2.9 1.1 %shard_map.111 = (f32[4,72,256]{2,1,0:T(8,128)S(1)}, f32[72,256]{1,0:T(8,128)S(1)}, f32[13,72,256]{2,1,0:T(8,128)S(1)}) custom-call(f32[4,72,256]{2,1,0:T(8,128)S(1)} %get-tuple-element.22.base, bf16[4,256,256]{2,1,0:T(8,128)(2,1)S(1)} %get-tuple-element.23.into, f32[4,1,256]{2,1,0:T(1,128)S(1)} %get-tuple-element.24.sea, ...), custom_call_target="tpu_custom_call" | custom-call | flops 1000000000 | bytes 2457152 | tf_op jit(solution)/shard_map/pallas_call | solution.py:569
  4.0 0.0 copy-start.4
  4.0 0.5 %collective-permute-start.2 = (f32[72,256]{1,0:T(8,128)S(1)}, f32[72,256]{1,0:T(8,128)S(1)}, u32[]{:S(2)}, u32[]{:S(2)}) collective-permute-start(f32[72,256]{1,0:T(8,128)S(1)} %get-tuple-element.27), channel_id=1, source_target_pairs={{0,16},{16,0},{1,17},{17,1},{2,18},{18,2},{3,19},{19,3},{4,20},{20... | collective-permute-start | bytes 221192 | tf_op jit(solution)/shard_map/ppermute | solution.py:614
  4.5 0.1 copy-done
  4.6 0.9 %shard_map.112 = (f32[4,1,256]{2,1,0:T(1,128)S(1)}, bf16[4,256,512]{2,1,0:T(8,128)(2,1)S(1)}, s32[1,1024]{1,0:T(1,128)S(1)}, bf16[1152,1152]{1,0:T(8,128)(2,1)S(1)}, f32[2,1152]{1,0:T(2,128)S(1)}) custom-call(s32[4,1,256]{2,1,0:T(1,128)S(1)} %get-tuple-element.30.rank, f32[4,1,256]{2,1,0:T(1,128)S(1)} %get-tuple-element.24.sea, ...), custom_call_target="tpu_custom_call" | custom-call | flops 1000000000 | bytes 6391808 | tf_op jit(solution)/shard_map/pallas_call | solution.py:569
  5.4 0.0 collective-permute-done.2.incoming
  5.4 0.0 copy-done.4
  5.5 1.0 %shard_map.113 = (f32[288,128]{1,0:T(8,128)S(1)}, f32[8,512]{1,0:T(8,128)S(1)}) custom-call(f32[4,72,256]{2,1,0:T(8,128)S(1)} %get-tuple-element.26.field_in, f32[72,256]{1,0:T(8,128)S(1)} %collective-permute-done.2.incoming, bf16[4,256,256]{2,1,0:T(8,128)(2,1)S(1)} %get-tuple-element.23.into, s32[2,256]{1,0:T(2,128)S(1)} %get-tuple-element.25.lists, ...), custom_call_target="tpu_custom_call" | custom-call | flops 1000000000 | bytes 3086336 | tf_op jit(solution)/shard_map/pallas_call | solution.py:569
  6.5 16.0 %all_to_all.10 = f32[16,1,2304]{2,1,0:T(1,128)S(1)} all-to-all(f32[16,1,2304]{2,1,0:T(1,128)S(1)} %bitcast.10), channel_id=1, replica_groups=mesh['nest'=2,'bin'=16] {'bin'}, dimensions={0} | all-to-all | bytes 294912 | tf_op jit(solution)/shard_map/all_to_all | solution.py:610
  22.4 2.3 %shard_map.114 = f32[288,128]{1,0:T(8,128)S(1)} custom-call(f32[288,128]{1,0:T(8,128)S(1)} %bitcast.11, bf16[1152,1152]{1,0:T(8,128)(2,1)S(1)} %get-tuple-element.35.weights, f32[2,1152]{1,0:T(2,128)S(1)} %get-tuple-element.36.rates, f32[8,512]{1,0:T(8,128)S(1)} %get-tuple-element.37.blown), custom_call_target="tpu_custom_call" | custom-call | flops 1000000000 | bytes 2974720 | tf_op jit(solution)/shard_map/pallas_call | solution.py:569
  24.8 11.0 %all_to_all.11 = f32[16,1,2304]{2,1,0:T(1,128)S(1)} all-to-all(f32[16,1,2304]{2,1,0:T(1,128)S(1)} %bitcast.12), channel_id=1, replica_groups=mesh['nest'=2,'bin'=16] {'bin'}, dimensions={0} | all-to-all | bytes 294912 | tf_op jit(solution)/shard_map/all_to_all | solution.py:610
  35.8 1.2 %shard_map.115 = f32[72,1024]{1,0:T(8,128)} custom-call(f32[288,128]{1,0:T(8,128)S(1)} %bitcast.9, s32[1,1024]{1,0:T(1,128)S(1)} %get-tuple-element.38.place), custom_call_target="tpu_custom_call" | custom-call | flops 100000000 | bytes 446464 | tf_op jit(solution)/shard_map/pallas_call | solution.py:569
  (2 shorter events, 0.0 us)
Async XLA Ops:
  0.0 1.4 %copy-start.1 = (f32[1,72,1024]{2,1,0:T(8,128)S(1)}, f32[1,72,1024]{2,1,0:T(8,128)}, u32[]{:S(2)}) copy-start(f32[1,72,1024]{2,1,0:T(8,128)} %param.11) | copy-start | bytes 884740
  0.0 1.4 %copy-start.6 = (s32[1,256]{1,0:T(1,128)S(1)}, s32[1,256]{1,0:T(1,128)}, u32[]{:S(2)}) copy-start(s32[1,256]{1,0:T(1,128)} %send.1) | copy-start | bytes 3076
  0.0 1.4 %copy-start.5 = (s32[1,256]{1,0:T(1,128)S(1)}, s32[1,256]{1,0:T(1,128)}, u32[]{:S(2)}) copy-start(s32[1,256]{1,0:T(1,128)} %recv.1) | copy-start | bytes 3076
  0.0 1.4 %copy-start.3 = (s32[1,1024]{1,0:T(1,128)S(1)}, s32[1,1024]{1,0:T(1,128)}, u32[]{:S(2)}) copy-start(s32[1,1024]{1,0:T(1,128)} %wet.1) | copy-start | bytes 12292
  0.0 1.4 %copy-start.2 = (s32[1,4,1024]{2,1,0:T(4,128)S(1)}, s32[1,4,1024]{2,1,0:T(4,128)}, u32[]{:S(2)}) copy-start(s32[1,4,1024]{2,1,0:T(4,128)} %param.17) | copy-start | bytes 49156
  0.0 2.9 %collective-permute-start = (f32[72,1024]{1,0:T(8,128)}, f32[72,1024]{1,0:T(8,128)S(1)}, u32[]{:S(2)}, u32[]{:S(2)}) collective-permute-start(f32[72,1024]{1,0:T(8,128)} %bitcast.13), channel_id=1, source_target_pairs={{0,16},{16,0},{1,17},{17,1},{2,18},{18,2},{3,19},{19,3},{4,20},{20... | collective-permute-start | bytes 884744 | tf_op jit(solution)/shard_map/ppermute | solution.py:614
  0.5 2.3 %collective-permute-start.1 = (s32[1,256]{1,0:T(1,128)}, s32[1,256]{1,0:T(1,128)S(1)}, u32[]{:S(2)}, u32[]{:S(2)}) collective-permute-start(s32[1,256]{1,0:T(1,128)} %send.1), channel_id=1, source_target_pairs={{0,16},{16,0},{1,17},{17,1},{2,18},{18,2},{3,19},{19,3},{4,20},{20... | collective-permute-start | bytes 3080 | tf_op jit(solution)/shard_map/ppermute | solution.py:614
  1.4 1.4 %copy-start.8 = (f32[1152]{0:T(1024)S(1)}, f32[1152]{0:T(1024)}, u32[]{:S(2)}) copy-start(f32[1152]{0:T(1024)} %param.14) | copy-start | bytes 13828
  1.4 1.5 %copy-start.9 = (f32[1152]{0:T(1024)S(1)}, f32[1152]{0:T(1024)}, u32[]{:S(2)}) copy-start(f32[1152]{0:T(1024)} %param.15) | copy-start | bytes 13828
  1.4 1.5 %copy-start.7 = (f32[2,72]{1,0:T(2,128)S(1)}, f32[2,72]{1,0:T(2,128)}, u32[]{:S(2)}) copy-start(f32[2,72]{1,0:T(2,128)} %courant.1) | copy-start | bytes 1732
  2.8 1.8 %copy-start = (bf16[1152,1152]{1,0:T(8,128)(2,1)S(1)}, bf16[1152,1152]{1,0:T(8,128)(2,1)}, u32[]{:S(2)}) copy-start(bf16[1152,1152]{1,0:T(8,128)(2,1)} %coupling.1) | copy-start | bytes 7962628
  4.0 1.5 %copy-start.4 = (f32[1,1024]{1,0:T(1,128)S(1)}, f32[1,1024]{1,0:T(1,128)}, u32[]{:S(2)}) copy-start(f32[1,1024]{1,0:T(1,128)} %wind.1) | copy-start | bytes 12292
  4.0 1.5 %collective-permute-start.2 = (f32[72,256]{1,0:T(8,128)S(1)}, f32[72,256]{1,0:T(8,128)S(1)}, u32[]{:S(2)}, u32[]{:S(2)}) collective-permute-start(f32[72,256]{1,0:T(8,128)S(1)} %get-tuple-element.27), channel_id=1, source_target_pairs={{0,16},{16,0},{1,17},{17,1},{2,18},{18,2},{3,19},{19,3},{4,20},{20... | collective-permute-start | bytes 221192 | tf_op jit(solution)/shard_map/ppermute | solution.py:614

commit v10 on v9

--- a/solution.py
+++ b/solution.py
@@ -453,13 +453,14 @@
     lane_group = lax.broadcasted_iota(jnp.int32, (block, LANES), 1) // share
 
     def fold(tile):
-        parts = [columns[tile, pl.ds(q, block, stride=groups)] for q in range(groups)]
+        parts = []
+        for q in range(groups):
+            part = columns[tile, pl.ds(q, block, stride=groups)]
+            parts.append(pltpu.roll(part, q * share, 1) if q else part)
         for j in range(groups):
-            piece = parts[j]
-            for q in range(groups):
-                if q != j:
-                    part = pltpu.roll(parts[q], ((q - j) % groups) * share, 1)
-                    piece = jnp.where(lane_group == q, part, piece)
+            piece = parts[-j % groups]
+            for g in range(1, groups):
+                piece = jnp.where(lane_group == g, parts[(g - j) % groups], piece)
             pieces[rows_of(tile * groups + j, block)] = piece
 
     each(tiles, fold)
@@ -475,6 +476,9 @@
 
     def bins_of(device, q):
         return pl.ds(device * bins + q, block, stride=groups)
+
+    me = lax.axis_index("bin")
+    shift = lax.rem(me, groups)
 
     def unfold(device):
         for q in range(groups):
@@ -488,9 +492,10 @@
     turned = jnp.transpose(values[0:size])
     group = lax.broadcasted_iota(jnp.int32, (share, size), 1) % bins % groups
     now = turned[0:share]
-    for q in range(1, groups):
-        now = jnp.where(group == q, turned[q * share : (q + 1) * share], now)
-    mine = pltpu.roll(blown[...], blown.shape[1] - lax.axis_index("bin") * share, 1)
+    for g in range(1, groups):
+        here = group == lax.rem(g + groups - shift, groups)
+        now = jnp.where(here, turned[g * share : (g + 1) * share], now)
+    mine = pltpu.roll(blown[...], blown.shape[1] - me * share, 1)
     push = 1.0 + source_dt * (rates[0:1] * column(mine[0:1, 0:share]))
     drag = source_dt * rates[1:2]
     for repeat in range(SRC):
@@ -512,7 +517,7 @@
     result = None
     for q in range(groups):
         part = values[pl.ds(q, devices * block, stride=groups)] if even else parts[q]
-        result = part if q == 0 else jnp.where(lane_group == q, part, result)
+        result = part if q == 0 else jnp.where(lane_group == lax.rem(q + shift, groups), part, result)
     out[...] = result
 
 
@@ -530,11 +535,11 @@
     def unfold(tile):
         parts = [pieces[rows_of(tile * groups + j, block)] for j in range(groups)]
         for q in range(groups):
-            part = parts[q]
-            for j in range(groups):
-                if j != q:
-                    other = pltpu.roll(parts[j], ((j - q) % groups) * share, 1)
-                    part = jnp.where(lane_group == j, other, part)
+            part = parts[-q % groups]
+            for g in range(1, groups):
+                part = jnp.where(lane_group == g, parts[(g - q) % groups], part)
+            if q:
+                part = pltpu.roll(part, LANES - q * share, 1)
             columns[tile, pl.ds(q, block, stride=groups)] = part
 
     each(tiles, unfold)
@@ -647,7 +652,7 @@
         [(grid, f32), ((bins, listed), f32), ((13, bins, cols_count), f32)],
         [pltpu.VMEM(grid, f32)] * 2,
         (base, into, sea, lists, spectra_b, send_b, courant, steps),
-        10**9,
+        10**8,
     )
     incoming = swap(outgoing)
     kept = rows_count if points * sea_count <= 1 << 22 else 1

time: 37.2 us -> 36.9 us (level)
  no operation moved by 1% of the time
where the time goes in v10:
time: 36.9 us; the launch traced here: 36.7 us
  blocking collectives  26.9 us (73%)
  Pallas kernels  7.75 us (21%)
  starting transfers between devices  1.11 us (3%)
  between operations  0.79 us (2%)
    all_to_all x2, blocking collectives, transpose_all(): pieces = lax.all_to_all(pieces, 'bin', split_axis=0, concat_axis=0)  26.9 us
    pallas_call x7, Pallas kernels, call(): pl.pallas_call(kernel, out_shape=shapes[0] if single else shapes, in_spec...  7.75 us
    ppermute x3, starting transfers between devices, swap(): return lax.ppermute(array, 'nest', [(0, 1), (1, 0)])  1.11 us
  transfers between devices with their start and end apart: 3, of which 0 were waited for; matrix products, arithmetic and copies ran while one was open for 0% of the time, Pallas kernels for 6%

profile of v10, /device:TPU:0, one launch (start us, length us, event | category | flops | bytes accessed | tf_op | source)
XLA Modules:
  0.0 36.7 jit_solution(17016174412759576686)
XLA Ops:
  0.0 0.0 copy-start.2
  0.0 0.0 copy-start.7
  0.0 0.0 copy-start.6
  0.0 0.0 copy-start.4
  0.0 0.0 copy-start.3
  0.0 0.5 %collective-permute-start = (f32[72,1024]{1,0:T(8,128)}, f32[72,1024]{1,0:T(8,128)S(1)}, u32[]{:S(2)}, u32[]{:S(2)}) collective-permute-start(f32[72,1024]{1,0:T(8,128)} %bitcast.13), channel_id=1, source_target_pairs={{0,16},{16,0},{1,17},{17,1},{2,18},{18,2},{3,19},{19,3},{4,20},{20... | collective-permute-start | bytes 884744 | tf_op jit(solution)/shard_map/ppermute | solution.py:619
  0.5 0.1 collective-permute-start.1
  1.3 0.1 shard_map.110.steps
  1.4 0.0 copy-start.8
  1.4 0.0 copy-start.9
  1.4 0.0 copy-start
  1.4 0.0 copy-start.1
  1.4 0.0 copy-done.2
  1.4 0.0 copy-done.7
  1.4 0.0 copy-done.6
  1.4 0.0 copy-done.4
  1.4 0.0 copy-done.3
  1.4 1.4 %shard_map.109 = (s32[4,1,256]{2,1,0:T(1,128)S(1)}, s32[4,1,256]{2,1,0:T(1,128)S(1)}, f32[4,72,256]{2,1,0:T(8,128)S(1)}, bf16[4,256,256]{2,1,0:T(8,128)(2,1)S(1)...) custom-call(f32[72,1024]{1,0:T(8,128)S(1)} %bitcast.14, s32[4,1024]{1,0:T(4,128)S(1)} %bitcast.15, ...), custom_call_target="tpu_custom_call" | custom-call | flops 1000000000 | bytes 1155072 | tf_op jit(solution)/shard_map/pallas_call | solution.py:574
  2.8 0.0 copy-done.8
  2.8 0.0 copy-start.5
  2.8 0.0 copy-done.9
  2.9 0.0 collective-permute-done.1.send_b
  2.9 0.0 collective-permute-done.spectra_b
  2.9 0.0 copy-done
  2.9 1.1 %shard_map.111 = (f32[4,72,256]{2,1,0:T(8,128)S(1)}, f32[72,256]{1,0:T(8,128)S(1)}, f32[13,72,256]{2,1,0:T(8,128)S(1)}) custom-call(f32[4,72,256]{2,1,0:T(8,128)S(1)} %get-tuple-element.22.base, bf16[4,256,256]{2,1,0:T(8,128)(2,1)S(1)} %get-tuple-element.23.into, f32[4,1,256]{2,1,0:T(1,128)S(1)} %get-tuple-element.24.sea, ...), custom_call_target="tpu_custom_call" | custom-call | flops 100000000 | bytes 2457152 | tf_op jit(solution)/shard_map/pallas_call | solution.py:574
  4.0 0.5 %collective-permute-start.2 = (f32[72,256]{1,0:T(8,128)S(1)}, f32[72,256]{1,0:T(8,128)S(1)}, u32[]{:S(2)}, u32[]{:S(2)}) collective-permute-start(f32[72,256]{1,0:T(8,128)S(1)} %get-tuple-element.27), channel_id=1, source_target_pairs={{0,16},{16,0},{1,17},{17,1},{2,18},{18,2},{3,19},{19,3},{4,20},{20... | collective-permute-start | bytes 221192 | tf_op jit(solution)/shard_map/ppermute | solution.py:619
  4.5 0.0 copy-done.1
  4.5 0.9 %shard_map.112 = (f32[4,1,256]{2,1,0:T(1,128)S(1)}, bf16[4,256,512]{2,1,0:T(8,128)(2,1)S(1)}, s32[1,1024]{1,0:T(1,128)S(1)}, bf16[1152,1152]{1,0:T(8,128)(2,1)S(1)}, f32[2,1152]{1,0:T(2,128)S(1)}) custom-call(s32[4,1,256]{2,1,0:T(1,128)S(1)} %get-tuple-element.30.rank, f32[4,1,256]{2,1,0:T(1,128)S(1)} %get-tuple-element.24.sea, ...), custom_call_target="tpu_custom_call" | custom-call | flops 1000000000 | bytes 6391808 | tf_op jit(solution)/shard_map/pallas_call | solution.py:574
  5.3 0.0 collective-permute-done.2.incoming
  5.4 0.0 copy-done.5
  5.4 0.9 %shard_map.113 = (f32[288,128]{1,0:T(8,128)S(1)}, f32[8,512]{1,0:T(8,128)S(1)}) custom-call(f32[4,72,256]{2,1,0:T(8,128)S(1)} %get-tuple-element.26.field_in, f32[72,256]{1,0:T(8,128)S(1)} %collective-permute-done.2.incoming, bf16[4,256,256]{2,1,0:T(8,128)(2,1)S(1)} %get-tuple-element.23.into, s32[2,256]{1,0:T(2,128)S(1)} %get-tuple-element.25.lists, ...), custom_call_target="tpu_custom_call" | custom-call | flops 1000000000 | bytes 3086336 | tf_op jit(solution)/shard_map/pallas_call | solution.py:574
  6.3 16.0 %all_to_all.10 = f32[16,1,2304]{2,1,0:T(1,128)S(1)} all-to-all(f32[16,1,2304]{2,1,0:T(1,128)S(1)} %bitcast.10), channel_id=1, replica_groups=mesh['nest'=2,'bin'=16] {'bin'}, dimensions={0} | all-to-all | bytes 294912 | tf_op jit(solution)/shard_map/all_to_all | solution.py:615
  22.2 2.3 %shard_map.114 = f32[288,128]{1,0:T(8,128)S(1)} custom-call(f32[288,128]{1,0:T(8,128)S(1)} %bitcast.11, bf16[1152,1152]{1,0:T(8,128)(2,1)S(1)} %get-tuple-element.35.weights, f32[2,1152]{1,0:T(2,128)S(1)} %get-tuple-element.36.rates, f32[8,512]{1,0:T(8,128)S(1)} %get-tuple-element.37.blown), custom_call_target="tpu_custom_call" | custom-call | flops 1000000000 | bytes 2974720 | tf_op jit(solution)/shard_map/pallas_call | solution.py:574
  24.6 11.0 %all_to_all.11 = f32[16,1,2304]{2,1,0:T(1,128)S(1)} all-to-all(f32[16,1,2304]{2,1,0:T(1,128)S(1)} %bitcast.12), channel_id=1, replica_groups=mesh['nest'=2,'bin'=16] {'bin'}, dimensions={0} | all-to-all | bytes 294912 | tf_op jit(solution)/shard_map/all_to_all | solution.py:615
  35.6 1.1 %shard_map.115 = f32[72,1024]{1,0:T(8,128)} custom-call(f32[288,128]{1,0:T(8,128)S(1)} %bitcast.9, s32[1,1024]{1,0:T(1,128)S(1)} %get-tuple-element.38.place), custom_call_target="tpu_custom_call" | custom-call | flops 100000000 | bytes 446464 | tf_op jit(solution)/shard_map/pallas_call | solution.py:574
  (2 shorter events, 0.0 us)
Async XLA Ops:
  0.0 1.4 %copy-start.2 = (f32[1,72,1024]{2,1,0:T(8,128)S(1)}, f32[1,72,1024]{2,1,0:T(8,128)}, u32[]{:S(2)}) copy-start(f32[1,72,1024]{2,1,0:T(8,128)} %param.11) | copy-start | bytes 884740
  0.0 1.4 %copy-start.7 = (s32[1,256]{1,0:T(1,128)S(1)}, s32[1,256]{1,0:T(1,128)}, u32[]{:S(2)}) copy-start(s32[1,256]{1,0:T(1,128)} %send.1) | copy-start | bytes 3076
  0.0 1.4 %copy-start.6 = (s32[1,256]{1,0:T(1,128)S(1)}, s32[1,256]{1,0:T(1,128)}, u32[]{:S(2)}) copy-start(s32[1,256]{1,0:T(1,128)} %recv.1) | copy-start | bytes 3076
  0.0 1.4 %copy-start.4 = (s32[1,1024]{1,0:T(1,128)S(1)}, s32[1,1024]{1,0:T(1,128)}, u32[]{:S(2)}) copy-start(s32[1,1024]{1,0:T(1,128)} %wet.1) | copy-start | bytes 12292
  0.0 1.4 %copy-start.3 = (s32[1,4,1024]{2,1,0:T(4,128)S(1)}, s32[1,4,1024]{2,1,0:T(4,128)}, u32[]{:S(2)}) copy-start(s32[1,4,1024]{2,1,0:T(4,128)} %param.17) | copy-start | bytes 49156
  0.0 2.9 %collective-permute-start = (f32[72,1024]{1,0:T(8,128)}, f32[72,1024]{1,0:T(8,128)S(1)}, u32[]{:S(2)}, u32[]{:S(2)}) collective-permute-start(f32[72,1024]{1,0:T(8,128)} %bitcast.13), channel_id=1, source_target_pairs={{0,16},{16,0},{1,17},{17,1},{2,18},{18,2},{3,19},{19,3},{4,20},{20... | collective-permute-start | bytes 884744 | tf_op jit(solution)/shard_map/ppermute | solution.py:619
  0.5 2.3 %collective-permute-start.1 = (s32[1,256]{1,0:T(1,128)}, s32[1,256]{1,0:T(1,128)S(1)}, u32[]{:S(2)}, u32[]{:S(2)}) collective-permute-start(s32[1,256]{1,0:T(1,128)} %send.1), channel_id=1, source_target_pairs={{0,16},{16,0},{1,17},{17,1},{2,18},{18,2},{3,19},{19,3},{4,20},{20... | collective-permute-start | bytes 3080 | tf_op jit(solution)/shard_map/ppermute | solution.py:619
  1.4 1.4 %copy-start.8 = (f32[1152]{0:T(1024)S(1)}, f32[1152]{0:T(1024)}, u32[]{:S(2)}) copy-start(f32[1152]{0:T(1024)} %param.14) | copy-start | bytes 13828
  1.4 1.5 %copy-start.9 = (f32[1152]{0:T(1024)S(1)}, f32[1152]{0:T(1024)}, u32[]{:S(2)}) copy-start(f32[1152]{0:T(1024)} %param.15) | copy-start | bytes 13828
  1.4 1.5 %copy-start = (f32[2,72]{1,0:T(2,128)S(1)}, f32[2,72]{1,0:T(2,128)}, u32[]{:S(2)}) copy-start(f32[2,72]{1,0:T(2,128)} %courant.1) | copy-start | bytes 1732
  1.4 3.1 %copy-start.1 = (bf16[1152,1152]{1,0:T(8,128)(2,1)S(1)}, bf16[1152,1152]{1,0:T(8,128)(2,1)}, u32[]{:S(2)}) copy-start(bf16[1152,1152]{1,0:T(8,128)(2,1)} %coupling.1) | copy-start | bytes 7962628
  2.8 2.6 %copy-start.5 = (f32[1,1024]{1,0:T(1,128)S(1)}, f32[1,1024]{1,0:T(1,128)}, u32[]{:S(2)}) copy-start(f32[1,1024]{1,0:T(1,128)} %wind.1) | copy-start | bytes 12292
  4.0 1.4 %collective-permute-start.2 = (f32[72,256]{1,0:T(8,128)S(1)}, f32[72,256]{1,0:T(8,128)S(1)}, u32[]{:S(2)}, u32[]{:S(2)}) collective-permute-start(f32[72,256]{1,0:T(8,128)S(1)} %get-tuple-element.27), channel_id=1, source_target_pairs={{0,16},{16,0},{1,17},{17,1},{2,18},{18,2},{3,19},{19,3},{4,20},{20... | collective-permute-start | bytes 221192 | tf_op jit(solution)/shard_map/ppermute | solution.py:619

commit v11 on v10

--- a/solution.py
+++ b/solution.py
@@ -47,9 +47,13 @@
     return terms[:half] + terms[half:]
 
 
+def marked(at, index):
+    same = at.astype(jnp.int16) == jnp.broadcast_to(index, at.shape).astype(jnp.int16)
+    return jnp.where(same, jnp.ones(at.shape, bf16), jnp.zeros(at.shape, bf16))
+
+
 def one_hot(rows, index):
-    at = lax.broadcasted_iota(jnp.int32, (rows, index.shape[1]), 0)
-    return jnp.where(at == index, 1.0, 0.0).astype(bf16)
+    return marked(lax.broadcasted_iota(jnp.int32, (rows, index.shape[1]), 0), index)
 
 
 def column(row):
@@ -191,7 +195,7 @@
 def one_hot_across(index, first, count):
     lane = lax.broadcasted_iota(jnp.int32, index.shape, 1)
     tiles = [
-        jnp.where(lane + (first + tile * LANES) == index, 1.0, 0.0).astype(bf16)
+        marked(lane, index - (first + tile * LANES))
         for tile in range(count // LANES)
     ]
     return jnp.concatenate(tiles, axis=1)

time: 36.9 us -> 36.8 us (level)
  no operation moved by 1% of the time
where the time goes in v11:
time: 36.8 us; the launch traced here: 36.5 us
  blocking collectives  26.9 us (73%)
  Pallas kernels  7.63 us (21%)
  starting transfers between devices  1.11 us (3%)
  between operations  0.8 us (2%)
    all_to_all x2, blocking collectives, transpose_all(): pieces = lax.all_to_all(pieces, 'bin', split_axis=0, concat_axis=0)  26.9 us
    pallas_call x7, Pallas kernels, call(): pl.pallas_call(kernel, out_shape=shapes[0] if single else shapes, in_spec...  7.63 us
    ppermute x3, starting transfers between devices, swap(): return lax.ppermute(array, 'nest', [(0, 1), (1, 0)])  1.11 us
  transfers between devices with their start and end apart: 3, of which 0 were waited for; matrix products, arithmetic and copies ran while one was open for 0% of the time, Pallas kernels for 6%

profile of v11, /device:TPU:0, one launch (start us, length us, event | category | flops | bytes accessed | tf_op | source)
XLA Modules:
  0.0 36.5 jit_solution(10853928027582306662)
XLA Ops:
  0.0 0.0 copy-start.2
  0.0 0.0 copy-start.7
  0.0 0.0 copy-start.6
  0.0 0.0 copy-start.4
  0.0 0.0 copy-start.3
  0.0 0.5 %collective-permute-start = (f32[72,1024]{1,0:T(8,128)}, f32[72,1024]{1,0:T(8,128)S(1)}, u32[]{:S(2)}, u32[]{:S(2)}) collective-permute-start(f32[72,1024]{1,0:T(8,128)} %bitcast.13), channel_id=1, source_target_pairs={{0,16},{16,0},{1,17},{17,1},{2,18},{18,2},{3,19},{19,3},{4,20},{20... | collective-permute-start | bytes 884744 | tf_op jit(solution)/shard_map/ppermute | solution.py:623
  0.5 0.1 collective-permute-start.1
  1.3 0.1 shard_map.110.steps
  1.4 0.0 copy-start.8
  1.4 0.0 copy-start.9
  1.4 0.0 copy-start
  1.4 0.0 copy-start.1
  1.4 0.0 copy-done.2
  1.4 0.0 copy-done.7
  1.4 0.0 copy-done.6
  1.4 0.0 copy-done.4
  1.4 0.0 copy-done.3
  1.4 1.3 %shard_map.109 = (s32[4,1,256]{2,1,0:T(1,128)S(1)}, s32[4,1,256]{2,1,0:T(1,128)S(1)}, f32[4,72,256]{2,1,0:T(8,128)S(1)}, bf16[4,256,256]{2,1,0:T(8,128)(2,1)S(1)...) custom-call(f32[72,1024]{1,0:T(8,128)S(1)} %bitcast.14, s32[4,1024]{1,0:T(4,128)S(1)} %bitcast.15, ...), custom_call_target="tpu_custom_call" | custom-call | flops 1000000000 | bytes 1155072 | tf_op jit(solution)/shard_map/pallas_call | solution.py:578
  2.7 0.0 copy-done.8
  2.7 0.0 copy-start.5
  2.7 0.0 copy-done.9
  2.7 0.0 collective-permute-done.1.send_b
  2.8 0.0 collective-permute-done.spectra_b
  2.8 0.0 copy-done
  2.8 1.0 %shard_map.111 = (f32[4,72,256]{2,1,0:T(8,128)S(1)}, f32[72,256]{1,0:T(8,128)S(1)}, f32[13,72,256]{2,1,0:T(8,128)S(1)}) custom-call(f32[4,72,256]{2,1,0:T(8,128)S(1)} %get-tuple-element.22.base, bf16[4,256,256]{2,1,0:T(8,128)(2,1)S(1)} %get-tuple-element.23.into, f32[4,1,256]{2,1,0:T(1,128)S(1)} %get-tuple-element.24.sea, ...), custom_call_target="tpu_custom_call" | custom-call | flops 100000000 | bytes 2457152 | tf_op jit(solution)/shard_map/pallas_call | solution.py:578
  3.8 0.5 %collective-permute-start.2 = (f32[72,256]{1,0:T(8,128)S(1)}, f32[72,256]{1,0:T(8,128)S(1)}, u32[]{:S(2)}, u32[]{:S(2)}) collective-permute-start(f32[72,256]{1,0:T(8,128)S(1)} %get-tuple-element.27), channel_id=1, source_target_pairs={{0,16},{16,0},{1,17},{17,1},{2,18},{18,2},{3,19},{19,3},{4,20},{20... | collective-permute-start | bytes 221192 | tf_op jit(solution)/shard_map/ppermute | solution.py:623
  4.3 0.0 copy-done.1
  4.3 0.9 %shard_map.112 = (f32[4,1,256]{2,1,0:T(1,128)S(1)}, bf16[4,256,512]{2,1,0:T(8,128)(2,1)S(1)}, s32[1,1024]{1,0:T(1,128)S(1)}, bf16[1152,1152]{1,0:T(8,128)(2,1)S(1)}, f32[2,1152]{1,0:T(2,128)S(1)}) custom-call(s32[4,1,256]{2,1,0:T(1,128)S(1)} %get-tuple-element.30.rank, f32[4,1,256]{2,1,0:T(1,128)S(1)} %get-tuple-element.24.sea, ...), custom_call_target="tpu_custom_call" | custom-call | flops 1000000000 | bytes 6391808 | tf_op jit(solution)/shard_map/pallas_call | solution.py:578
  5.2 0.0 collective-permute-done.2.incoming
  5.3 0.0 copy-done.5
  5.3 0.9 %shard_map.113 = (f32[288,128]{1,0:T(8,128)S(1)}, f32[8,512]{1,0:T(8,128)S(1)}) custom-call(f32[4,72,256]{2,1,0:T(8,128)S(1)} %get-tuple-element.26.field_in, f32[72,256]{1,0:T(8,128)S(1)} %collective-permute-done.2.incoming, bf16[4,256,256]{2,1,0:T(8,128)(2,1)S(1)} %get-tuple-element.23.into, s32[2,256]{1,0:T(2,128)S(1)} %get-tuple-element.25.lists, ...), custom_call_target="tpu_custom_call" | custom-call | flops 1000000000 | bytes 3086336 | tf_op jit(solution)/shard_map/pallas_call | solution.py:578
  6.2 16.0 %all_to_all.10 = f32[16,1,2304]{2,1,0:T(1,128)S(1)} all-to-all(f32[16,1,2304]{2,1,0:T(1,128)S(1)} %bitcast.10), channel_id=1, replica_groups=mesh['nest'=2,'bin'=16] {'bin'}, dimensions={0} | all-to-all | bytes 294912 | tf_op jit(solution)/shard_map/all_to_all | solution.py:619
  22.1 2.3 %shard_map.114 = f32[288,128]{1,0:T(8,128)S(1)} custom-call(f32[288,128]{1,0:T(8,128)S(1)} %bitcast.11, bf16[1152,1152]{1,0:T(8,128)(2,1)S(1)} %get-tuple-element.35.weights, f32[2,1152]{1,0:T(2,128)S(1)} %get-tuple-element.36.rates, f32[8,512]{1,0:T(8,128)S(1)} %get-tuple-element.37.blown), custom_call_target="tpu_custom_call" | custom-call | flops 1000000000 | bytes 2974720 | tf_op jit(solution)/shard_map/pallas_call | solution.py:578
  24.5 11.0 %all_to_all.11 = f32[16,1,2304]{2,1,0:T(1,128)S(1)} all-to-all(f32[16,1,2304]{2,1,0:T(1,128)S(1)} %bitcast.12), channel_id=1, replica_groups=mesh['nest'=2,'bin'=16] {'bin'}, dimensions={0} | all-to-all | bytes 294912 | tf_op jit(solution)/shard_map/all_to_all | solution.py:619
  35.5 1.1 %shard_map.115 = f32[72,1024]{1,0:T(8,128)} custom-call(f32[288,128]{1,0:T(8,128)S(1)} %bitcast.9, s32[1,1024]{1,0:T(1,128)S(1)} %get-tuple-element.38.place), custom_call_target="tpu_custom_call" | custom-call | flops 100000000 | bytes 446464 | tf_op jit(solution)/shard_map/pallas_call | solution.py:578
  (2 shorter events, 0.0 us)
Async XLA Ops:
  0.0 1.4 %copy-start.2 = (f32[1,72,1024]{2,1,0:T(8,128)S(1)}, f32[1,72,1024]{2,1,0:T(8,128)}, u32[]{:S(2)}) copy-start(f32[1,72,1024]{2,1,0:T(8,128)} %param.11) | copy-start | bytes 884740
  0.0 1.4 %copy-start.7 = (s32[1,256]{1,0:T(1,128)S(1)}, s32[1,256]{1,0:T(1,128)}, u32[]{:S(2)}) copy-start(s32[1,256]{1,0:T(1,128)} %send.1) | copy-start | bytes 3076
  0.0 1.4 %copy-start.6 = (s32[1,256]{1,0:T(1,128)S(1)}, s32[1,256]{1,0:T(1,128)}, u32[]{:S(2)}) copy-start(s32[1,256]{1,0:T(1,128)} %recv.1) | copy-start | bytes 3076
  0.0 1.4 %copy-start.4 = (s32[1,1024]{1,0:T(1,128)S(1)}, s32[1,1024]{1,0:T(1,128)}, u32[]{:S(2)}) copy-start(s32[1,1024]{1,0:T(1,128)} %wet.1) | copy-start | bytes 12292
  0.0 1.4 %copy-start.3 = (s32[1,4,1024]{2,1,0:T(4,128)S(1)}, s32[1,4,1024]{2,1,0:T(4,128)}, u32[]{:S(2)}) copy-start(s32[1,4,1024]{2,1,0:T(4,128)} %param.17) | copy-start | bytes 49156
  0.0 2.7 %collective-permute-start = (f32[72,1024]{1,0:T(8,128)}, f32[72,1024]{1,0:T(8,128)S(1)}, u32[]{:S(2)}, u32[]{:S(2)}) collective-permute-start(f32[72,1024]{1,0:T(8,128)} %bitcast.13), channel_id=1, source_target_pairs={{0,16},{16,0},{1,17},{17,1},{2,18},{18,2},{3,19},{19,3},{4,20},{20... | collective-permute-start | bytes 884744 | tf_op jit(solution)/shard_map/ppermute | solution.py:623
  0.5 2.2 %collective-permute-start.1 = (s32[1,256]{1,0:T(1,128)}, s32[1,256]{1,0:T(1,128)S(1)}, u32[]{:S(2)}, u32[]{:S(2)}) collective-permute-start(s32[1,256]{1,0:T(1,128)} %send.1), channel_id=1, source_target_pairs={{0,16},{16,0},{1,17},{17,1},{2,18},{18,2},{3,19},{19,3},{4,20},{20... | collective-permute-start | bytes 3080 | tf_op jit(solution)/shard_map/ppermute | solution.py:623
  1.4 1.3 %copy-start.8 = (f32[1152]{0:T(1024)S(1)}, f32[1152]{0:T(1024)}, u32[]{:S(2)}) copy-start(f32[1152]{0:T(1024)} %param.14) | copy-start | bytes 13828
  1.4 1.4 %copy-start.9 = (f32[1152]{0:T(1024)S(1)}, f32[1152]{0:T(1024)}, u32[]{:S(2)}) copy-start(f32[1152]{0:T(1024)} %param.15) | copy-start | bytes 13828
  1.4 1.4 %copy-start = (f32[2,72]{1,0:T(2,128)S(1)}, f32[2,72]{1,0:T(2,128)}, u32[]{:S(2)}) copy-start(f32[2,72]{1,0:T(2,128)} %courant.1) | copy-start | bytes 1732
  1.4 3.0 %copy-start.1 = (bf16[1152,1152]{1,0:T(8,128)(2,1)S(1)}, bf16[1152,1152]{1,0:T(8,128)(2,1)}, u32[]{:S(2)}) copy-start(bf16[1152,1152]{1,0:T(8,128)(2,1)} %coupling.1) | copy-start | bytes 7962628
  2.7 2.6 %copy-start.5 = (f32[1,1024]{1,0:T(1,128)S(1)}, f32[1,1024]{1,0:T(1,128)}, u32[]{:S(2)}) copy-start(f32[1,1024]{1,0:T(1,128)} %wind.1) | copy-start | bytes 12292
  3.8 1.4 %collective-permute-start.2 = (f32[72,256]{1,0:T(8,128)S(1)}, f32[72,256]{1,0:T(8,128)S(1)}, u32[]{:S(2)}, u32[]{:S(2)}) collective-permute-start(f32[72,256]{1,0:T(8,128)S(1)} %get-tuple-element.27), channel_id=1, source_target_pairs={{0,16},{16,0},{1,17},{17,1},{2,18},{18,2},{3,19},{19,3},{4,20},{20... | collective-permute-start | bytes 221192 | tf_op jit(solution)/shard_map/ppermute | solution.py:623

commit v12 on v11

--- a/solution.py
+++ b/solution.py
@@ -126,19 +126,32 @@
     point = (at % count) * LANES + lane
     column_at = lane * count + at % count
 
-    first = tables[0:1, 0:cols_count]
-    ahead = jnp.where(at < count, rows_stacked(tiles_of(first)), 0)
-    behind = rows_stacked(tiles_of(tables[1:2, 0:cols_count]))
-    behind = jnp.where(point == 0, 0, behind)
-    steps = jnp.where(point == 0, 0, 1)
-    for bit in range(bits):
-        far = taken_from([ahead[k : k + 1] for k in range(count)], ahead)
-        both = (steps << bits) + behind
-        back = taken_from([both[k : k + 1] for k in range(count)], behind)
-        ahead = jnp.where((at >= count) & ((column_at >> bit) & 1 == 0), ahead, far)
-        steps = steps + (back >> bits)
-        behind = back & ((1 << bits) - 1)
-    order[0] = jnp.concatenate([ahead[count + k : count + k + 1] for k in range(count)], axis=1)
+    def doubled(pointers, near):
+        for bit in range(bits - 1):
+            far = taken_from([pointers[k : k + 1] for k in range(count)], pointers)
+            pointers = jnp.where((at >= count) & ((near >> bit) & 1 == 0), pointers, far)
+        return [pointers[count + k : count + k + 1] for k in range(count)]
+
+    def stopped(pointers):
+        pointers = jnp.where(point == 0, 0, pointers)
+        steps = jnp.where(point == 0, 0, 1)
+        for bit in range(bits - 1):
+            both = (steps << bits) + pointers
+            back = taken_from([both[k : k + 1] for k in range(count)], pointers)
+            steps = steps + (back >> bits)
+            pointers = back & ((1 << bits) - 1)
+        return steps, pointers == 0
+
+    east, west = (rows_stacked(tiles_of(tables[k : k + 1, 0:cols_count])) for k in range(2))
+    last = jnp.broadcast_to(tables[1:2, 0:1], (SUBLANES, LANES))
+    onward = doubled(jnp.where(at < count, east, 0), column_at)
+    backward = doubled(jnp.where(at < count, west, last), cols_count - 1 - column_at)
+    near = column_at < 1 << (bits - 1)
+    found = [jnp.where(near[k : k + 1], onward[k], backward[k]) for k in range(count)]
+    order[0] = jnp.concatenate(found, axis=1)
+    by_west, reached = stopped(west)
+    by_east, _ = stopped(east)
+    steps = jnp.where(reached, by_west, cols_count - by_east)
     steps = steps % count * LANES + steps // count
     rank[0] = jnp.concatenate([steps[k : k + 1] for k in range(count)], axis=1)
 

time: 36.8 us -> 36.7 us (level)
  no operation moved by 1% of the time
where the time goes in v12:
time: 36.7 us; the launch traced here: 36.5 us
  blocking collectives  26.9 us (73%)
  Pallas kernels  7.6 us (21%)
  starting transfers between devices  1.11 us (3%)
  between operations  0.8 us (2%)
    all_to_all x2, blocking collectives, transpose_all(): pieces = lax.all_to_all(pieces, 'bin', split_axis=0, concat_axis=0)  26.9 us
    pallas_call x7, Pallas kernels, call(): pl.pallas_call(kernel, out_shape=shapes[0] if single else shapes, in_spec...  7.6 us
    ppermute x3, starting transfers between devices, swap(): return lax.ppermute(array, 'nest', [(0, 1), (1, 0)])  1.11 us
  transfers between devices with their start and end apart: 3, of which 0 were waited for; matrix products, arithmetic and copies ran while one was open for 0% of the time, Pallas kernels for 6%

profile of v12, /device:TPU:0, one launch (start us, length us, event | category | flops | bytes accessed | tf_op | source)
XLA Modules:
  0.0 36.5 jit_solution(4407759609774298813)
XLA Ops:
  0.0 0.0 copy-start.2
  0.0 0.0 copy-start.7
  0.0 0.0 copy-start.6
  0.0 0.0 copy-start.4
  0.0 0.0 copy-start.3
  0.0 0.5 %collective-permute-start = (f32[72,1024]{1,0:T(8,128)}, f32[72,1024]{1,0:T(8,128)S(1)}, u32[]{:S(2)}, u32[]{:S(2)}) collective-permute-start(f32[72,1024]{1,0:T(8,128)} %bitcast.13), channel_id=1, source_target_pairs={{0,16},{16,0},{1,17},{17,1},{2,18},{18,2},{3,19},{19,3},{4,20},{20... | collective-permute-start | bytes 884744 | tf_op jit(solution)/shard_map/ppermute | solution.py:636
  0.5 0.1 collective-permute-start.1
  1.3 0.1 shard_map.110.steps
  1.4 0.0 copy-start.8
  1.4 0.0 copy-start.9
  1.4 0.0 copy-start
  1.4 0.0 copy-start.1
  1.4 0.0 copy-done.2
  1.4 0.0 copy-done.7
  1.4 0.0 copy-done.6
  1.4 0.0 copy-done.4
  1.4 0.0 copy-done.3
  1.4 1.2 %shard_map.109 = (s32[4,1,256]{2,1,0:T(1,128)S(1)}, s32[4,1,256]{2,1,0:T(1,128)S(1)}, f32[4,72,256]{2,1,0:T(8,128)S(1)}, bf16[4,256,256]{2,1,0:T(8,128)(2,1)S(1)...) custom-call(f32[72,1024]{1,0:T(8,128)S(1)} %bitcast.14, s32[4,1024]{1,0:T(4,128)S(1)} %bitcast.15, ...), custom_call_target="tpu_custom_call" | custom-call | flops 1000000000 | bytes 1155072 | tf_op jit(solution)/shard_map/pallas_call | solution.py:591
  2.6 0.0 copy-done.8
  2.7 0.0 copy-start.5
  2.7 0.0 copy-done.9
  2.7 0.0 collective-permute-done.1.send_b
  2.7 0.0 collective-permute-done.spectra_b
  2.7 0.0 copy-done
  2.7 1.0 %shard_map.111 = (f32[4,72,256]{2,1,0:T(8,128)S(1)}, f32[72,256]{1,0:T(8,128)S(1)}, f32[13,72,256]{2,1,0:T(8,128)S(1)}) custom-call(f32[4,72,256]{2,1,0:T(8,128)S(1)} %get-tuple-element.22.base, bf16[4,256,256]{2,1,0:T(8,128)(2,1)S(1)} %get-tuple-element.23.into, f32[4,1,256]{2,1,0:T(1,128)S(1)} %get-tuple-element.24.sea, ...), custom_call_target="tpu_custom_call" | custom-call | flops 100000000 | bytes 2457152 | tf_op jit(solution)/shard_map/pallas_call | solution.py:591
  3.8 0.5 %collective-permute-start.2 = (f32[72,256]{1,0:T(8,128)S(1)}, f32[72,256]{1,0:T(8,128)S(1)}, u32[]{:S(2)}, u32[]{:S(2)}) collective-permute-start(f32[72,256]{1,0:T(8,128)S(1)} %get-tuple-element.27), channel_id=1, source_target_pairs={{0,16},{16,0},{1,17},{17,1},{2,18},{18,2},{3,19},{19,3},{4,20},{20... | collective-permute-start | bytes 221192 | tf_op jit(solution)/shard_map/ppermute | solution.py:636
  4.3 0.0 copy-done.1
  4.3 0.9 %shard_map.112 = (f32[4,1,256]{2,1,0:T(1,128)S(1)}, bf16[4,256,512]{2,1,0:T(8,128)(2,1)S(1)}, s32[1,1024]{1,0:T(1,128)S(1)}, bf16[1152,1152]{1,0:T(8,128)(2,1)S(1)}, f32[2,1152]{1,0:T(2,128)S(1)}) custom-call(s32[4,1,256]{2,1,0:T(1,128)S(1)} %get-tuple-element.30.rank, f32[4,1,256]{2,1,0:T(1,128)S(1)} %get-tuple-element.24.sea, ...), custom_call_target="tpu_custom_call" | custom-call | flops 1000000000 | bytes 6391808 | tf_op jit(solution)/shard_map/pallas_call | solution.py:591
  5.2 0.0 collective-permute-done.2.incoming
  5.2 0.0 copy-done.5
  5.2 0.9 %shard_map.113 = (f32[288,128]{1,0:T(8,128)S(1)}, f32[8,512]{1,0:T(8,128)S(1)}) custom-call(f32[4,72,256]{2,1,0:T(8,128)S(1)} %get-tuple-element.26.field_in, f32[72,256]{1,0:T(8,128)S(1)} %collective-permute-done.2.incoming, bf16[4,256,256]{2,1,0:T(8,128)(2,1)S(1)} %get-tuple-element.23.into, s32[2,256]{1,0:T(2,128)S(1)} %get-tuple-element.25.lists, ...), custom_call_target="tpu_custom_call" | custom-call | flops 1000000000 | bytes 3086336 | tf_op jit(solution)/shard_map/pallas_call | solution.py:591
  6.1 16.0 %all_to_all.10 = f32[16,1,2304]{2,1,0:T(1,128)S(1)} all-to-all(f32[16,1,2304]{2,1,0:T(1,128)S(1)} %bitcast.10), channel_id=1, replica_groups=mesh['nest'=2,'bin'=16] {'bin'}, dimensions={0} | all-to-all | bytes 294912 | tf_op jit(solution)/shard_map/all_to_all | solution.py:632
  22.1 2.3 %shard_map.114 = f32[288,128]{1,0:T(8,128)S(1)} custom-call(f32[288,128]{1,0:T(8,128)S(1)} %bitcast.11, bf16[1152,1152]{1,0:T(8,128)(2,1)S(1)} %get-tuple-element.35.weights, f32[2,1152]{1,0:T(2,128)S(1)} %get-tuple-element.36.rates, f32[8,512]{1,0:T(8,128)S(1)} %get-tuple-element.37.blown), custom_call_target="tpu_custom_call" | custom-call | flops 1000000000 | bytes 2974720 | tf_op jit(solution)/shard_map/pallas_call | solution.py:591
  24.4 11.0 %all_to_all.11 = f32[16,1,2304]{2,1,0:T(1,128)S(1)} all-to-all(f32[16,1,2304]{2,1,0:T(1,128)S(1)} %bitcast.12), channel_id=1, replica_groups=mesh['nest'=2,'bin'=16] {'bin'}, dimensions={0} | all-to-all | bytes 294912 | tf_op jit(solution)/shard_map/all_to_all | solution.py:632
  35.4 1.1 %shard_map.115 = f32[72,1024]{1,0:T(8,128)} custom-call(f32[288,128]{1,0:T(8,128)S(1)} %bitcast.9, s32[1,1024]{1,0:T(1,128)S(1)} %get-tuple-element.38.place), custom_call_target="tpu_custom_call" | custom-call | flops 100000000 | bytes 446464 | tf_op jit(solution)/shard_map/pallas_call | solution.py:591
  (2 shorter events, 0.0 us)
Async XLA Ops:
  0.0 1.4 %copy-start.2 = (f32[1,72,1024]{2,1,0:T(8,128)S(1)}, f32[1,72,1024]{2,1,0:T(8,128)}, u32[]{:S(2)}) copy-start(f32[1,72,1024]{2,1,0:T(8,128)} %param.11) | copy-start | bytes 884740
  0.0 1.4 %copy-start.7 = (s32[1,256]{1,0:T(1,128)S(1)}, s32[1,256]{1,0:T(1,128)}, u32[]{:S(2)}) copy-start(s32[1,256]{1,0:T(1,128)} %send.1) | copy-start | bytes 3076
  0.0 1.4 %copy-start.6 = (s32[1,256]{1,0:T(1,128)S(1)}, s32[1,256]{1,0:T(1,128)}, u32[]{:S(2)}) copy-start(s32[1,256]{1,0:T(1,128)} %recv.1) | copy-start | bytes 3076
  0.0 1.4 %copy-start.4 = (s32[1,1024]{1,0:T(1,128)S(1)}, s32[1,1024]{1,0:T(1,128)}, u32[]{:S(2)}) copy-start(s32[1,1024]{1,0:T(1,128)} %wet.1) | copy-start | bytes 12292
  0.0 1.4 %copy-start.3 = (s32[1,4,1024]{2,1,0:T(4,128)S(1)}, s32[1,4,1024]{2,1,0:T(4,128)}, u32[]{:S(2)}) copy-start(s32[1,4,1024]{2,1,0:T(4,128)} %param.17) | copy-start | bytes 49156
  0.0 2.7 %collective-permute-start = (f32[72,1024]{1,0:T(8,128)}, f32[72,1024]{1,0:T(8,128)S(1)}, u32[]{:S(2)}, u32[]{:S(2)}) collective-permute-start(f32[72,1024]{1,0:T(8,128)} %bitcast.13), channel_id=1, source_target_pairs={{0,16},{16,0},{1,17},{17,1},{2,18},{18,2},{3,19},{19,3},{4,20},{20... | collective-permute-start | bytes 884744 | tf_op jit(solution)/shard_map/ppermute | solution.py:636
  0.5 2.2 %collective-permute-start.1 = (s32[1,256]{1,0:T(1,128)}, s32[1,256]{1,0:T(1,128)S(1)}, u32[]{:S(2)}, u32[]{:S(2)}) collective-permute-start(s32[1,256]{1,0:T(1,128)} %send.1), channel_id=1, source_target_pairs={{0,16},{16,0},{1,17},{17,1},{2,18},{18,2},{3,19},{19,3},{4,20},{20... | collective-permute-start | bytes 3080 | tf_op jit(solution)/shard_map/ppermute | solution.py:636
  1.4 1.3 %copy-start.8 = (f32[1152]{0:T(1024)S(1)}, f32[1152]{0:T(1024)}, u32[]{:S(2)}) copy-start(f32[1152]{0:T(1024)} %param.14) | copy-start | bytes 13828
  1.4 1.3 %copy-start.9 = (f32[1152]{0:T(1024)S(1)}, f32[1152]{0:T(1024)}, u32[]{:S(2)}) copy-start(f32[1152]{0:T(1024)} %param.15) | copy-start | bytes 13828
  1.4 1.4 %copy-start = (f32[2,72]{1,0:T(2,128)S(1)}, f32[2,72]{1,0:T(2,128)}, u32[]{:S(2)}) copy-start(f32[2,72]{1,0:T(2,128)} %courant.1) | copy-start | bytes 1732
  1.4 2.9 %copy-start.1 = (bf16[1152,1152]{1,0:T(8,128)(2,1)S(1)}, bf16[1152,1152]{1,0:T(8,128)(2,1)}, u32[]{:S(2)}) copy-start(bf16[1152,1152]{1,0:T(8,128)(2,1)} %coupling.1) | copy-start | bytes 7962628
  2.7 2.6 %copy-start.5 = (f32[1,1024]{1,0:T(1,128)S(1)}, f32[1,1024]{1,0:T(1,128)}, u32[]{:S(2)}) copy-start(f32[1,1024]{1,0:T(1,128)} %wind.1) | copy-start | bytes 12292
  3.8 1.4 %collective-permute-start.2 = (f32[72,256]{1,0:T(8,128)S(1)}, f32[72,256]{1,0:T(8,128)S(1)}, u32[]{:S(2)}, u32[]{:S(2)}) collective-permute-start(f32[72,256]{1,0:T(8,128)S(1)} %get-tuple-element.27), channel_id=1, source_target_pairs={{0,16},{16,0},{1,17},{17,1},{2,18},{18,2},{3,19},{19,3},{4,20},{20... | collective-permute-start | bytes 221192 | tf_op jit(solution)/shard_map/ppermute | solution.py:636

commit v13 on v12

--- a/solution.py
+++ b/solution.py
@@ -390,7 +390,9 @@
     return one_hot_across(down(ranks[row] - 1.0), 0, sea_count)
 
 
-def places_kernel(rank, sea, coupling, growth, dissipation, ranks, picks, place, weights, rates):
+def places_kernel(
+    rank, order, wind, sea, coupling, growth, dissipation, ranks, picks, place, winds, weights, rates
+):
     rows_count, _, cols_count = rank.shape
     sea_count = picks.shape[2]
     at = lax.broadcasted_iota(jnp.int32, (cols_count, cols_count), 0)
@@ -402,6 +404,7 @@
         number_of = dot(eight(here).astype(bf16), upper)[0:1] + before
         number_of = jnp.where(here > 0.0, number_of, 0.0)
         ranks[row] = number_of
+        winds[row] = look_up(wind[0:1, span(row, cols_count)], order[row])
         if picks.shape[0] == rows_count:
             picks[row] = one_hot_across(down(number_of - 1.0), 0, sea_count)
         place[0:1, span(row, cols_count)] = look_up(number_of.astype(jnp.int32), rank[row])
@@ -413,7 +416,7 @@
             before = number(row, before)
     else:
         lax.fori_loop(0, rows_count, number, before)
-    turned = min(2, weights.shape[0] // cols_count) * cols_count
+    turned = min(3, weights.shape[0] // cols_count) * cols_count
     unit = jnp.where(at == across, 1.0, 0.0).astype(bf16)
     for first in range(0, turned, cols_count):
         here = slice(first, first + cols_count)
@@ -434,8 +437,7 @@
     rates,
     ranks,
     picks,
-    order,
-    wind,
+    winds,
     pieces,
     blown,
     field,
@@ -456,8 +458,7 @@
     advance(field, moved, faces, sea, coefs_of(rates, 2), coefs_of(rates, 3))
 
     def at_sea(row):
-        by_grid = look_up(wind[0:1, span(row, cols_count)], order[row])
-        terms = jnp.concatenate([split(field[row]), split(eight(by_grid))], axis=0)
+        terms = jnp.concatenate([split(field[row]), split(eight(winds[row]))], axis=0)
         return dot(terms, picked(row, ranks, picks, sea_count))
 
     total = total_of(rows_count, (2 * bins + 2 * SUBLANES, sea_count), at_sea)
@@ -673,17 +674,18 @@
     )
     incoming = swap(outgoing)
     kept = rows_count if points * sea_count <= 1 << 22 else 1
-    ranks, picks, place, weights, source_rates = call(
+    ranks, picks, place, winds, weights, source_rates = call(
         places_kernel,
         [
             (row_of, f32),
             ((kept, cols_count, sea_count), bf16),
             ((1, points), jnp.int32),
+            (row_of, f32),
             ((size, size), bf16),
             ((2, size), f32),
         ],
         [],
-        (rank, sea, coupling, growth.reshape(1, size), dissipation.reshape(1, size)),
+        (rank, order, wind, sea, coupling, growth.reshape(1, size), dissipation.reshape(1, size)),
         10**9,
     )
     tiles = sea_count // LANES
@@ -691,7 +693,7 @@
         functools.partial(second_kernel, share),
         [((devices * block, LANES), f32), ((SUBLANES, sea_count), f32)],
         [*[pltpu.VMEM(grid, f32)] * 3, pltpu.VMEM((tiles, bins, LANES), f32)],
-        (field, incoming, into, lists, taken, sea, rates, ranks, picks, order, wind),
+        (field, incoming, into, lists, taken, sea, rates, ranks, picks, winds),
         10**9,
     )
     pieces = transpose_all(pieces)

time: 36.7 us -> 36.7 us (level)
  transfers between devices with their start and end apart: 3 -> 3, of which waited for: 0 -> 1; matrix products, arithmetic and copies ran while one was open for 0% -> 0% of each run, Pallas kernels for 6% -> 6%
where the time goes in v13:
time: 36.7 us; the launch traced here: 36.5 us
  blocking collectives  26.9 us (73%)
  Pallas kernels  7.48 us (20%)
  starting transfers between devices  1.11 us (3%)
  between operations  0.79 us (2%)
    all_to_all x2, blocking collectives, transpose_all(): pieces = lax.all_to_all(pieces, 'bin', split_axis=0, concat_axis=0)  26.9 us
    pallas_call x7, Pallas kernels, call(): pl.pallas_call(kernel, out_shape=shapes[0] if single else shapes, in_spec...  7.48 us
    ppermute x3, starting transfers between devices, swap(): return lax.ppermute(array, 'nest', [(0, 1), (1, 0)])  1.11 us
  transfers between devices with their start and end apart: 3, of which 1 were waited for; matrix products, arithmetic and copies ran while one was open for 0% of the time, Pallas kernels for 6%

profile of v13, /device:TPU:0, one launch (start us, length us, event | category | flops | bytes accessed | tf_op | source)
XLA Modules:
  0.0 36.5 jit_solution(17675593235097297745)
XLA Ops:
  0.0 0.0 copy-start.2
  0.0 0.0 copy-start.7
  0.0 0.0 copy-start.6
  0.0 0.0 copy-start.4
  0.0 0.0 copy-start.3
  0.0 0.5 %collective-permute-start = (f32[72,1024]{1,0:T(8,128)}, f32[72,1024]{1,0:T(8,128)S(1)}, u32[]{:S(2)}, u32[]{:S(2)}) collective-permute-start(f32[72,1024]{1,0:T(8,128)} %bitcast.13), channel_id=1, source_target_pairs={{0,16},{16,0},{1,17},{17,1},{2,18},{18,2},{3,19},{19,3},{4,20},{20... | collective-permute-start | bytes 884744 | tf_op jit(solution)/shard_map/ppermute | solution.py:637
  0.5 0.1 collective-permute-start.1
  1.3 0.1 shard_map.110.steps
  1.4 0.0 copy-start.8
  1.4 0.0 copy-start.9
  1.4 0.0 copy-start
  1.4 0.0 copy-start.1
  1.4 0.0 copy-start.5
  1.4 0.0 copy-done.2
  1.4 0.0 copy-done.7
  1.4 0.0 copy-done.6
  1.4 0.0 copy-done.4
  1.4 0.0 copy-done.3
  1.4 1.2 %shard_map.109 = (s32[4,1,256]{2,1,0:T(1,128)S(1)}, s32[4,1,256]{2,1,0:T(1,128)S(1)}, f32[4,72,256]{2,1,0:T(8,128)S(1)}, bf16[4,256,256]{2,1,0:T(8,128)(2,1)S(1)...) custom-call(f32[72,1024]{1,0:T(8,128)S(1)} %bitcast.14, s32[4,1024]{1,0:T(4,128)S(1)} %bitcast.15, ...), custom_call_target="tpu_custom_call" | custom-call | flops 1000000000 | bytes 1155072 | tf_op jit(solution)/shard_map/pallas_call | solution.py:592
  2.7 0.0 copy-done.8
  2.7 0.0 copy-done.9
  2.7 0.0 collective-permute-done.1.send_b
  2.7 0.0 collective-permute-done.spectra_b
  2.7 0.0 copy-done
  2.7 1.0 %shard_map.111 = (f32[4,72,256]{2,1,0:T(8,128)S(1)}, f32[72,256]{1,0:T(8,128)S(1)}, f32[13,72,256]{2,1,0:T(8,128)S(1)}) custom-call(f32[4,72,256]{2,1,0:T(8,128)S(1)} %get-tuple-element.23.base, bf16[4,256,256]{2,1,0:T(8,128)(2,1)S(1)} %get-tuple-element.24.into, f32[4,1,256]{2,1,0:T(1,128)S(1)} %get-tuple-element.25.sea, ...), custom_call_target="tpu_custom_call" | custom-call | flops 100000000 | bytes 2457152 | tf_op jit(solution)/shard_map/pallas_call | solution.py:592
  3.8 0.5 %collective-permute-start.2 = (f32[72,256]{1,0:T(8,128)S(1)}, f32[72,256]{1,0:T(8,128)S(1)}, u32[]{:S(2)}, u32[]{:S(2)}) collective-permute-start(f32[72,256]{1,0:T(8,128)S(1)} %get-tuple-element.28), channel_id=1, source_target_pairs={{0,16},{16,0},{1,17},{17,1},{2,18},{18,2},{3,19},{19,3},{4,20},{20... | collective-permute-start | bytes 221192 | tf_op jit(solution)/shard_map/ppermute | solution.py:637
  4.3 0.0 copy-done.1
  4.3 0.0 copy-done.5
  4.3 0.8 %shard_map.112 = (f32[4,1,256]{2,1,0:T(1,128)S(1)}, bf16[4,256,512]{2,1,0:T(8,128)(2,1)S(1)}, s32[1,1024]{1,0:T(1,128)S(1)}, f32[4,1,256]{2,1,0:T(1,128)S(1)}, b...) custom-call(s32[4,1,256]{2,1,0:T(1,128)S(1)} %get-tuple-element.31.rank, s32[4,1,256]{2,1,0:T(1,128)S(1)} %get-tuple-element.32.order, ...), custom_call_target="tpu_custom_call" | custom-call | flops 1000000000 | bytes 6404096 | tf_op jit(solution)/shard_map/pallas_call | solution.py:592
  5.1 0.1 collective-permute-done.2.incoming
  5.2 0.9 %shard_map.113 = (f32[288,128]{1,0:T(8,128)S(1)}, f32[8,512]{1,0:T(8,128)S(1)}) custom-call(f32[4,72,256]{2,1,0:T(8,128)S(1)} %get-tuple-element.27.field_in, f32[72,256]{1,0:T(8,128)S(1)} %collective-permute-done.2.incoming, bf16[4,256,256]{2,1,0:T(8,128)(2,1)S(1)} %get-tuple-element.24.into, s32[2,256]{1,0:T(2,128)S(1)} %get-tuple-element.26.lists, ...), custom_call_target="tpu_custom_call" | custom-call | flops 1000000000 | bytes 3082240 | tf_op jit(solution)/shard_map/pallas_call | solution.py:592
  6.1 16.0 %all_to_all.10 = f32[16,1,2304]{2,1,0:T(1,128)S(1)} all-to-all(f32[16,1,2304]{2,1,0:T(1,128)S(1)} %bitcast.10), channel_id=1, replica_groups=mesh['nest'=2,'bin'=16] {'bin'}, dimensions={0} | all-to-all | bytes 294912 | tf_op jit(solution)/shard_map/all_to_all | solution.py:633
  22.1 2.3 %shard_map.114 = f32[288,128]{1,0:T(8,128)S(1)} custom-call(f32[288,128]{1,0:T(8,128)S(1)} %bitcast.11, bf16[1152,1152]{1,0:T(8,128)(2,1)S(1)} %get-tuple-element.37.weights, f32[2,1152]{1,0:T(2,128)S(1)} %get-tuple-element.38.rates, f32[8,512]{1,0:T(8,128)S(1)} %get-tuple-element.39.blown), custom_call_target="tpu_custom_call" | custom-call | flops 1000000000 | bytes 2974720 | tf_op jit(solution)/shard_map/pallas_call | solution.py:592
  24.4 11.0 %all_to_all.11 = f32[16,1,2304]{2,1,0:T(1,128)S(1)} all-to-all(f32[16,1,2304]{2,1,0:T(1,128)S(1)} %bitcast.12), channel_id=1, replica_groups=mesh['nest'=2,'bin'=16] {'bin'}, dimensions={0} | all-to-all | bytes 294912 | tf_op jit(solution)/shard_map/all_to_all | solution.py:633
  35.4 1.1 %shard_map.115 = f32[72,1024]{1,0:T(8,128)} custom-call(f32[288,128]{1,0:T(8,128)S(1)} %bitcast.9, s32[1,1024]{1,0:T(1,128)S(1)} %get-tuple-element.40.place), custom_call_target="tpu_custom_call" | custom-call | flops 100000000 | bytes 446464 | tf_op jit(solution)/shard_map/pallas_call | solution.py:592
  (2 shorter events, 0.0 us)
Async XLA Ops:
  0.0 1.4 %copy-start.2 = (f32[1,72,1024]{2,1,0:T(8,128)S(1)}, f32[1,72,1024]{2,1,0:T(8,128)}, u32[]{:S(2)}) copy-start(f32[1,72,1024]{2,1,0:T(8,128)} %param.11) | copy-start | bytes 884740
  0.0 1.4 %copy-start.7 = (s32[1,256]{1,0:T(1,128)S(1)}, s32[1,256]{1,0:T(1,128)}, u32[]{:S(2)}) copy-start(s32[1,256]{1,0:T(1,128)} %send.1) | copy-start | bytes 3076
  0.0 1.4 %copy-start.6 = (s32[1,256]{1,0:T(1,128)S(1)}, s32[1,256]{1,0:T(1,128)}, u32[]{:S(2)}) copy-start(s32[1,256]{1,0:T(1,128)} %recv.1) | copy-start | bytes 3076
  0.0 1.4 %copy-start.4 = (s32[1,1024]{1,0:T(1,128)S(1)}, s32[1,1024]{1,0:T(1,128)}, u32[]{:S(2)}) copy-start(s32[1,1024]{1,0:T(1,128)} %wet.1) | copy-start | bytes 12292
  0.0 1.4 %copy-start.3 = (s32[1,4,1024]{2,1,0:T(4,128)S(1)}, s32[1,4,1024]{2,1,0:T(4,128)}, u32[]{:S(2)}) copy-start(s32[1,4,1024]{2,1,0:T(4,128)} %param.17) | copy-start | bytes 49156
  0.0 2.7 %collective-permute-start = (f32[72,1024]{1,0:T(8,128)}, f32[72,1024]{1,0:T(8,128)S(1)}, u32[]{:S(2)}, u32[]{:S(2)}) collective-permute-start(f32[72,1024]{1,0:T(8,128)} %bitcast.13), channel_id=1, source_target_pairs={{0,16},{16,0},{1,17},{17,1},{2,18},{18,2},{3,19},{19,3},{4,20},{20... | collective-permute-start | bytes 884744 | tf_op jit(solution)/shard_map/ppermute | solution.py:637
  0.5 2.2 %collective-permute-start.1 = (s32[1,256]{1,0:T(1,128)}, s32[1,256]{1,0:T(1,128)S(1)}, u32[]{:S(2)}, u32[]{:S(2)}) collective-permute-start(s32[1,256]{1,0:T(1,128)} %send.1), channel_id=1, source_target_pairs={{0,16},{16,0},{1,17},{17,1},{2,18},{18,2},{3,19},{19,3},{4,20},{20... | collective-permute-start | bytes 3080 | tf_op jit(solution)/shard_map/ppermute | solution.py:637
  1.4 1.3 %copy-start.8 = (f32[1152]{0:T(1024)S(1)}, f32[1152]{0:T(1024)}, u32[]{:S(2)}) copy-start(f32[1152]{0:T(1024)} %param.14) | copy-start | bytes 13828
  1.4 1.3 %copy-start.9 = (f32[1152]{0:T(1024)S(1)}, f32[1152]{0:T(1024)}, u32[]{:S(2)}) copy-start(f32[1152]{0:T(1024)} %param.15) | copy-start | bytes 13828
  1.4 1.4 %copy-start = (f32[2,72]{1,0:T(2,128)S(1)}, f32[2,72]{1,0:T(2,128)}, u32[]{:S(2)}) copy-start(f32[2,72]{1,0:T(2,128)} %courant.1) | copy-start | bytes 1732
  1.4 2.9 %copy-start.1 = (bf16[1152,1152]{1,0:T(8,128)(2,1)S(1)}, bf16[1152,1152]{1,0:T(8,128)(2,1)}, u32[]{:S(2)}) copy-start(bf16[1152,1152]{1,0:T(8,128)(2,1)} %coupling.1) | copy-start | bytes 7962628
  1.4 2.9 %copy-start.5 = (f32[1,1024]{1,0:T(1,128)S(1)}, f32[1,1024]{1,0:T(1,128)}, u32[]{:S(2)}) copy-start(f32[1,1024]{1,0:T(1,128)} %wind.1) | copy-start | bytes 12292
  3.8 1.4 %collective-permute-start.2 = (f32[72,256]{1,0:T(8,128)S(1)}, f32[72,256]{1,0:T(8,128)S(1)}, u32[]{:S(2)}, u32[]{:S(2)}) collective-permute-start(f32[72,256]{1,0:T(8,128)S(1)} %get-tuple-element.28), channel_id=1, source_target_pairs={{0,16},{16,0},{1,17},{17,1},{2,18},{18,2},{3,19},{19,3},{4,20},{20... | collective-permute-start | bytes 221192 | tf_op jit(solution)/shard_map/ppermute | solution.py:637

commit v14 on v12

--- a/solution.py
+++ b/solution.py
@@ -419,8 +419,8 @@
         here = slice(first, first + cols_count)
         weights[here] = dot_t(unit, coupling[:, here]).astype(bf16)
     weights[turned:] = jnp.transpose(coupling[:, turned:])
-    rates[0:1] = growth[...]
-    rates[1:2] = dissipation[...]
+    rates[0:1] = growth[...].reshape(1, growth.shape[0])
+    rates[1:2] = dissipation[...].reshape(1, growth.shape[0])
 
 
 def second_kernel(
@@ -683,7 +683,7 @@
             ((2, size), f32),
         ],
         [],
-        (rank, sea, coupling, growth.reshape(1, size), dissipation.reshape(1, size)),
+        (rank, sea, coupling, growth, dissipation),
         10**9,
     )
     tiles = sea_count // LANES

time: 36.7 us -> 36.7 us (level)
  no operation moved by 1% of the time
where the time goes in v14:
time: 36.7 us; the launch traced here: 36.5 us
  blocking collectives  26.9 us (73%)
  Pallas kernels  7.58 us (21%)
  starting transfers between devices  1.11 us (3%)
  between operations  0.77 us (2%)
    all_to_all x2, blocking collectives, transpose_all(): pieces = lax.all_to_all(pieces, 'bin', split_axis=0, concat_axis=0)  26.9 us
    pallas_call x7, Pallas kernels, call(): pl.pallas_call(kernel, out_shape=shapes[0] if single else shapes, in_spec...  7.58 us
    ppermute x3, starting transfers between devices, swap(): return lax.ppermute(array, 'nest', [(0, 1), (1, 0)])  1.11 us
  transfers between devices with their start and end apart: 3, of which 0 were waited for; matrix products, arithmetic and copies ran while one was open for 0% of the time, Pallas kernels for 6%

profile of v14, /device:TPU:0, one launch (start us, length us, event | category | flops | bytes accessed | tf_op | source)
XLA Modules:
  0.0 36.5 jit_solution(14801924489595497538)
XLA Ops:
  0.0 0.0 copy-start.2
  0.0 0.0 copy-start.9
  0.0 0.0 copy-start.8
  0.0 0.0 copy-start.6
  0.0 0.0 copy-start.3
  0.0 0.5 %collective-permute-start = (f32[72,1024]{1,0:T(8,128)}, f32[72,1024]{1,0:T(8,128)S(1)}, u32[]{:S(2)}, u32[]{:S(2)}) collective-permute-start(f32[72,1024]{1,0:T(8,128)} %bitcast.13), channel_id=1, source_target_pairs={{0,16},{16,0},{1,17},{17,1},{2,18},{18,2},{3,19},{19,3},{4,20},{20... | collective-permute-start | bytes 884744 | tf_op jit(solution)/shard_map/ppermute | solution.py:636
  0.5 0.1 collective-permute-start.1
  1.3 0.1 shard_map.110.steps
  1.4 0.0 copy-start
  1.4 0.0 copy-start.1
  1.4 0.0 copy-start.4
  1.4 0.0 copy-start.5
  1.4 0.0 copy-done.2
  1.4 0.0 copy-done.9
  1.4 0.0 copy-done.8
  1.4 0.0 copy-done.6
  1.4 0.0 copy-done.3
  1.4 1.2 %shard_map.109 = (s32[4,1,256]{2,1,0:T(1,128)S(1)}, s32[4,1,256]{2,1,0:T(1,128)S(1)}, f32[4,72,256]{2,1,0:T(8,128)S(1)}, bf16[4,256,256]{2,1,0:T(8,128)(2,1)S(1)...) custom-call(f32[72,1024]{1,0:T(8,128)S(1)} %bitcast.14, s32[4,1024]{1,0:T(4,128)S(1)} %bitcast.15, ...), custom_call_target="tpu_custom_call" | custom-call | flops 1000000000 | bytes 1155072 | tf_op jit(solution)/shard_map/pallas_call | solution.py:591
  2.6 0.0 copy-start.7
  2.7 0.0 collective-permute-done.1.send_b
  2.7 0.0 collective-permute-done.spectra_b
  2.7 0.0 copy-done
  2.7 1.0 %shard_map.111 = (f32[4,72,256]{2,1,0:T(8,128)S(1)}, f32[72,256]{1,0:T(8,128)S(1)}, f32[13,72,256]{2,1,0:T(8,128)S(1)}) custom-call(f32[4,72,256]{2,1,0:T(8,128)S(1)} %get-tuple-element.22.base, bf16[4,256,256]{2,1,0:T(8,128)(2,1)S(1)} %get-tuple-element.23.into, f32[4,1,256]{2,1,0:T(1,128)S(1)} %get-tuple-element.24.sea, ...), custom_call_target="tpu_custom_call" | custom-call | flops 100000000 | bytes 2457152 | tf_op jit(solution)/shard_map/pallas_call | solution.py:591
  3.7 0.5 %collective-permute-start.2 = (f32[72,256]{1,0:T(8,128)S(1)}, f32[72,256]{1,0:T(8,128)S(1)}, u32[]{:S(2)}, u32[]{:S(2)}) collective-permute-start(f32[72,256]{1,0:T(8,128)S(1)} %get-tuple-element.27), channel_id=1, source_target_pairs={{0,16},{16,0},{1,17},{17,1},{2,18},{18,2},{3,19},{19,3},{4,20},{20... | collective-permute-start | bytes 221192 | tf_op jit(solution)/shard_map/ppermute | solution.py:636
  4.2 0.0 copy-done.1
  4.2 0.0 copy-done.4
  4.2 0.0 copy-done.5
  4.2 0.9 %shard_map.112 = (f32[4,1,256]{2,1,0:T(1,128)S(1)}, bf16[4,256,512]{2,1,0:T(8,128)(2,1)S(1)}, s32[1,1024]{1,0:T(1,128)S(1)}, bf16[1152,1152]{1,0:T(8,128)(2,1)S(1)}, f32[2,1152]{1,0:T(2,128)S(1)}) custom-call(s32[4,1,256]{2,1,0:T(1,128)S(1)} %get-tuple-element.30.rank, f32[4,1,256]{2,1,0:T(1,128)S(1)} %get-tuple-element.24.sea, ...), custom_call_target="tpu_custom_call" | custom-call | flops 1000000000 | bytes 6391808 | tf_op jit(solution)/shard_map/pallas_call | solution.py:591
  5.2 0.0 collective-permute-done.2.incoming
  5.2 0.0 copy-done.7
  5.2 0.9 %shard_map.113 = (f32[288,128]{1,0:T(8,128)S(1)}, f32[8,512]{1,0:T(8,128)S(1)}) custom-call(f32[4,72,256]{2,1,0:T(8,128)S(1)} %get-tuple-element.26.field_in, f32[72,256]{1,0:T(8,128)S(1)} %collective-permute-done.2.incoming, bf16[4,256,256]{2,1,0:T(8,128)(2,1)S(1)} %get-tuple-element.23.into, s32[2,256]{1,0:T(2,128)S(1)} %get-tuple-element.25.lists, ...), custom_call_target="tpu_custom_call" | custom-call | flops 1000000000 | bytes 3086336 | tf_op jit(solution)/shard_map/pallas_call | solution.py:591
  6.1 16.0 %all_to_all.10 = f32[16,1,2304]{2,1,0:T(1,128)S(1)} all-to-all(f32[16,1,2304]{2,1,0:T(1,128)S(1)} %bitcast.10), channel_id=1, replica_groups=mesh['nest'=2,'bin'=16] {'bin'}, dimensions={0} | all-to-all | bytes 294912 | tf_op jit(solution)/shard_map/all_to_all | solution.py:632
  22.1 2.3 %shard_map.114 = f32[288,128]{1,0:T(8,128)S(1)} custom-call(f32[288,128]{1,0:T(8,128)S(1)} %bitcast.11, bf16[1152,1152]{1,0:T(8,128)(2,1)S(1)} %get-tuple-element.35.weights, f32[2,1152]{1,0:T(2,128)S(1)} %get-tuple-element.36.rates, f32[8,512]{1,0:T(8,128)S(1)} %get-tuple-element.37.blown), custom_call_target="tpu_custom_call" | custom-call | flops 1000000000 | bytes 2974720 | tf_op jit(solution)/shard_map/pallas_call | solution.py:591
  24.4 11.0 %all_to_all.11 = f32[16,1,2304]{2,1,0:T(1,128)S(1)} all-to-all(f32[16,1,2304]{2,1,0:T(1,128)S(1)} %bitcast.12), channel_id=1, replica_groups=mesh['nest'=2,'bin'=16] {'bin'}, dimensions={0} | all-to-all | bytes 294912 | tf_op jit(solution)/shard_map/all_to_all | solution.py:632
  35.4 1.1 %shard_map.115 = f32[72,1024]{1,0:T(8,128)} custom-call(f32[288,128]{1,0:T(8,128)S(1)} %bitcast.9, s32[1,1024]{1,0:T(1,128)S(1)} %get-tuple-element.38.place), custom_call_target="tpu_custom_call" | custom-call | flops 100000000 | bytes 446464 | tf_op jit(solution)/shard_map/pallas_call | solution.py:591
Async XLA Ops:
  0.0 1.4 %copy-start.2 = (f32[1,72,1024]{2,1,0:T(8,128)S(1)}, f32[1,72,1024]{2,1,0:T(8,128)}, u32[]{:S(2)}) copy-start(f32[1,72,1024]{2,1,0:T(8,128)} %param.11) | copy-start | bytes 884740
  0.0 1.4 %copy-start.9 = (s32[1,256]{1,0:T(1,128)S(1)}, s32[1,256]{1,0:T(1,128)}, u32[]{:S(2)}) copy-start(s32[1,256]{1,0:T(1,128)} %send.1) | copy-start | bytes 3076
  0.0 1.4 %copy-start.8 = (s32[1,256]{1,0:T(1,128)S(1)}, s32[1,256]{1,0:T(1,128)}, u32[]{:S(2)}) copy-start(s32[1,256]{1,0:T(1,128)} %recv.1) | copy-start | bytes 3076
  0.0 1.4 %copy-start.6 = (s32[1,1024]{1,0:T(1,128)S(1)}, s32[1,1024]{1,0:T(1,128)}, u32[]{:S(2)}) copy-start(s32[1,1024]{1,0:T(1,128)} %wet.1) | copy-start | bytes 12292
  0.0 1.4 %copy-start.3 = (s32[1,4,1024]{2,1,0:T(4,128)S(1)}, s32[1,4,1024]{2,1,0:T(4,128)}, u32[]{:S(2)}) copy-start(s32[1,4,1024]{2,1,0:T(4,128)} %param.17) | copy-start | bytes 49156
  0.0 2.7 %collective-permute-start = (f32[72,1024]{1,0:T(8,128)}, f32[72,1024]{1,0:T(8,128)S(1)}, u32[]{:S(2)}, u32[]{:S(2)}) collective-permute-start(f32[72,1024]{1,0:T(8,128)} %bitcast.13), channel_id=1, source_target_pairs={{0,16},{16,0},{1,17},{17,1},{2,18},{18,2},{3,19},{19,3},{4,20},{20... | collective-permute-start | bytes 884744 | tf_op jit(solution)/shard_map/ppermute | solution.py:636
  0.5 2.1 %collective-permute-start.1 = (s32[1,256]{1,0:T(1,128)}, s32[1,256]{1,0:T(1,128)S(1)}, u32[]{:S(2)}, u32[]{:S(2)}) collective-permute-start(s32[1,256]{1,0:T(1,128)} %send.1), channel_id=1, source_target_pairs={{0,16},{16,0},{1,17},{17,1},{2,18},{18,2},{3,19},{19,3},{4,20},{20... | collective-permute-start | bytes 3080 | tf_op jit(solution)/shard_map/ppermute | solution.py:636
  1.4 1.3 %copy-start = (f32[2,72]{1,0:T(2,128)S(1)}, f32[2,72]{1,0:T(2,128)}, u32[]{:S(2)}) copy-start(f32[2,72]{1,0:T(2,128)} %courant.1) | copy-start | bytes 1732
  1.4 2.9 %copy-start.1 = (bf16[1152,1152]{1,0:T(8,128)(2,1)S(1)}, bf16[1152,1152]{1,0:T(8,128)(2,1)}, u32[]{:S(2)}) copy-start(bf16[1152,1152]{1,0:T(8,128)(2,1)} %coupling.1) | copy-start | bytes 7962628
  1.4 2.9 %copy-start.4 = (f32[1152]{0:T(1024)S(1)}, f32[1152]{0:T(1024)}, u32[]{:S(2)}) copy-start(f32[1152]{0:T(1024)} %growth.1) | copy-start | bytes 13828
  1.4 2.9 %copy-start.5 = (f32[1152]{0:T(1024)S(1)}, f32[1152]{0:T(1024)}, u32[]{:S(2)}) copy-start(f32[1152]{0:T(1024)} %dissipation.1) | copy-start | bytes 13828
  2.6 2.5 %copy-start.7 = (f32[1,1024]{1,0:T(1,128)S(1)}, f32[1,1024]{1,0:T(1,128)}, u32[]{:S(2)}) copy-start(f32[1,1024]{1,0:T(1,128)} %wind.1) | copy-start | bytes 12292
  3.7 1.4 %collective-permute-start.2 = (f32[72,256]{1,0:T(8,128)S(1)}, f32[72,256]{1,0:T(8,128)S(1)}, u32[]{:S(2)}, u32[]{:S(2)}) collective-permute-start(f32[72,256]{1,0:T(8,128)S(1)} %get-tuple-element.27), channel_id=1, source_target_pairs={{0,16},{16,0},{1,17},{17,1},{2,18},{18,2},{3,19},{19,3},{4,20},{20... | collective-permute-start | bytes 221192 | tf_op jit(solution)/shard_map/ppermute | solution.py:636
